TPU v7x, 32 devices: a whole 2x2x4 slice. The times are simulated.
32 devices in a mesh: dp: 8 (over z, y), tensor: 4 (over x, core).
Axes of the slice: x: 2, y: 2, z: 4, core: 2. Of those that a mesh axis runs over, the one named last changes fastest.
Arguments:
- tokens: bfloat16 [8192, 2048], P('dp'), may hold values from -8 to 8
- positions: int32 [8192], P('dp'), may hold values from 0 to 3069, as said below
- out_grad: bfloat16 [8192, 2048], P('dp'), may hold values from -8 to 8
- qkv_weight: float32 [2048, 8, 4, 128], P('dp', 'tensor'), may hold values from -0.125 to 0.125
- qkv_first: float32 [2048, 8, 4, 128], P('dp', 'tensor'), may hold values from -40 to 40
- qkv_second: float32 [2048, 8, 4, 128], P('dp', 'tensor'), may hold values from 212.992 to 860.16
- out_weight: float32 [2048, 2048], P('dp', 'tensor'), may hold values from -1 to 1
- out_first: float32 [2048, 2048], P('dp', 'tensor'), may hold values from -10 to 10
- out_second: float32 [2048, 2048], P('dp', 'tensor'), may hold values from 9.8304 to 39.3216
- gate_up: float32 [2, 2048, 6144], P(None, 'dp', 'tensor'), may hold values from -0.125 to 0.125
- gate_up_first: float32 [2, 2048, 6144], P(None, 'dp', 'tensor'), may hold values from -32 to 32
- gate_up_second: float32 [2, 2048, 6144], P(None, 'dp', 'tensor'), may hold values from 106.496 to 434.176
- down_weight: float32 [2048, 6144], P('dp', 'tensor'), may hold values from -0.078125 to 0.078125
- down_first: float32 [2048, 6144], P('dp', 'tensor'), may hold values from -32 to 32
- down_second: float32 [2048, 6144], P('dp', 'tensor'), may hold values from 155.648 to 622.592
- gains: float32 [4352], P('dp'), may hold values from 0.5 to 1.5
- gains_first: float32 [4352], P('dp'), may hold values from -64 to 64
- gains_second: float32 [4352], P('dp'), may hold values from 434.176 to 1720.32
Outputs:
- block_out: bfloat16 [8192, 2048], P('dp')
- grad_input: float32 [8192, 2048], P('dp')
- qkv_first_new: float32 [2048, 8, 4, 128], P('dp', 'tensor')
- qkv_second_new: float32 [2048, 8, 4, 128], P('dp', 'tensor')
- qkv_new: float32 [2048, 8, 4, 128], P('dp', 'tensor')
- out_first_new: float32 [2048, 2048], P('dp', 'tensor')
- out_second_new: float32 [2048, 2048], P('dp', 'tensor')
- out_new: float32 [2048, 2048], P('dp', 'tensor')
- gate_up_first_new: float32 [2, 2048, 6144], P(None, 'dp', 'tensor')
- gate_up_second_new: float32 [2, 2048, 6144], P(None, 'dp', 'tensor')
- gate_up_new: float32 [2, 2048, 6144], P(None, 'dp', 'tensor')
- down_first_new: float32 [2048, 6144], P('dp', 'tensor')
- down_second_new: float32 [2048, 6144], P('dp', 'tensor')
- down_new: float32 [2048, 6144], P('dp', 'tensor')
- gains_first_new: float32 [4352], P('dp')
- gains_second_new: float32 [4352], P('dp')
- gains_new: float32 [4352], P('dp')
Inputs may be any that keep to these rules, and one draw needn't show every extreme that they name: Within each sequence of 1024 tokens the positions start at 0 and rise by 1 to 3 from one token to the next; in one sequence, drawn from the seed, they rise by 3 at every token.
All inputs are finite; a program needn't handle non-finite values.
Results may differ from a plain program's by a relative error of at most 0.03.
Values may be sent and summed in bfloat16 or wider, within the bound.
A program may use at most 320 MiB of HBM per device.

v0:
```python
import functools
import math

import jax
import jax.numpy as jnp
from jax import lax
from jax.experimental import pallas as pl
from jax.experimental.pallas import tpu as pltpu
from jax.sharding import PartitionSpec as P

SEQ = 1024
STEP = 10


EPS_NORM = 1e-06
THETA = 1000000.0
BETA_ONE = 0.9
BETA_TWO = 0.95
ADAM_EPS = 1e-08
DECAY_RATE = 0.1
RATE_QKV = 0.05
RATE_OUT = 0.3
RATE_GATE = 0.05
RATE_DOWN = 0.03
RATE_GAIN = 1.0


def rotary(positions, head_size):
    freq_index = jnp.arange(head_size // 2, dtype=jnp.float32)
    inverse = jnp.exp(freq_index * (-2.0 * math.log(THETA) / head_size))
    angles = positions.astype(jnp.float32)[:, None] * inverse[None, :]
    cosine = jnp.cos(angles)
    sine_table = jnp.sin(angles)
    return (jnp.concatenate([cosine, cosine], -1), jnp.concatenate([sine_table, sine_table], -1))


def rotate(values, cosine, sine_table):
    half_size = values.shape[-1] // 2
    turned = jnp.concatenate([-values[..., half_size:], values[..., :half_size]], -1)
    return values * cosine[:, None, :] + turned * sine_table[:, None, :]


def unrotate(gradient, cosine, sine_table):
    half_size = gradient.shape[-1] // 2
    turned = gradient * sine_table[:, None, :]
    rotated_back = jnp.concatenate([turned[..., half_size:], -turned[..., :half_size]], -1)
    return gradient * cosine[:, None, :] + rotated_back


def norm_back(grad_unit, unit_vals, factor):
    return factor * (grad_unit - unit_vals * jnp.mean(grad_unit * unit_vals, -1, keepdims=True))


def contract_rows(left, right):
    return lax.dot_general(
        left, right, (((0,), (0,)), ((), ())), preferred_element_type=jnp.float32
    )


def contract_cols(left, right):
    return lax.dot_general(
        left, right, (((1,), (1,)), ((), ())), preferred_element_type=jnp.float32
    )


def block_scores(query_part, key_part, first_row, block_rows, last_row):
    scores = jnp.einsum(
        "nqkgd,nskd->nkgqs", query_part, key_part, preferred_element_type=jnp.float32
    )
    causal = (first_row + jnp.arange(block_rows))[:, None] >= jnp.arange(last_row)[None, :]
    return jnp.where(causal, scores, -1000000000.0)


def attention_forward(query, key_rot, values_low, seq_len):
    block_rows = min(512, seq_len)
    outputs = []
    log_sums = []
    for first_row in range(0, seq_len, block_rows):
        last_row = first_row + block_rows
        query_part = query[:, first_row:last_row]
        scores = block_scores(query_part, key_rot[:, :last_row], first_row, block_rows, last_row)
        row_max = jnp.max(scores, -1, keepdims=True)
        exponent = jnp.exp(scores - row_max)
        row_total = jnp.sum(exponent, -1, keepdims=True)
        probs_low = (exponent / row_total).astype(jnp.bfloat16)
        outputs.append(
            jnp.einsum(
                "nkgqs,nskd->nqkgd",
                probs_low,
                values_low[:, :last_row],
                preferred_element_type=jnp.float32,
            )
        )
        log_sums.append(row_max + jnp.log(row_total))
    return (jnp.concatenate(outputs, 1), log_sums)


def attention_backward(query, key_rot, values_low, grad_att, log_sums, seq_len):
    block_rows = min(512, seq_len)
    query_grads = []
    key_grad = jnp.zeros(key_rot.shape, jnp.float32)
    value_grad = jnp.zeros(values_low.shape, jnp.float32)
    for block_index, first_row in enumerate(range(0, seq_len, block_rows)):
        last_row = first_row + block_rows
        query_part = query[:, first_row:last_row]
        grad_part = grad_att[:, first_row:last_row]
        key_part = key_rot[:, :last_row]
        value_part = values_low[:, :last_row]
        scores = block_scores(query_part, key_part, first_row, block_rows, last_row)
        probs = jnp.exp(scores - log_sums[block_index])
        probs_low = probs.astype(jnp.bfloat16)
        grad_probs = jnp.einsum(
            "nqkgd,nskd->nkgqs", grad_part, value_part, preferred_element_type=jnp.float32
        )
        grad_scores = (
            probs * (grad_probs - jnp.sum(probs * grad_probs, -1, keepdims=True))
        ).astype(jnp.bfloat16)
        query_grads.append(
            jnp.einsum(
                "nkgqs,nskd->nqkgd", grad_scores, key_part, preferred_element_type=jnp.float32
            )
        )
        padding = ((0, 0), (0, seq_len - last_row), (0, 0), (0, 0))
        key_grad = key_grad + jnp.pad(
            jnp.einsum(
                "nkgqs,nqkgd->nskd", grad_scores, query_part, preferred_element_type=jnp.float32
            ),
            padding,
        )
        value_grad = value_grad + jnp.pad(
            jnp.einsum(
                "nkgqs,nqkgd->nskd", probs_low, grad_part, preferred_element_type=jnp.float32
            ),
            padding,
        )
    return (jnp.concatenate(query_grads, 1), key_grad, value_grad)


def adamw(weight, gradient, moment, second, step_rate, decay_rate):
    moment = BETA_ONE * moment + (1.0 - BETA_ONE) * gradient
    second = BETA_TWO * second + (1.0 - BETA_TWO) * gradient * gradient
    first_hat = moment / (1.0 - BETA_ONE**STEP)
    second_hat = second / (1.0 - BETA_TWO**STEP)
    weight = weight - step_rate * (
        first_hat / (jnp.sqrt(second_hat) + ADAM_EPS) + decay_rate * weight
    )
    return (moment, second, weight)


def fence(*values):
    return lax.optimization_barrier(values)


MESH = pl.DeviceIdType.MESH
HEAD = 128
AHEAD = 2


def place_here():
    index, place = lax.axis_index("dp"), lax.axis_index("tensor")
    return lax.div(index, 2), lax.rem(index, 2), lax.div(place, 2), lax.rem(place, 2)


def device(zone, side, row, core):
    return (zone * 2 + side, row * 2 + core)


def flipped(zone, flip):
    bit = 1
    while bit <= flip:
        if flip & bit:
            zone = zone + bit - 2 * bit * lax.rem(lax.div(zone, bit), 2)
        bit *= 2
    return zone


def greet(devices, amount=None):
    barrier = pltpu.get_barrier_semaphore()
    for peer in devices:
        pl.semaphore_signal(barrier, inc=1, device_id=peer, device_id_type=MESH)
    pl.semaphore_wait(barrier, len(devices) if amount is None else amount)


def for_rows(count, body):
    step = 32

    def one(block, carry):
        body(pl.multiple_of(block * step, step), step)
        return carry

    lax.fori_loop(0, count // step, one, 0)


class Copies:
    def __init__(self, send_sems, recv_sems):
        self.send_sems, self.recv_sems = send_sems, recv_sems
        self.number = 0

    def make(self, source, target, peer):
        number, self.number = self.number, self.number + 1
        return pltpu.make_async_remote_copy(
            src_ref=source,
            dst_ref=target,
            send_sem=self.send_sems.at[number],
            recv_sem=self.recv_sems.at[number],
            device_id=peer,
            device_id_type=MESH,
        )

    def start(self, source, target, peer):
        copy = self.make(source, target, peer)
        copy.start()
        return copy


class GainSum:
    def __init__(self, plan, rest, width):
        self.plan, self.width = plan, width
        self.total = width + rest
        self.scratch = [
            pltpu.VMEM((8, 1, self.total), jnp.float32),
            pltpu.VMEM((plan.zones, 1, self.total), jnp.float32),
        ]
        self.output = jax.ShapeDtypeStruct((1, self.total), jnp.float32)
        self.count = 7 + plan.zones - 1

    def plane_peers(self, zone, side, row, core):
        steps = [(s, r, c) for s in range(2) for r in range(2) for c in range(2)][1:]
        turn = lambda value, step: 1 - value if step else value
        return [device(zone, turn(side, s), turn(row, r), turn(core, c)) for s, r, c in steps]

    def zone_peers(self, zone, side, row, core):
        return {flip: device(flipped(zone, flip), side, row, core) for flip in self.plan.flips[1:]}

    def start(self, copies, rest, blocks, plane_sums, zone_sums):
        zone, side, row, core = place_here()
        plan = self.plan
        size = self.width // plan.total
        self.copies, self.plane_sums, self.zone_sums, self.zone = copies, plane_sums, zone_sums, zone
        here = side * 4 + row * 2 + core
        plane_sums[here, :, pl.ds(self.width, self.total - self.width)] = rest[...]
        for slot in range(plan.total):
            owner = flipped(zone, plan.flips[slot % plan.zones]) * 2
            owner = owner + (core if slot < plan.zones else 1 - core)
            spot = pl.ds(pl.multiple_of(owner * size, size), size)
            plane_sums[here, :, spot] = blocks[:, pl.ds(slot * size, size)]
        self.plane = [
            copies.start(plane_sums.at[here], plane_sums.at[here], peer)
            for peer in self.plane_peers(zone, side, row, core)
        ]

    def middle(self):
        for copy in self.plane:
            copy.wait_recv()
        total = self.plane_sums[0]
        for place in range(1, 8):
            total = total + self.plane_sums[place]
        self.zone_sums[self.zone] = total
        zone, side, row, core = place_here()
        self.across = [
            self.copies.start(self.zone_sums.at[self.zone], self.zone_sums.at[self.zone], peer)
            for peer in self.zone_peers(zone, side, row, core).values()
        ]

    def finish(self, out):
        for copy in self.across:
            copy.wait_recv()
        total = self.zone_sums[0]
        for place in range(1, self.plan.zones):
            total = total + self.zone_sums[place]
        out[...] = total
        for copy in self.plane + self.across:
            copy.wait_send()


class ZoneBlocks:
    scratch = []

    def __init__(self, plan, source, slots, begin=0):
        self.flips, self.slots, self.sources, self.begin = plan.flips, list(slots), [source], begin
        self.outputs = [
            jax.ShapeDtypeStruct((len(self.slots),) + source.shape[1:], source.dtype)
        ]
        self.count, self.count_local = len(self.slots), 0
        self.in_hbm = False

    def peers(self, zone, side, row, core):
        return {
            self.flips[slot]: device(flipped(zone, self.flips[slot]), side, row, core)
            for slot in self.slots
        }

    def start(self, copies, local_sems, sources, targets, stages):
        zone, side, row, core = place_here()
        self.started = [
            copies.make(
                sources[0].at[slot],
                targets[0].at[number],
                device(flipped(zone, self.flips[slot]), side, row, core),
            )
            for number, slot in enumerate(self.slots)
        ]
        self.waiting = True
        if self.begin == 0:
            self.pump([0])

    def pump(self, steps):
        if self.waiting and self.begin in steps:
            self.waiting = False
            for copy in self.started:
                copy.start()

    def finish(self):
        for copy in self.started:
            copy.wait_send()
        for copy in self.started:
            copy.wait_recv()


def inner_zone(zone):
    return lax.rem(lax.div(zone + 1, 2), 2)


class SideDot:
    count, count_local, scratch, in_hbm = 0, 0, [], False

    def __init__(self, left, right):
        self.sources = [left, right]
        self.outputs = [jax.ShapeDtypeStruct((left.shape[0], right.shape[0]), jnp.bfloat16)]

    def peers(self, zone, side, row, core):
        return {}

    def some(self, first, last):
        left, right = self.refs
        size = 256

        def one(step, carry):
            here = pl.ds(pl.multiple_of(step * size, size), size)
            self.out[:, here] = dot(left[...], right[here, :], 1, 1).astype(jnp.bfloat16)
            return carry

        lax.fori_loop(first, last, one, 0)

    def start(self, copies, local_sems, sources, targets, stages):
        self.refs, self.out = sources, targets[0]
        self.steps = self.out.shape[1] // 256
        self.some(0, self.steps // 2)

    def pump(self, steps):
        if 0 in steps:
            self.some(self.steps // 2, self.steps)

    def finish(self):
        pass


class PairScatter:
    def __init__(self, parts, ready, pieces):
        self.sources, self.pieces = [parts, ready], pieces
        _, rows, columns = parts.shape
        self.size = rows // pieces
        self.outputs = [jax.ShapeDtypeStruct((2, rows, columns), parts.dtype)]
        self.scratch = [pltpu.VMEM((2, rows, columns), parts.dtype)] * 2
        self.count, self.count_local = 3 * pieces, 0
        self.in_hbm = False

    def peers(self, zone, side, row, core):
        return {
            1: device(flipped(zone, 1), side, row, core),
            3: device(flipped(zone, 3), side, row, core),
        }

    def start(self, copies, local_sems, sources, targets, stages):
        zone, side, row, core = place_here()
        self.parts, self.ready = sources
        self.out = targets[0]
        self.inward, self.crossed = stages
        inner_peer = device(flipped(zone, 3), side, row, core)
        outer_peer = device(flipped(zone, 1), side, row, core)
        self.inner = inner_zone(zone) == 1
        self.outer = inner_zone(zone) == 0
        pieces = [pl.ds(piece * self.size, self.size) for piece in range(self.pieces)]
        self.steps = [(slot, rows) for slot in (0, 1) for rows in pieces]
        self.to_inner = [
            copies.make(self.parts.at[2, rows], self.inward.at[1, rows], outer_peer)
            for rows in pieces
        ]
        self.across = [
            copies.make(self.inward.at[slot, rows], self.crossed.at[slot, rows], inner_peer)
            for slot, rows in self.steps
        ]

        @pl.when(self.outer)
        def _():
            for copy in self.to_inner[:AHEAD]:
                copy.start()

        @pl.when(self.inner)
        def _():
            for step in range(self.pieces):
                slot, rows = self.steps[step]
                self.add(self.inward, slot, rows, self.parts.at[2], self.ready)
                self.across[step].start()

    def add(self, target, slot, rows, left, right):
        def some(row, count):
            here = pl.ds(rows.start + row, count)
            both = left[here, :].astype(jnp.float32) + right[here, :].astype(jnp.float32)
            target.at[slot][here, :] = both.astype(jnp.bfloat16)

        for_rows(self.size, some)

    def pump(self, steps):
        steps = [step for step in steps if step < self.pieces]

        @pl.when(self.inner)
        def _():
            for step in steps:
                slot, rows = self.steps[self.pieces + step]
                self.to_inner[step].wait_recv()
                self.add(self.inward, slot, rows, self.parts.at[3], self.inward.at[1])
                self.across[self.pieces + step].start()
                self.settle(step)

        @pl.when(self.outer)
        def _():
            for step in steps:
                self.to_inner[step].wait_send()
                for copy in self.to_inner[step + AHEAD : step + AHEAD + 1]:
                    copy.start()

    def settle(self, step):
        slot, rows = self.steps[step]
        self.across[step].wait_recv()
        self.add(self.out, slot, rows, self.parts.at[slot], self.crossed.at[slot])

    def finish(self):
        @pl.when(self.inner)
        def _():
            for step in range(self.pieces, len(self.steps)):
                self.settle(step)
            for copy in self.across:
                copy.wait_send()

        @pl.when(self.outer)
        def _():
            for slot in (0, 1):

                def some(row, count, slot=slot):
                    here = pl.ds(row, count)
                    self.out.at[slot][here, :] = self.parts.at[slot][here, :]

                for_rows(self.parts.shape[1], some)


class BlockGrad:
    in_hbm = False

    def __init__(self, plan, left, right):
        self.zones, self.flips = plan.zones, plan.flips
        self.sources = [left, right]
        shape = (left.shape[1] // plan.total, right.shape[1])
        low = jnp.bfloat16
        self.outputs = [jax.ShapeDtypeStruct(shape, low)]
        self.scratch = [pltpu.VMEM((plan.zones,) + shape, low)] * 4
        self.count, self.count_local = 2 * plan.zones, 0

    def peers(self, zone, side, row, core):
        return {flip: device(flipped(zone, flip), side, row, core) for flip in self.flips[1:]}

    def product(self, block):
        size = self.out.shape[0]
        return dot(self.left[:, pl.ds(block * size, size)], self.right[...], 0, 0)

    def start(self, copies, local_sems, sources, targets, stages):
        zone, side, row, core = place_here()
        self.left, self.right = sources
        self.out = targets[0]
        self.far, self.got, self.parts, self.arrived = stages
        core_peer = device(zone, side, row, 1 - core)
        self.order = list(range(1, self.zones)) + [0]
        self.over = [
            copies.make(self.far.at[slot], self.got.at[slot], core_peer)
            for slot in range(self.zones)
        ]
        self.along = [
            copies.make(
                self.parts.at[slot],
                self.arrived.at[slot],
                device(flipped(zone, self.flips[slot]), side, row, core),
            )
            for slot in range(1, self.zones)
        ]
        for slot in self.order:
            self.far[slot] = self.product(self.zones + slot).astype(jnp.bfloat16)
            self.over[slot].start()

    def pump(self, steps):
        for slot in self.order if 0 in steps else []:
            near = self.product(slot)
            self.over[slot].wait_recv()
            self.parts[slot] = (near + self.got[slot].astype(jnp.float32)).astype(jnp.bfloat16)
            if slot:
                self.along[slot - 1].start()

    def finish(self):
        total = self.parts[0].astype(jnp.float32)
        for slot in range(1, self.zones):
            self.along[slot - 1].wait_recv()
            total = total + self.arrived[slot].astype(jnp.float32)
        self.out[...] = total.astype(jnp.bfloat16)
        for copy in self.over + self.along:
            copy.wait_send()


class PairTree:
    def __init__(self, pairs, pieces):
        self.pairs = [len(pair) for pair in pairs]
        self.sources = [shard for pair in pairs for shard in pair]
        self.pieces = pieces
        self.outputs = [
            jax.ShapeDtypeStruct((8,) + own.shape, own.dtype) for own, *_ in pairs
        ]
        self.count = 6 * sum(pieces) + 2 * len(pairs) + self.pairs.count(1)
        self.count_local = 2 * len(pairs) + 2 * sum(pieces)
        self.scratch = [pltpu.VMEM((2,) + own.shape, own.dtype) for own, *_ in pairs]
        self.scratch += [pltpu.VMEM(p[0].shape, p[0].dtype) for p in pairs if len(p) == 1]
        self.in_hbm = True

    def peers(self, zone, side, row, core):
        return {
            1: device(flipped(zone, 1), side, row, core),
            3: device(flipped(zone, 3), side, row, core),
            "core": device(zone, side, row, 1 - core),
        }

    def start(self, copies, local_sems, sources, targets, stages):
        zone, side, row, core = place_here()
        inner_peer = device(flipped(zone, 3), side, row, core)
        outer_peer = device(flipped(zone, 1), side, row, core)
        core_peer = device(zone, side, row, 1 - core)
        self.inner = inner_zone(zone) == 1
        self.outer = inner_zone(zone) == 0
        self.across, self.onward, self.late, self.place = [], [], [], []
        self.shared, self.kept, self.partners, self.later = [], [], [], []
        sem = 0
        sources, late_stages = list(sources), list(stages[len(targets) :])
        for weight, full in enumerate(targets):
            landing = stages[weight]
            pair = [sources.pop(0) for _ in range(self.pairs[weight])]
            if len(pair) == 1:
                pair.append(late_stages.pop(0))
                self.partners.append(copies.start(pair[0], pair[1], outer_peer))
            size = pair[0].shape[0] // self.pieces[weight]
            for piece in range(self.pieces[weight]):
                rows = pl.ds(piece * size, size)
                for slot in (0, 1):
                    here = landing.at[slot, rows]
                    self.across.append(copies.make(pair[slot].at[rows], here, inner_peer))
                    self.onward.append(copies.make(here, landing.at[1 - slot, rows], outer_peer))
                    self.late.append(copies.make(here, full.at[6 + slot, rows], core_peer))
                    self.place.append(
                        pltpu.make_async_copy(here, full.at[2 + slot, rows], local_sems.at[sem])
                    )
                    sem += 1
            for slot in (0, 1):
                self.shared.append(copies.make(pair[slot], full.at[4 + slot], core_peer))
                self.kept.append(
                    pltpu.make_async_copy(pair[slot], full.at[slot], local_sems.at[sem])
                )
                sem += 1
                if slot >= self.pairs[weight]:
                    self.later += [self.shared[-1], self.kept[-1]]
                else:
                    self.shared[-1].start()
                    self.kept[-1].start()

        @pl.when(self.inner)
        def _():
            for copy in self.across[:AHEAD]:
                copy.start()

    def arrive(self, number):
        self.onward[number].wait_recv()
        swapped = number + 1 - 2 * (number % 2)
        self.late[swapped].start()
        self.place[swapped].start()

    def pump(self, steps):
        steps = [step for step in steps if step < len(self.across)]

        @pl.when(self.inner)
        def _():
            for here in steps:
                self.across[here].wait_recv()
                for copy in self.across[here + AHEAD : here + AHEAD + 1]:
                    copy.start()
                self.onward[here].start()
                self.late[here].start()
                self.place[here].start()

        @pl.when(self.outer)
        def _():
            for step in steps:
                if step > 0:
                    self.arrive(step - 1)

        for copy in self.partners if 1 in steps else []:
            copy.wait_recv()
            copy.wait_send()
        for copy in self.later if 1 in steps else []:
            copy.start()

    def finish(self):
        @pl.when(self.inner)
        def _():
            for copy in self.across + self.onward:
                copy.wait_send()

        @pl.when(self.outer)
        def _():
            self.arrive(len(self.onward) - 1)

        for copy in self.kept + self.place:
            copy.wait()
        for copy in self.shared + self.late:
            copy.wait_send()
        for copy in self.shared + self.late:
            copy.wait_recv()


def sum_eighths(
    copies, row_peer, side_peer, send, keep, forward, first, second, store, begin, pump
):
    size = send.shape[0] // 4
    part = lambda ref, slot: ref.at[pl.ds(slot * size, size)]
    arrivals = [
        copies.start(part(send, 1), part(first, 1), row_peer),
        copies.start(part(send, 3), part(first, 3), side_peer),
        copies.start(part(send, 0), part(first, 0), row_peer),
        copies.start(part(send, 2), part(first, 2), side_peer),
    ]
    begin()
    passed = []
    for number, slot, peer in ((0, 1, side_peer), (1, 3, row_peer)):
        arrivals[number].wait_recv()

        def add(row, count, number=number, slot=slot):
            here = pl.ds(slot * size + row, count)
            both = keep[here, :].astype(jnp.float32) + first[here, :].astype(jnp.float32)
            forward[pl.ds(number * size + row, count), :] = both.astype(jnp.bfloat16)

        for_rows(size, add)
        passed.append(copies.start(part(forward, number), part(second, number), peer))
    pump([0])
    for number, slot in ((0, 0), (1, 2)):
        arrivals[2 + number].wait_recv()
        passed[number].wait_recv()

        def total(row, count, number=number, slot=slot):
            here = pl.ds(slot * size + row, count)
            sums = keep[here, :].astype(jnp.float32) + first[here, :].astype(jnp.float32)
            sums = sums + second[pl.ds(number * size + row, count), :].astype(jnp.float32)
            store(number, row, count, sums)

        for_rows(size, total)
        yield number
    for copy in arrivals + passed:
        copy.wait_send()


def halves(terms):
    rows = terms.shape[0] // 2
    return terms.at[pl.ds(0, rows)], terms.at[pl.ds(rows, rows)]


def split_refs(refs, jobs, extra_count, out_count):
    refs = list(refs)
    take = lambda count: [refs.pop(0) for _ in range(count)]
    extras = take(extra_count)
    sources = [take(len(job.sources)) for job in jobs]
    full = take(1)[0]
    outs = take(out_count)
    targets = [take(len(job.outputs)) for job in jobs]
    return extras, sources, full, outs, targets, refs


def spread_kernel(middle, jobs, extra_count, out_count, gain_sum, plan, terms, *refs):
    keep, send = halves(terms)
    extras, sources, full, outs, targets, scratch = split_refs(refs, jobs, extra_count, out_count)
    forward, first, second, send_sems, recv_sems, local_sems, *stages = scratch
    zone, side, row, core = place_here()
    row_peer, side_peer = device(zone, side, 1 - row, core), device(zone, 1 - side, row, core)
    copies = Copies(send_sems, recv_sems)
    size = send.shape[0] // 4
    part = lambda slot: full.at[pl.ds(slot * size, size)]
    for out in outs:
        if out.shape[0] == 1:
            out[...] = jnp.zeros_like(out)
    peers = {}
    for job in jobs:
        peers.update(job.peers(zone, side, row, core))
    greet([row_peer, side_peer] + list(peers.values()))

    def begin():
        spot = 0
        for job, source, target in zip(jobs, sources, targets):
            own_stages = stages[spot : spot + len(job.scratch)]
            job.start(copies, local_sems, source, target, own_stages)
            spot += len(job.scratch)

    def pump(steps):
        for job in jobs:
            job.pump(steps)

    def store(number, row, count, sums):
        own = pl.ds(number * size + row, count)
        full[pl.ds(2 * number * size + row, count), :] = middle(own, sums, extras, outs)

    firsts, seconds = [], []
    for number in sum_eighths(
        copies, row_peer, side_peer, send, keep, forward, first, second, store, begin, pump
    ):
        near, other = (side_peer, row_peer) if number == 0 else (row_peer, side_peer)
        slot = 2 * number
        firsts.append(copies.start(part(slot), part(slot + 1), near))
        seconds.append(copies.start(part(slot), part(4 + slot), other))
    pump([1])
    firsts[0].wait_recv()
    seconds.append(copies.start(part(1), part(5), row_peer))
    firsts[1].wait_recv()
    seconds.append(copies.start(part(3), part(7), side_peer))
    pump(range(2, 64))
    for copy in seconds:
        copy.wait_recv()
    for copy in firsts + seconds:
        copy.wait_send()
    for job in jobs:
        job.finish()


def home_kernel(middle, jobs, extra_count, out_count, gain_sum, plan, terms, *refs):
    keep, send = halves(terms)
    extras, sources, result, outs, targets, scratch = split_refs(refs, jobs, extra_count, out_count)
    forward, first, second, own, full, send_sems, recv_sems, local_sems, *rest = scratch
    gain_scratch, stages = (rest[:2], rest[2:]) if gain_sum is not None else ([], rest)
    block = extras[3]
    zone, side, row, core = place_here()
    row_peer, side_peer = device(zone, side, 1 - row, core), device(zone, 1 - side, row, core)
    core_peer, other_peer = device(zone, side, row, 1 - core), device(zone, 1 - side, row, 1 - core)
    copies = Copies(send_sems, recv_sems)
    size = send.shape[0] // 4
    at_home = side == core
    away = side != core
    for out in outs:
        if out.shape[0] == 1:
            out[...] = jnp.zeros_like(out)
    peers = {}
    for job in jobs:
        peers.update(job.peers(zone, side, row, core))
    plane = [row_peer, side_peer, core_peer, other_peer]
    if gain_sum is not None:
        plane = gain_sum.plane_peers(zone, side, row, core)
        peers.update(gain_sum.zone_peers(zone, side, row, core))
    greet(plane + list(peers.values()))

    def begin():
        spot = 0
        for job, source, target in zip(jobs, sources, targets):
            own_stages = stages[spot : spot + len(job.scratch)]
            job.start(copies, local_sems, source, target, own_stages)
            spot += len(job.scratch)

    def pump(steps):
        for job in jobs:
            job.pump(steps)

    def store(number, start, count, sums):
        here = pl.ds(number * size + start, count)
        values = middle(here, sums, extras, outs)
        own[here, :] = values
        eighth = row * 2 + side if number == 0 else 4 + side * 2 + row

        @pl.when(at_home)
        def _():
            full[pl.ds(pl.multiple_of(eighth * size + start, 32), count), :] = values

    def piece(number, x, y):
        start = (x * 2 + y) * size if number == 0 else (4 + y * 2 + x) * size
        return full.at[pl.ds(pl.multiple_of(start, size), size)]

    both = (0, 1)
    part = lambda ref, number: ref.at[pl.ds(number * size, size)]
    block_over = [copies.make(part(block, k), piece(k, row, side), core_peer) for k in both]
    block_side = [copies.make(part(block, k), piece(k, row, side), other_peer) for k in both]
    to_side = [copies.make(part(own, k), piece(k, row, side), side_peer) for k in both]
    to_row = [copies.make(piece(k, row, side), piece(k, row, side), row_peer) for k in both]
    pass_row = [
        copies.make(piece(k, row, 1 - side), piece(k, row, 1 - side), row_peer) for k in both
    ]

    @pl.when(at_home)
    def _():
        for copy in block_over:
            copy.start()

    for _ in sum_eighths(
        copies, row_peer, side_peer, send, keep, forward, first, second, store, begin, pump
    ):
        pass
    pump([1])
    if gain_sum is not None:
        gain_sum.start(copies, extras[-1], outs[0], *gain_scratch)

    @pl.when(away)
    def _():
        for copy in to_side + block_side:
            copy.start()
        for copy in block_over:
            copy.wait_recv()

    for copy in to_row:
        copy.start()
    if gain_sum is not None:
        gain_sum.middle()

    @pl.when(at_home)
    def _():
        for copy in to_side:
            copy.wait_recv()
        for copy in block_over:
            copy.wait_send()

    @pl.when(away)
    def _():
        for copy in block_side:
            copy.wait_recv()
        for copy in to_side + block_side:
            copy.wait_send()

    for copy in pass_row:
        copy.start()
    for copy in to_row + pass_row:
        copy.wait_recv()
        copy.wait_send()
    natural, local = block_columns(plan, full.shape[1], side)

    def some(start, count):
        here = pl.ds(start, count)
        for a, b in zip(natural, local):
            result[here, a] = full[here, b]

    for_rows(full.shape[0], some)
    if gain_sum is not None:
        gain_sum.finish(outs[-1])
    for job in jobs:
        job.finish()


def sum_rows(plan, kernel, middle, terms, extras, outs, number, jobs=(), gain_sum=None):
    half, width = terms.shape[0] // 2, terms.shape[1]
    eighth = half // 4
    low = jnp.bfloat16
    vmem, hbm = pl.BlockSpec(memory_space=pltpu.VMEM), pl.BlockSpec(memory_space=pl.ANY)
    scratch = [
        pltpu.VMEM((2 * eighth, width), low),
        pltpu.VMEM((half, width), low),
        pltpu.VMEM((2 * eighth, width), low),
    ]
    if kernel is home_kernel:
        scratch.append(pltpu.VMEM((2 * eighth, width), low))
        scratch.append(pltpu.VMEM((2 * half, width), low))
    copies = (12 if kernel is spread_kernel else 16) + sum(job.count for job in jobs)
    local = max([2] + [job.count_local for job in jobs])
    if gain_sum is not None:
        copies += gain_sum.count
        outs = outs + [gain_sum.output]
    scratch += [pltpu.SemaphoreType.DMA((count,)) for count in (copies, copies, local)]
    if gain_sum is not None:
        scratch += gain_sum.scratch
    scratch += [stage for job in jobs for stage in job.scratch]
    sources = [source for job in jobs for source in job.sources]
    targets = [target for job in jobs for target in job.outputs]
    return pl.pallas_call(
        functools.partial(kernel, middle, jobs, len(extras), len(outs), gain_sum, plan),
        out_shape=[jax.ShapeDtypeStruct((2 * half, width), low)] + outs + targets,
        in_specs=[vmem] * (1 + len(extras) + len(sources)),
        out_specs=[vmem] * (1 + len(outs))
        + [hbm if job.in_hbm else vmem for job in jobs for _ in job.outputs],
        scratch_shapes=scratch,
        compiler_params=pltpu.CompilerParams(
            collective_id=number, has_side_effects=True, vmem_limit_bytes=56 * 2**20
        ),
        cost_estimate=pl.CostEstimate(flops=10**6, bytes_accessed=10**5, transcendentals=0),
        name=middle.__name__,
    )(terms, *extras, *sources)


def block_columns(plan, width, of_core=None):
    if not plan.ordered:
        return [pl.ds(0, width)], [pl.ds(0, width)]
    zone, _, _, core = place_here()
    core = core if of_core is None else of_core
    size, zones = width // plan.total, plan.zones
    owners = [
        flipped(zone, plan.flips[slot % zones]) * 2 + (core if slot < zones else 1 - core)
        for slot in range(plan.total)
    ]
    natural = [pl.ds(pl.multiple_of(owner * size, size), size) for owner in owners]
    return natural, [pl.ds(slot * size, size) for slot in range(plan.total)]


def copy_rows(source, target):
    def some(row, count):
        target[pl.ds(row, count), :] = source[pl.ds(row, count), :]

    if source.shape[0] % 32:
        target[...] = source[...]
    else:
        for_rows(source.shape[0], some)


def cast_rows(source, target):
    def some(row, count):
        here = pl.ds(row, count)
        target[here, :] = source[here, :].astype(target.dtype)

    for_rows(source.shape[0], some)


def opening_kernel(plan, wide_qkv, gains, wide_gate, wide_out, wide_down, tokens, angles, *refs):
    qkv_full, gains_full, turned_gate, turned_out, turned_down, turned_tokens, turned_angles = refs[:7]
    partner_gate, send_sems, recv_sems, tokens_stage, qkv, gate, out, down = refs[7:]
    cast_rows(wide_qkv, qkv)
    zone, side, row, core = place_here()
    partner = device(zone, core, row, side)
    row_peer, core_peer = device(zone, side, 1 - row, core), device(zone, side, row, 1 - core)
    zone_peers = [device(flipped(zone, flip), side, row, core) for flip in plan.flips[1:]]
    at_home, away = side == core, side != core
    always = [row_peer, core_peer] + zone_peers

    @pl.when(at_home)
    def _():
        greet(always)

    @pl.when(away)
    def _():
        greet(always + [partner])

    copies = Copies(send_sems, recv_sems)
    zones = plan.zones
    own = (gains, qkv, angles, gate, out, down)
    ends = (gains_full.at[0], qkv_full.at[0], turned_angles, turned_gate, turned_out, turned_down)
    units = wide_gate.shape[2]

    def cast_rest():
        for half in (0, 1):
            cast_rows(wide_gate.at[half], gate.at[:, pl.ds(half * units, units)])
        cast_rows(wide_out, out)
        cast_rows(wide_down, down)

    turn = [copies.make(source, target, partner) for source, target in zip(own, ends)]
    pieces = 2
    size = tokens.shape[0] // (2 * pieces)
    spots = [
        pl.ds(pl.multiple_of((row * pieces + piece) * size, size), size) for piece in range(pieces)
    ]
    turn_rows = [copies.make(tokens.at[s], tokens_stage.at[s], partner) for s in spots]
    pass_rows = [copies.make(tokens_stage.at[s], tokens_stage.at[s], row_peer) for s in spots]
    natural, local = block_columns(plan, tokens.shape[1])

    def lay_down(all_tokens):
        def some(start, count):
            here = pl.ds(start, count)
            for a, b in zip(natural, local):
                turned_tokens[here, b] = all_tokens[here, a]

        for_rows(all_tokens.shape[0], some)

    slots = list(range(1, zones))
    weights = ((gains, gains_full), (qkv, qkv_full))
    from_own = [
        [copies.make(source, full.at[slot], zone_peers[slot - 1]) for slot in slots]
        + [copies.make(source, full.at[zones], core_peer)]
        for source, full in weights
    ] + [[copies.make(gate, partner_gate, zone_peers[0])]]
    copies.number -= 2 * zones + 1
    from_turned = [
        [copies.make(full.at[0], full.at[slot], zone_peers[slot - 1]) for slot in slots]
        + [copies.make(full.at[0], full.at[zones], core_peer)]
        for _, full in weights
    ] + [[copies.make(turned_gate, partner_gate, zone_peers[0])]]
    cross = [
        [copies.make(full.at[slot], full.at[zones + slot], core_peer) for slot in slots]
        for _, full in weights
    ]

    def cross_over(k):
        for which in (0, 1):
            from_turned[which][k].wait_recv()
            cross[which][k].start()

    @pl.when(away)
    def _():
        for copy in turn[:3]:
            copy.start()
        cast_rest()
        for which in (0, 1):
            turn[which].wait_recv()
            for copy in from_turned[which]:
                copy.start()
        turn[3].start()
        turn_rows[0].start()
        turn[3].wait_recv()
        from_turned[2][0].start()
        turn_rows[1].start()
        cross_over(0)
        turn_rows[0].wait_recv()
        pass_rows[0].start()
        for copy in turn[4:]:
            copy.start()
        turn_rows[1].wait_recv()
        pass_rows[1].start()

    @pl.when(at_home)
    def _():
        for copy in from_own[0] + from_own[1]:
            copy.start()
        cast_rest()
        for copy in from_own[2]:
            copy.start()
        for source, target in zip(own, ends):
            copy_rows(source, target)
        lay_down(tokens)
        cross_over(0)

    for k in range(1, zones - 1):
        cross_over(k)
    for which in (0, 1):
        from_turned[which][zones - 1].wait_recv()
        for copy in from_turned[which]:
            copy.wait_send()
        for copy in cross[which]:
            copy.wait_recv()
            copy.wait_send()
    from_turned[2][0].wait_recv()
    from_turned[2][0].wait_send()

    @pl.when(away)
    def _():
        for copy in pass_rows + turn[2:3] + turn[4:]:
            copy.wait_recv()
        lay_down(tokens_stage)
        for copy in turn + turn_rows + pass_rows:
            copy.wait_send()


def opening(plan, qkv, gains, gate, out, down, tokens, angles, number):
    low = jnp.bfloat16
    vmem = pl.BlockSpec(memory_space=pltpu.VMEM)
    like = lambda v: jax.ShapeDtypeStruct(v.shape, v.dtype)
    whole = lambda v: jax.ShapeDtypeStruct((2 * plan.zones,) + v.shape, low)
    operands = (qkv, gains, gate, out, down, tokens, angles)
    low_gate = jax.ShapeDtypeStruct((gate.shape[1], 2 * gate.shape[2]), low)
    low_out = jax.ShapeDtypeStruct(out.shape, low)
    low_down = jax.ShapeDtypeStruct(down.shape, low)
    outputs = [whole(qkv), whole(gains), low_gate, low_out, low_down, like(tokens), like(angles)]
    outputs += [low_gate]
    copies = 6 + 4 + 2 * plan.zones + 1 + 2 * (plan.zones - 1)
    return pl.pallas_call(
        functools.partial(opening_kernel, plan),
        out_shape=outputs,
        in_specs=[vmem] * len(operands),
        out_specs=[vmem] * len(outputs),
        scratch_shapes=[
            pltpu.SemaphoreType.DMA((copies,)),
            pltpu.SemaphoreType.DMA((copies,)),
            pltpu.VMEM(tokens.shape, tokens.dtype),
            pltpu.VMEM(qkv.shape, low),
            pltpu.VMEM(low_gate.shape, low),
            pltpu.VMEM(out.shape, low),
            pltpu.VMEM(down.shape, low),
        ],
        compiler_params=pltpu.CompilerParams(
            collective_id=number, has_side_effects=True, vmem_limit_bytes=56 * 2**20
        ),
        cost_estimate=pl.CostEstimate(flops=10**6, bytes_accessed=10**5, transcendentals=0),
        name="opening",
    )(*operands)


def inverse_rms(values):
    return lax.rsqrt(jnp.mean(values * values, -1, keepdims=True) + EPS_NORM)


def hidden_rows(own, sums, extras, outs):
    tokens, gain = extras
    hidden = tokens[own, :].astype(jnp.float32) + sums
    outs[0][own, :] = hidden
    return (hidden * inverse_rms(hidden) * gain[...]).astype(jnp.bfloat16)


def grad_hidden_rows(own, sums, extras, outs):
    hidden, out_grad, gain = extras
    values = hidden[own, :]
    factor = inverse_rms(values)
    unit = values * factor
    outs[1][...] += jnp.sum(sums * unit, 0, keepdims=True)
    grad = out_grad[own, :].astype(jnp.float32) + norm_back(sums * gain[...], unit, factor)
    outs[0][own, :] = grad
    return grad.astype(jnp.bfloat16)


def grad_input_rows(own, sums, extras, outs):
    tokens, grad_hidden, gain = extras[:3]
    values = tokens[own, :].astype(jnp.float32)
    factor = inverse_rms(values)
    unit = values * factor
    outs[0][...] += jnp.sum(sums * unit, 0, keepdims=True)
    return (grad_hidden[own, :] + norm_back(sums * gain[...], unit, factor)).astype(jnp.bfloat16)


def dot(left, right, left_dim=1, right_dim=0):
    return lax.dot_general(
        left, right, (((left_dim,), (right_dim,)), ((), ())), preferred_element_type=jnp.float32
    )


def turn_head(values, cosine, signed_sine):
    return values * cosine + pltpu.roll(values, HEAD // 2, 1) * signed_sine


def turn_back(gradient, cosine, signed_sine):
    return gradient * cosine + pltpu.roll(gradient * signed_sine, HEAD // 2, 1)


def softmax_block(query, key, first_row):
    rows, keys = query.shape[0], key.shape[0]
    scores = dot(query, key, 1, 1)
    row_at = lax.broadcasted_iota(jnp.int32, (rows, keys), 0) + first_row
    key_at = lax.broadcasted_iota(jnp.int32, (rows, keys), 1)
    scores = jnp.where(key_at <= row_at, scores, -1000000000.0)
    exponent = jnp.exp(scores - jnp.max(scores, -1, keepdims=True))
    return exponent / jnp.sum(exponent, -1, keepdims=True)


def eighth_owners():
    _, side, row, _ = place_here()
    own, off = (row, side), (1 - row, 1 - side)
    first = lambda x, y: x * 2 + y
    second = lambda x, y: 4 + y * 2 + x
    return [
        first(own[0], own[1]),
        first(own[0], off[1]),
        second(own[0], own[1]),
        second(off[0], own[1]),
        first(off[0], own[1]),
        first(off[0], off[1]),
        second(own[0], off[1]),
        second(off[0], off[1]),
    ]


def reorder_rows(source, target, into_local):
    size = source.shape[0] // 8
    for slot, owner in enumerate(eighth_owners()):
        natural = pl.ds(pl.multiple_of(owner * size, size), size)
        local = pl.ds(slot * size, size)
        if into_local:
            target[local, :] = source[natural, :]
        else:
            target[natural, :] = source[local, :]


def forward_kernel(
    tokens, weights, gain_in, gain_q, gain_k, cosine, sine,
    normed, raw, query, key, value, local, attended,
):
    low = jnp.bfloat16
    total, heads = tokens.shape[0], query.shape[1] // HEAD
    block, wide = 256, 512

    def project(step, carry):
        rows = pl.ds(pl.multiple_of(step * wide, wide), wide)
        values = tokens[rows, :].astype(jnp.float32)
        normed[rows, :] = (values * inverse_rms(values) * gain_in[...]).astype(low)
        raw[rows, :] = dot(normed[rows, :], weights[...])
        turns = (cosine[rows, :], sine[rows, :])
        for head in range(heads):
            column = (head // 2) * 4 * HEAD + (head % 2) * HEAD
            values = raw[rows, pl.ds(column, HEAD)]
            values = turn_head(values * inverse_rms(values) * gain_q[...], *turns)
            query[rows, pl.ds(head * HEAD, HEAD)] = (values * (1.0 / math.sqrt(HEAD))).astype(low)
        for group in range(heads // 2):
            column = group * 4 * HEAD + 2 * HEAD
            here = pl.ds(group * HEAD, HEAD)
            values = raw[rows, pl.ds(column, HEAD)]
            values = turn_head(values * inverse_rms(values) * gain_k[...], *turns)
            key[rows, here] = values.astype(low)
            value[rows, here] = raw[rows, pl.ds(column + HEAD, HEAD)].astype(low)
        return carry

    lax.fori_loop(0, total // wide, project, 0)

    def attend(head, carry):
        mine = pl.ds(pl.multiple_of(head * HEAD, HEAD), HEAD)
        shared = pl.ds(pl.multiple_of(lax.div(head, 2) * HEAD, HEAD), HEAD)
        for start in range(0, total, SEQ):
            for first in range(0, SEQ, block):
                rows, keys = pl.ds(start + first, block), pl.ds(start, first + block)
                probs = softmax_block(query[rows, mine], key[keys, shared], first)
                attended[rows, mine] = dot(probs.astype(low), value[keys, shared]).astype(low)
        return carry

    lax.fori_loop(0, heads, attend, 0)
    reorder_rows(attended, local, True)


def attention(tokens, weights, gain_in, gain_q, gain_k, cosine, sine):
    total = tokens.shape[0]
    columns = weights.shape[1]
    low = jnp.bfloat16
    shape = lambda width, kind=low: jax.ShapeDtypeStruct((total, width), kind)
    vmem = pl.BlockSpec(memory_space=pltpu.VMEM)
    return pl.pallas_call(
        forward_kernel,
        out_shape=[
            shape(tokens.shape[1]),
            shape(columns, jnp.float32),
            shape(columns // 2),
            shape(columns // 4),
            shape(columns // 4),
            shape(columns // 2),
        ],
        in_specs=[vmem] * 7,
        out_specs=[vmem] * 6,
        scratch_shapes=[pltpu.VMEM((total, columns // 2), low)],
        compiler_params=pltpu.CompilerParams(vmem_limit_bytes=48 * 2**20),
        cost_estimate=pl.CostEstimate(flops=10**6, bytes_accessed=10**5, transcendentals=0),
        name="attention",
    )(tokens, weights, gain_in, gain_q, gain_k, cosine, sine)


def backward_kernel(
    query, key, value, raw, grad_rows, gain_q, gain_k, cosine, sine,
    mixed, mixed_local, query_gain, key_gain, grad, key_sum, value_sum,
):
    low = jnp.bfloat16
    total, heads = query.shape[0], query.shape[1] // HEAD
    block = 256
    reorder_rows(grad_rows, grad, False)
    query_gain[...] = jnp.zeros_like(query_gain)
    key_gain[...] = jnp.zeros_like(key_gain)

    def head_norm_back(rows, column, gradient, gain, gain_grad):
        values = raw[rows, column]
        factor = inverse_rms(values)
        unit = values * factor
        turned = turn_back(gradient, cosine[rows, :], sine[rows, :])
        gain_grad[...] += jnp.sum(turned * unit, 0, keepdims=True)
        mixed[rows, column] = norm_back(turned * gain[...], unit, factor).astype(low)

    def one_group(group, carry):
        at = lambda offset: pl.ds(pl.multiple_of(group * 4 * HEAD + offset * HEAD, HEAD), HEAD)
        shared = pl.ds(pl.multiple_of(group * HEAD, HEAD), HEAD)
        key_sum[...] = jnp.zeros_like(key_sum)
        value_sum[...] = jnp.zeros_like(value_sum)
        for head in (0, 1):
            mine = pl.ds(pl.multiple_of((group * 2 + head) * HEAD, HEAD), HEAD)
            for start in range(0, total, SEQ):
                for first in range(0, SEQ, block):
                    rows, keys = pl.ds(start + first, block), pl.ds(start, first + block)
                    query_part, grad_part = query[rows, mine], grad[rows, mine]
                    probs = softmax_block(query_part, key[keys, shared], first)
                    weighed = probs * dot(grad_part, value[keys, shared], 1, 1)
                    scores = weighed - probs * jnp.sum(weighed, -1, keepdims=True)
                    scores = scores.astype(low)
                    grad_query = dot(scores, key[keys, shared]) * (1.0 / math.sqrt(HEAD))
                    head_norm_back(rows, at(head), grad_query, gain_q, query_gain)
                    key_sum[keys, :] += dot(scores, query_part, 0, 0)
                    value_sum[keys, :] += dot(probs.astype(low), grad_part, 0, 0)
        for first in range(0, total, block):
            rows = pl.ds(first, block)
            head_norm_back(rows, at(2), key_sum[rows, :], gain_k, key_gain)
            mixed[rows, at(3)] = value_sum[rows, :].astype(low)
        return carry

    lax.fori_loop(0, heads // 2, one_group, 0)
    reorder_rows(mixed, mixed_local, True)


def attention_back(query, key, value, raw, grad_rows, gain_q, gain_k, cosine, sine):
    total, columns = raw.shape
    low = jnp.bfloat16
    vmem = pl.BlockSpec(memory_space=pltpu.VMEM)
    return pl.pallas_call(
        backward_kernel,
        out_shape=[
            jax.ShapeDtypeStruct((total, columns), low),
            jax.ShapeDtypeStruct((total, columns), low),
            jax.ShapeDtypeStruct((1, HEAD), jnp.float32),
            jax.ShapeDtypeStruct((1, HEAD), jnp.float32),
        ],
        in_specs=[vmem] * 9,
        out_specs=[vmem] * 4,
        scratch_shapes=[
            pltpu.VMEM(grad_rows.shape, low),
            pltpu.VMEM((total, HEAD), jnp.float32),
            pltpu.VMEM((total, HEAD), jnp.float32),
        ],
        compiler_params=pltpu.CompilerParams(vmem_limit_bytes=48 * 2**20),
        cost_estimate=pl.CostEstimate(flops=10**6, bytes_accessed=10**5, transcendentals=0),
        name="attention_back",
    )(query, key, value, raw, grad_rows, gain_q, gain_k, cosine, sine)


def feed_kernel(plan, rows, own_grad, got_grad, gate_up, up_part, down, active, grads, out_grad):
    low = jnp.bfloat16
    block = 512
    tile = down.shape[1]
    step = pl.program_id(0)
    gate_at = pl.ds(pl.multiple_of(step * tile, tile), tile)
    up_at = pl.ds(pl.multiple_of(grads.shape[1] // 2 + step * tile, tile), tile)
    _, side, _, core = place_here()

    def lay_down(source):
        natural, blocks = block_columns(plan, source.shape[1])
        eighth = source.shape[0] // 8
        for slot, owner in enumerate(eighth_owners()):

            def some(start, count, slot=slot, owner=owner):
                here = pl.ds(pl.multiple_of(owner * eighth + start, 32), count)
                there = pl.ds(slot * eighth + start, count)
                for a, b in zip(natural, blocks):
                    out_grad[there, b] = source[here, a]

            for_rows(eighth, some)

    @pl.when((step == 0) & (side == core))
    def _():
        lay_down(own_grad)

    @pl.when((step == 0) & (side != core))
    def _():
        lay_down(got_grad)

    def one(block_at, carry):
        here = pl.ds(pl.multiple_of(block_at * block, block), block)
        gate = dot(rows[here, :], gate_up[...])
        up = dot(rows[here, :], up_part[...])
        grad = dot(out_grad[here, :], down[...])
        sigmoid = jax.nn.sigmoid(gate)
        silu = gate * sigmoid
        active[here, :] = (silu * up).astype(low)
        grads[here, gate_at] = (grad * up * sigmoid * (1.0 + gate * (1.0 - sigmoid))).astype(low)
        grads[here, up_at] = (grad * silu).astype(low)
        return carry

    lax.fori_loop(0, rows.shape[0] // block, one, 0)


def feed_forward(plan, rows, own_grad, got_grad, gate_up, down, tile):
    total, width = rows.shape
    units = down.shape[1]
    low = jnp.bfloat16
    tiles = units // tile
    whole = pl.BlockSpec(memory_space=pltpu.VMEM)
    return pl.pallas_call(
        functools.partial(feed_kernel, plan),
        grid=(tiles,),
        out_shape=[
            jax.ShapeDtypeStruct((total, units), low),
            jax.ShapeDtypeStruct((total, 2 * units), low),
            jax.ShapeDtypeStruct((total, width), low),
        ],
        in_specs=[
            whole,
            whole,
            whole,
            pl.BlockSpec((width, tile), lambda step: (0, step)),
            pl.BlockSpec((width, tile), lambda step: (0, step + tiles)),
            pl.BlockSpec((width, tile), lambda step: (0, step)),
        ],
        out_specs=[
            pl.BlockSpec((total, tile), lambda step: (0, step)),
            whole,
            whole,
        ],
        compiler_params=pltpu.CompilerParams(vmem_limit_bytes=56 * 2**20),
        cost_estimate=pl.CostEstimate(
            flops=6 * total * width * units, bytes_accessed=4 * 10**7, transcendentals=total * units
        ),
        name="feed_forward",
    )(rows, own_grad, got_grad, gate_up, gate_up, down)


class Plan:
    def __init__(self, mesh):
        self.total = mesh.shape["dp"]
        self.zones = self.total // 2
        self.tensor = mesh.shape["tensor"]
        self.flips = [k ^ (k >> 1) for k in range(self.zones)]

    def place(self):
        self.index = lax.axis_index("dp")
        self.zone = self.index // 2
        self.side = self.index % 2
        self.row = lax.axis_index("tensor") // 2
        self.core = lax.axis_index("tensor") % 2
        self.home = self.side == self.core

    def move(self, value, target):
        pairs = []
        for d in range(self.total):
            for t in range(self.tensor):
                to = target(d // 2, d % 2, t // 2, t % 2)
                if to is not None:
                    zone, side, row, core = to
                    pairs.append((d * self.tensor + t, (zone * 2 + side) * self.tensor + row * 2 + core))
        return lax.ppermute(value, ("dp", "tensor"), pairs)

    def turn(self, value):
        got = self.move(value, lambda z, y, x, c: (z, c, x, y) if y != c else None)
        return jnp.where(self.home, value, got)

    def zone_flip(self, value, bit):
        return self.move(value, lambda z, y, x, c: (z ^ bit, y, x, c))

    def core_swap(self, value):
        return self.move(value, lambda z, y, x, c: (z, y, x, 1 - c))

    def side_swap(self, value):
        return self.move(value, lambda z, y, x, c: (z, 1 - y, x, c))

    def row_swap(self, value):
        return self.move(value, lambda z, y, x, c: (z, y, 1 - x, c))

    def to_local(self, value, axis):
        width = value.shape[axis] // self.total
        parts = []
        for core in (self.core, 1 - self.core):
            for slot in range(self.zones):
                owner = (self.zone ^ self.flips[slot]) * 2 + core
                parts.append(lax.dynamic_slice_in_dim(value, owner * width, width, axis))
        return jnp.concatenate(parts, axis)

    def to_natural(self, value, axis, core=None):
        core = self.core if core is None else core
        width = value.shape[axis] // self.total
        parts = []
        for block in range(self.total):
            slot = flip = (block // 2) ^ self.zone
            for bits in range(1, self.zones.bit_length()):
                slot = slot ^ (flip >> bits)
            slot = slot + jnp.where(block % 2 == core, 0, self.zones)
            parts.append(lax.dynamic_slice_in_dim(value, slot * width, width, axis))
        return jnp.concatenate(parts, axis)

    def row_owners(self):
        own, off = (self.row, self.side), (1 - self.row, 1 - self.side)
        first = lambda x, y: x * 2 + y
        second = lambda x, y: 4 + y * 2 + x
        return [
            first(own[0], own[1]),
            first(own[0], off[1]),
            second(own[0], own[1]),
            second(off[0], own[1]),
            first(off[0], own[1]),
            first(off[0], off[1]),
            second(own[0], off[1]),
            second(off[0], off[1]),
        ]

    def rows_local(self, value, slots=range(8)):
        size = value.shape[0] // 8
        owners = self.row_owners()
        return jnp.concatenate(
            [lax.dynamic_slice_in_dim(value, owners[slot] * size, size, 0) for slot in slots], 0
        )

    def rows_natural(self, value, order=range(8)):
        size = value.shape[0] // 8
        place = [list(order).index(slot) for slot in range(8)]
        parts = []
        for piece in range(8):
            x, y = (piece // 2, piece % 2) if piece < 4 else (piece % 2, (piece - 4) // 2)
            slots = (0, 1, 4, 5) if piece < 4 else (2, 6, 3, 7)
            same_x, same_y = x == self.row, y == self.side
            slot = jnp.where(
                same_x,
                jnp.where(same_y, place[slots[0]], place[slots[1]]),
                jnp.where(same_y, place[slots[2]], place[slots[3]]),
            )
            parts.append(lax.dynamic_slice_in_dim(value, slot * size, size, 0))
        return jnp.concatenate(parts, 0)

    def from_zones(self, shard):
        return [self.zone_flip(shard, flip) for flip in self.flips[1:]]

    def to_zones(self, parts, slots):
        return [self.zone_flip(parts[slot], self.flips[slot]) for slot in slots]

    def middle_swap(self, pair):
        return self.move(pair, lambda z, y, x, c: (z ^ 3, y, x, c) if z in (1, 2) else None)

    def inward(self, part):
        return self.move(part, lambda z, y, x, c: (z ^ 1, y, x, c) if z in (0, 3) else None)

    def pass_outward(self, pair):
        return self.move(pair, lambda z, y, x, c: (z ^ 1, y, x, c) if z in (1, 2) else None)

    def far_pair(self, middle, passed):
        inner = (self.zone == 1) | (self.zone == 2)
        return jnp.where(inner, middle, passed[::-1])

    def first_swap(self, send):
        half = send.shape[0] // 2
        return self.row_swap(send[:half]), self.side_swap(send[half:])

    def second_swap(self, keep, got):
        quarter = keep.shape[0] // 4
        row_part = keep[: 2 * quarter] + got[0].astype(jnp.float32)
        side_part = keep[2 * quarter :] + got[1].astype(jnp.float32)
        own = jnp.concatenate([row_part[:quarter], side_part[:quarter]], 0)
        return own, (
            self.side_swap(row_part[quarter:].astype(jnp.bfloat16)),
            self.row_swap(side_part[quarter:].astype(jnp.bfloat16)),
        )

    def spread_first(self, own):
        half = own.shape[0] // 2
        return (self.side_swap(own[:half]), self.row_swap(own[half:]))

    def spread_second(self, own, got):
        half = own.shape[0] // 2
        row_part = jnp.concatenate([own[:half], got[0]], 0)
        side_part = jnp.concatenate([own[half:], got[1]], 0)
        return row_part, side_part, self.row_swap(row_part), self.side_swap(side_part)

    def send_home(self, own):
        to_home = lambda z, y, x, c: (z, c, x, c) if y != c else None
        return jnp.concatenate([own, self.move(own, to_home)], 0)

    def row_home(self, part):
        return self.move(part, lambda z, y, x, c: (z, y, 1 - x, c) if y == c else None)

    def share_home(self, part, other):
        full = jnp.concatenate([part, other], 0)
        full = self.to_natural(self.rows_natural(full, (0, 2, 1, 6, 4, 3, 5, 7)), 1)
        got = self.move(full, lambda z, y, x, c: (z, y, x, 1 - c) if y == c else None)
        return full, got

    def turned(self, own, got):
        return jnp.where(self.home, own, got)

    def sum_everywhere(self, value):
        value = value + self.row_swap(value)
        value = value + self.side_swap(value)
        value = value + self.core_swap(value)
        bit = 1
        while bit < self.zones:
            value = value + self.zone_flip(value, bit)
            bit *= 2
        return value


def shards(
    plan,
    tokens,
    positions,
    out_grad,
    qkv_weight,
    qkv_first,
    qkv_second,
    out_weight,
    out_first,
    out_second,
    gate_up,
    gate_up_first,
    gate_up_second,
    down_weight,
    down_first,
    down_second,
    gains,
    gains_first,
    gains_second,
):
    plan.place()
    low = jnp.bfloat16
    tok_rows, model_width = tokens.shape
    groups = qkv_weight.shape[1]
    head_size = qkv_weight.shape[3]
    shard_rows = qkv_weight.shape[0]
    seq_count = tok_rows // SEQ
    mixed_cols = groups * 4 * head_size
    near_cols = model_width // 2
    kept = tok_rows // 2
    gain_count = gains.shape[0]

    tree = plan.zones == 4
    slots = range(1, plan.zones)

    def column_parts(value):
        return value.reshape((plan.zones, -1) + value.shape[1:])

    units = gate_up.shape[2]
    plan.ordered = (model_width // plan.total) % 128 == 0
    gain_rows = 16
    gain_block = jnp.pad(gains.astype(low), (0, gain_rows * 128 - gain_count)).reshape(gain_rows, 128)
    tile = min(units, 256)
    angle_at = positions.astype(jnp.float32).reshape(-1, 128)
    both_qkv, both_gains, turned_gate, turned_out, turned_down, tokens, angle_at, partner_gate = opening(
        plan,
        qkv_weight.reshape(shard_rows, mixed_cols),
        gain_block,
        gate_up,
        out_weight,
        down_weight,
        tokens,
        angle_at,
        3,
    )
    positions = angle_at.reshape(-1)
    turned_out, turned_gate, turned_down, tokens, positions, both_qkv, both_gains, out_grad = fence(
        turned_out, turned_gate, turned_down, tokens, positions, both_qkv, both_gains, out_grad
    )

    got_grad = plan.move(out_grad, lambda z, y, x, c: (z, c, x, y) if y != c else None)
    zone_out = plan.from_zones(turned_out)
    if tree:
        partner_down = plan.zone_flip(turned_down, 1)
    else:
        partner_down = plan.from_zones(turned_down)
        partner_gate = plan.from_zones(turned_gate)
    if not plan.ordered:
        tokens = plan.to_local(tokens, 1)
    cosine, sine_table = rotary(positions, head_size)
    signed_sine = jnp.concatenate(
        [-sine_table[:, : head_size // 2], sine_table[:, head_size // 2 :]], 1
    )
    full_qkv = both_qkv.reshape(model_width, mixed_cols)
    gain_slots = both_gains.reshape(plan.total, -1)[:, :gain_count]
    gain_all = plan.to_natural(gain_slots.reshape(-1), 0).astype(jnp.float32)
    gain_in = plan.to_local(gain_all[:model_width], 0)[None]
    gain_post = plan.to_local(gain_all[model_width : 2 * model_width], 0)[None]
    gain_q = gain_all[2 * model_width : 2 * model_width + head_size][None]
    gain_k = gain_all[2 * model_width + head_size :][None]
    normed, raw, query, key_rot, values_low, attended = attention(
        tokens, full_qkv, gain_in, gain_q, gain_k, cosine, signed_sine
    )
    attended, zone_out, turned_out, turned_down, turned_gate, partner_gate, partner_down = fence(
        attended, zone_out, turned_out, turned_down, turned_gate, partner_gate, partner_down
    )

    near_out = jnp.concatenate([turned_out] + zone_out, 0)
    far_out = plan.core_swap(near_out)
    own_tokens = plan.rows_local(tokens, (0, 2))
    near_out, far_out, own_tokens = fence(near_out, far_out, own_tokens)

    full_out = jnp.concatenate([near_out, far_out], 0)
    branch_terms = contract_cols(attended, full_out).astype(low)
    pairs = [(turned_gate, partner_gate), (turned_down, partner_down)]
    jobs = [PairTree(pairs, (2, 2))] if tree else []
    normed_rows, hidden, *gathered = sum_rows(
        plan,
        spread_kernel,
        hidden_rows,
        branch_terms,
        [own_tokens, gain_post],
        [jax.ShapeDtypeStruct((tok_rows // 4, model_width), jnp.float32)],
        0,
        jobs,
    )
    if not tree:
        near = [jnp.concatenate([own] + rest, 0) for own, rest in pairs]
        gathered = [jnp.concatenate([part, plan.core_swap(part)], 0) for part in near]
    full_gate = gathered[0].reshape(model_width, 2 * units)
    full_down = gathered[1].reshape(model_width, units)
    normed_rows, hidden, full_gate, full_down, got_grad = fence(
        normed_rows, hidden, full_gate, full_down, got_grad
    )

    def zone_parts(near, got):
        both = (near + got.astype(jnp.float32)).astype(low)
        return both.reshape((plan.zones, -1) + both.shape[1:])

    def zone_total(parts, *arrived):
        total = parts[0].astype(jnp.float32)
        for part in sum([list(group) for group in arrived], []):
            total = total + part.astype(jnp.float32)
        return total.astype(low)

    active, grad_both, out_grad = feed_forward(
        plan, normed_rows, out_grad, got_grad, full_gate, full_down, tile
    )
    if not plan.ordered:
        out_grad = plan.to_local(out_grad, 1)
    gate_far = contract_rows(normed_rows[:, near_cols:], grad_both).astype(low)
    gate_far, active, grad_both, out_grad, normed_rows = fence(
        gate_far, active, grad_both, out_grad, normed_rows
    )

    gate_got = plan.core_swap(gate_far)
    down_far = contract_rows(out_grad[:, near_cols:], active).astype(low)
    gate_got, down_far, active, grad_both, normed_rows = fence(
        gate_got, down_far, active, grad_both, normed_rows
    )

    down_got = plan.core_swap(down_far)
    gate_parts = zone_parts(contract_rows(normed_rows[:, :near_cols], grad_both), gate_got)
    gate_parts, down_got, grad_both, active, out_grad = fence(
        gate_parts, down_got, grad_both, active, out_grad
    )

    half_rows = shard_rows // 2
    if tree:
        gate_ready = [plan.inward(gate_parts[3, :half_rows])]
    else:
        gate_ready = [gate_parts[0]]
    post_terms = contract_cols(grad_both, full_gate).astype(low)
    post_terms, gate_parts, gate_ready, down_got, active, out_grad = fence(
        post_terms, gate_parts, gate_ready, down_got, active, out_grad
    )
    if tree:
        gate_ready += [plan.inward(gate_parts[3, half_rows:])]
    down_parts = zone_parts(contract_rows(out_grad[:, :near_cols], active), down_got)
    post_terms, gate_parts, gate_ready, down_parts = fence(
        post_terms, gate_parts, gate_ready, down_parts
    )
    gate_ready = jnp.concatenate(gate_ready, 0)

    if tree:
        down_sums = [plan.inward(down_parts[3]), plan.inward(down_parts[2])]
    else:
        down_sums = plan.to_zones(down_parts, slots)
    eighth = tok_rows // 8
    own_grad = jnp.concatenate([out_grad[:eighth], out_grad[2 * eighth : 3 * eighth]], 0)
    branch_rows, grad_hidden, post_gain_grad, mlp_terms, gate_sums = sum_rows(
        plan,
        spread_kernel,
        grad_hidden_rows,
        post_terms,
        [hidden, own_grad, gain_post],
        [
            jax.ShapeDtypeStruct((tok_rows // 4, model_width), jnp.float32),
            jax.ShapeDtypeStruct((1, model_width), jnp.float32),
        ],
        1,
        [
            SideDot(active, full_down),
            PairScatter(gate_parts, gate_ready, 2) if tree else ZoneBlocks(plan, gate_parts, slots),
        ],
    )
    branch_rows, grad_hidden, post_gain_grad, gate_sums, mlp_terms, down_parts, down_sums = fence(
        branch_rows, grad_hidden, post_gain_grad, gate_sums, mlp_terms, down_parts, down_sums
    )

    mlp_got = plan.first_swap(mlp_terms[kept:])
    if tree:
        gate_last = [plan.zone_flip(gate_sums[1], 1)]
        gate_own = gate_sums
        down_pair = down_parts[2:].astype(jnp.float32) + jnp.stack(down_sums).astype(jnp.float32)
        down_sums = plan.middle_swap(down_pair.astype(low))
    else:
        gate_last, gate_own = gate_sums, gate_parts
    grad_att = jnp.dot(branch_rows, full_out, preferred_element_type=jnp.float32).astype(low)
    grad_mixed, mixed_rows, query_gain_grad, key_gain_grad = attention_back(
        query, key_rot, values_low, raw, grad_att, gain_q, gain_k, cosine, signed_sine
    )
    gain_terms = jnp.concatenate(
        [plan.to_natural(post_gain_grad, 1), query_gain_grad, key_gain_grad], 1
    )
    if tree:
        down_own = (down_parts[:2].astype(jnp.float32) + down_sums.astype(jnp.float32)).astype(low)
    grad_mixed, mixed_rows, gain_terms, normed, gate_last, branch_rows, mlp_got, down_sums = fence(
        grad_mixed, mixed_rows, gain_terms, normed, gate_last, branch_rows, mlp_got, down_sums
    )

    mlp_own, mlp_last = plan.second_swap(mlp_terms[:kept].astype(jnp.float32), mlp_got)
    if tree:
        total_down = zone_total(down_own, [plan.zone_flip(down_own[1], 1)])
    else:
        total_down = zone_total(down_parts, down_sums)
    total_gate = zone_total(gate_own, gate_last)
    summed_gate = plan.turn(jnp.stack([total_gate[:, :units], total_gate[:, units:]]))
    out_far = contract_rows(branch_rows[:, near_cols:], attended).astype(low)
    out_got = plan.core_swap(out_far)
    normed_terms = contract_cols(mixed_rows, full_qkv).astype(low)
    out_parts = zone_parts(contract_rows(branch_rows[:, :near_cols], attended), out_got)
    block_own = (hidden + mlp_own + jnp.concatenate(mlp_last, 0).astype(jnp.float32)).astype(low)
    out_parts, normed_terms, summed_gate, total_down, block_own, normed, grad_mixed = fence(
        out_parts, normed_terms, summed_gate, total_down, block_own, normed, grad_mixed
    )

    gain_sum = GainSum(plan, gain_terms.shape[1], model_width) if plan.ordered else None
    mine, input_gain_grad, *rest = sum_rows(
        plan,
        home_kernel,
        grad_input_rows,
        normed_terms,
        [own_tokens, grad_hidden, gain_in, block_own] + ([gain_terms] if plan.ordered else []),
        [jax.ShapeDtypeStruct((1, model_width), jnp.float32)],
        2,
        [BlockGrad(plan, normed, grad_mixed), ZoneBlocks(plan, out_parts, slots)],
        gain_sum,
    )
    if plan.ordered:
        summed_gains, total_qkv, out_sent = rest
    else:
        total_qkv, out_sent = rest
        summed_gains = plan.sum_everywhere(
            jnp.concatenate([plan.to_natural(input_gain_grad, 1), gain_terms], 1)
        )
    mine, summed_gains, total_qkv, out_sent, total_down = fence(
        mine, summed_gains, total_qkv, out_sent, total_down
    )

    summed_down = plan.turn(total_down)
    other = plan.core_swap(mine)
    input_full, block_out = jnp.where(plan.home, mine, other), jnp.where(plan.home, other, mine)
    if not plan.ordered:
        input_full = plan.to_natural(input_full, 1, plan.side)
        block_out = plan.to_natural(block_out, 1, plan.side)
    summed_both = plan.turn(
        jnp.concatenate([total_qkv, zone_total(out_parts, out_sent)], 1)
    ).astype(jnp.float32)
    summed_qkv = summed_both[:, :mixed_cols].reshape(qkv_weight.shape)
    summed_out = summed_both[:, mixed_cols:]
    summed_gate = summed_gate.astype(jnp.float32)
    summed_down = summed_down.astype(jnp.float32)
    summed_gains = lax.dynamic_slice_in_dim(summed_gains[0], plan.index * gain_count, gain_count, 0)
    input_rows = input_full.astype(jnp.float32)

    qkv_moment, qkv_square, qkv_updated = adamw(
        qkv_weight, summed_qkv, qkv_first, qkv_second, RATE_QKV, DECAY_RATE
    )
    out_moment, out_square, out_updated = adamw(
        out_weight, summed_out, out_first, out_second, RATE_OUT, DECAY_RATE
    )
    gate_moment, gate_square, gate_updated = adamw(
        gate_up, summed_gate, gate_up_first, gate_up_second, RATE_GATE, DECAY_RATE
    )
    down_moment, down_square, down_updated = adamw(
        down_weight, summed_down, down_first, down_second, RATE_DOWN, DECAY_RATE
    )
    gain_moment, gain_square, gain_updated = adamw(
        gains, summed_gains, gains_first, gains_second, RATE_GAIN, 0.0
    )
    return (
        block_out,
        input_rows,
        qkv_moment,
        qkv_square,
        qkv_updated,
        out_moment,
        out_square,
        out_updated,
        gate_moment,
        gate_square,
        gate_updated,
        down_moment,
        down_square,
        down_updated,
        gain_moment,
        gain_square,
        gain_updated,
    )


def solution(mesh):
    plan = Plan(mesh)
    placed = (
        P("dp", None),
        P("dp"),
        P("dp", None),
        P("dp", "tensor", None, None),
        P("dp", "tensor", None, None),
        P("dp", "tensor", None, None),
        P("dp", "tensor"),
        P("dp", "tensor"),
        P("dp", "tensor"),
        P(None, "dp", "tensor"),
        P(None, "dp", "tensor"),
        P(None, "dp", "tensor"),
        P("dp", "tensor"),
        P("dp", "tensor"),
        P("dp", "tensor"),
        P("dp"),
        P("dp"),
        P("dp"),
    )
    return jax.shard_map(
        functools.partial(shards, plan),
        mesh=mesh,
        in_specs=placed,
        out_specs=(
            P("dp", None),
            P("dp", None),
            P("dp", "tensor", None, None),
            P("dp", "tensor", None, None),
            P("dp", "tensor", None, None),
            P("dp", "tensor"),
            P("dp", "tensor"),
            P("dp", "tensor"),
            P(None, "dp", "tensor"),
            P(None, "dp", "tensor"),
            P(None, "dp", "tensor"),
            P("dp", "tensor"),
            P("dp", "tensor"),
            P("dp", "tensor"),
            P("dp"),
            P("dp"),
            P("dp"),
        ),
        check_vma=False,
    )
```

profile of v0, /device:TPU:1, one launch (start us, length us, event | category | flops | bytes accessed | tf_op | source)
XLA Modules:
  0.0 706.6 jit_solution(14329513874745622484)
XLA Ops:
  0.7 2.6 reshape.92.wide_qkv
  5.8 84.2 %opening.1 = (bf16[8,256,1024]{2,1,0:T(8,128)(2,1)}, bf16[8,16,128]{2,1,0:T(8,128)(2,1)}, bf16[256,3072]{1,0:T(8,128)(2,1)}, bf16[256,512]{1,0:T(8,128)(2,1)}, b...) custom-call(f32[256,1024]{1,0:T(8,128)} %reshape.92.wide_qkv, ...), custom_call_target="tpu_custom_call" | custom-call | flops 1000000 | bytes 100000 | tf_op jit(solution)/shard_map/opening/pallas_call | solution.py:1071
  90.0 1.3 collective-permute-start
  92.7 2.2 collective-permute-start.3
  94.9 3.7 collective-permute-start.5
  100.5 2.6 fusion.24
  103.6 21.4 %attention.1 = (bf16[1024,2048]{1,0:T(8,128)(2,1)}, f32[1024,1024]{1,0:T(8,128)}, bf16[1024,512]{1,0:T(8,128)(2,1)S(1)}, bf16[1024,256]{1,0:T(8,128)(2,1)S(1)}, ...) custom-call(bf16[1024,2048]{1,0:T(8,128)(2,1)} %get-tuple-element.137.tokens, bf16[2048,1024]{1,0:T(8,128)(2,1)} %bitcast.73, ...), custom_call_target="tpu_custom_call" | custom-call | flops 1000000 | bytes 100000 | tf_op jit(solution)/shard_map/attention/pallas_call | solution.py:1226
  130.4 4.4 convolution_convert_fusion.2.terms
  134.8 136.4 %hidden_rows.1 = (bf16[1024,2048]{1,0:T(8,128)(2,1)}, f32[256,2048]{1,0:T(8,128)}, bf16[8,256,3072]{2,1,0:T(8,128)(2,1)}, bf16[8,256,1536]{2,1,0:T(8,128)(2,1)}) custom-call(bf16[1024,2048]{1,0:T(8,128)(2,1)} %convolution_convert_fusion.2.terms, bf16[256,2048]{1,0:T(8,128)(2,1)} %pad_maximum_fusion.2.refs_0_, f32[1,2048]{1,0:T(1,128)} %bitcast.79, ...), custom_call_target="tpu_custom_call" | custom-call | flops 1000000 | bytes 100000 | tf_op jit(solution)/shard_map/hidden_rows/pallas_call | solution.py:885
  271.3 33.8 %feed_forward.1 = (bf16[1024,1536]{1,0:T(8,128)(2,1)}, bf16[1024,3072]{1,0:T(8,128)(2,1)}, bf16[1024,2048]{1,0:T(8,128)(2,1)}) custom-call(bf16[1024,2048]{1,0:T(8,128)(2,1)} %get-tuple-element.179.rows, bf16[1024,2048]{1,0:T(8,128)(2,1)} %own_grad, bf16[1024,2048]{1,0:T(8,128)(2,1)} %collective-permute-done.5.got_grad, bf16[2048,3072]{1,0:T(8,128)(2,1)} %bitcast.82, ...), custom_call_target="tpu_custom_call" | custom-call | flops 19327352832 | bytes 40000000 | tf_op jit(solution)/shard_map/feed_forward/pallas_call | solution.py:1369
  305.1 10.1 %convolution_convert_fusion = bf16[1024,3072]{1,0:T(8,128)(2,1)S(1)} fusion(bf16[1024,3072]{1,0:T(8,128)(2,1)} %get-tuple-element.184, bf16[1024,2048]{1,0:T(8,128)(2,1)S(1)} %copy-done.35), kind=kOutput, calls=%fused_computation.2 | convolution fusion | flops 6445596672 | bytes 14680064 | tf_op jit(solution)/shard_map/dot_general | solution.py:55
  315.5 4.8 convolution_convert_fusion.3
  320.3 5.3 collective-permute-done.6
  325.7 11.1 %add_convert_fusion = bf16[1024,3072]{1,0:T(8,128)(2,1)S(1)} fusion(bf16[1024,3072]{1,0:T(8,128)(2,1)} %collective-permute-done.6, bf16[1024,3072]{1,0:T(8,128)(2,1)} %get-tuple-element.184, bf16[1024,2048]{1,0:T(8,128)(2,1)} %get-tuple-element.179.rows), kind=kOutput, calls=%fused_computation | convolution fusion | flops 6451888128 | bytes 20971520 | tf_op jit(solution)/shard_map/dot_general | solution.py:55
  336.9 1.3 collective-permute-start.8
  338.3 20.0 %convolution_convert_fusion.1.terms = bf16[1024,2048]{1,0:T(8,128)(2,1)} fusion(bf16[1024,3072]{1,0:T(8,128)(2,1)} %get-tuple-element.184, bf16[2048,3072]{1,0:T(8,128)(2,1)} %bitcast.84), kind=kOutput, calls=%fused_computation.7 | convolution fusion | flops 12886999040 | bytes 23068672 | tf_op jit(solution)/shard_map/dot_general | solution.py:61
  360.5 7.0 add_convert_fusion.1
  367.5 9.4 %collective-permute-done.9 = bf16[128,3072]{1,0:T(8,128)(2,1)S(1)} collective-permute-done((bf16[128,3072]{1,0:T(8,128)(2,1)S(1)}, bf16[128,3072]{1,0:T(8,128)(2,1)S(1)}, u32[]{:S(2)}, u32[]{:S(2)}) %collective-permute-start.9) | collective-permute-done | bytes 786464 | tf_op jit(solution)/shard_map/ppermute | solution.py:1421
  378.1 5.0 collective-permute-start.10
  383.1 2.2 collective-permute-start.11
  389.0 86.0 %grad_hidden_rows.1 = (bf16[1024,2048]{1,0:T(8,128)(2,1)}, f32[256,2048]{1,0:T(8,128)}, f32[1,2048]{1,0:T(1,128)}, bf16[1024,2048]{1,0:T(8,128)(2,1)}, bf16[2,256,3072]{2,1,0:T(8,128)(2,1)}) custom-call(bf16[1024,2048]{1,0:T(8,128)(2,1)} %convolution_convert_fusion.1.terms, f32[256,2048]{1,0:T(8,128)} %get-tuple-element.196.refs_0_, ...), custom_call_target="tpu_custom_call" | custom-call | flops 1000000 | bytes 100000 | tf_op jit(solution)/shard_map/grad_hidden_rows/pallas_call | solution.py:885
  475.1 5.3 convolution_convert_fusion.5.grad_rows
  482.1 1.6 fusion.34
  484.9 3.6 collective-permute-start.14
  488.5 2.9 add_convert_fusion.3
  491.4 2.3 collective-permute-start.15
  493.7 22.8 %attention_back.1 = (bf16[1024,1024]{1,0:T(8,128)(2,1)}, bf16[1024,1024]{1,0:T(8,128)(2,1)}, f32[1,128]{1,0:T(1,128)S(1)}, f32[1,128]{1,0:T(1,128)S(1)}) custom-call(bf16[1024,512]{1,0:T(8,128)(2,1)S(1)} %get-tuple-element.141.query, bf16[1024,256]{1,0:T(8,128)(2,1)S(1)} %get-tuple-element.142.key, bf16[1024,256]{1,0:T(8,128)(2,1)S(1)} %get-tuple-element.143.value, ...), custom_call_target="tpu_custom_call" | custom-call | flops 1000000 | bytes 100000 | tf_op jit(solution)/shard_map/attention_back/pallas_call | solution.py:1297
  519.1 2.3 fusion.16
  521.4 3.4 collective-permute-start.16
  524.8 2.0 fusion.2
  527.1 3.4 collective-permute-start.17
  530.5 1.8 add_convert_fusion.2
  532.4 6.5 collective-permute-start.18
  538.8 2.1 slice_add_fusion.1
  542.2 7.9 %convolution_convert_fusion.4.terms = bf16[1024,2048]{1,0:T(8,128)(2,1)} fusion(bf16[1024,1024]{1,0:T(8,128)(2,1)} %get-tuple-element.219, bf16[2048,1024]{1,0:T(8,128)(2,1)S(1)} %bitcast.74), kind=kOutput, calls=%fused_computation.10 | convolution fusion | flops 4297064448 | bytes 10485760 | tf_op jit(solution)/shard_map/dot_general | solution.py:61
  550.3 4.3 collective-permute-done.20
  554.6 4.4 collective-permute-done.19
  559.1 1.5 fusion.4.refs_3_
  561.7 3.5 add_convert_fusion.4
  565.4 103.8 %grad_input_rows.1 = (bf16[1024,2048]{1,0:T(8,128)(2,1)}, f32[1,2048]{1,0:T(1,128)}, f32[1,4352]{1,0:T(1,128)}, bf16[256,1024]{1,0:T(8,128)(2,1)}, bf16[3,256,512]{2,1,0:T(8,128)(2,1)}) custom-call(bf16[1024,2048]{1,0:T(8,128)(2,1)} %convolution_convert_fusion.4.terms, bf16[256,2048]{1,0:T(8,128)(2,1)} %pad_maximum_fusion.2.refs_0_, ...), custom_call_target="tpu_custom_call" | custom-call | flops 1000000 | bytes 100000 | tf_op jit(solution)/shard_map/grad_input_rows/pallas_call | solution.py:885
  671.7 1.9 collective-permute-start.22
  673.6 3.6 collective-permute-start.23
  678.7 6.1 multiply_subtract_fusion
  686.3 2.8 reshape.104
  689.1 2.8 multiply_subtract_fusion.3
  691.9 3.2 multiply_subtract_fusion.2
  695.2 4.4 multiply_subtract_fusion.1
  699.6 6.8 select_convert_fusion
  (174 shorter events, 32.8 us)
Async XLA Ops:
  90.0 35.2 %collective-permute-start = (bf16[256,512]{1,0:T(8,128)(2,1)}, bf16[256,512]{1,0:T(8,128)(2,1)S(1)}, u32[]{:S(2)}, u32[]{:S(2)}) collective-permute-start(bf16[256,512]{1,0:T(8,128)(2,1)} %get-tuple-element.151), channel_id=1, source_target_pairs={{0,8},{1,9},{2,10},{3,11},{4,12},{5,13},{6,14},{7,15},{8,0},{9,1},... | collective-permute-start | bytes 786440 | tf_op jit(solution)/shard_map/ppermute | solution.py:1421
  91.3 33.9 %collective-permute-start.1 = (bf16[256,512]{1,0:T(8,128)(2,1)}, bf16[256,512]{1,0:T(8,128)(2,1)}, u32[]{:S(2)}, u32[]{:S(2)}) collective-permute-start(bf16[256,512]{1,0:T(8,128)(2,1)} %get-tuple-element.151), channel_id=1, source_target_pairs={{0,24},{1,25},{2,26},{3,27},{4,28},{5,29},{6,30},{7,31},{8,16},{9,... | collective-permute-start | bytes 786440 | tf_op jit(solution)/shard_map/ppermute | solution.py:1421
  92.5 32.7 %collective-permute-start.2 = (bf16[256,512]{1,0:T(8,128)(2,1)}, bf16[256,512]{1,0:T(8,128)(2,1)}, u32[]{:S(2)}, u32[]{:S(2)}) collective-permute-start(bf16[256,512]{1,0:T(8,128)(2,1)} %get-tuple-element.151), channel_id=1, source_target_pairs={{0,16},{1,17},{2,18},{3,19},{4,20},{5,21},{6,22},{7,23},{8,24},{9,... | collective-permute-start | bytes 786440 | tf_op jit(solution)/shard_map/ppermute | solution.py:1421
  92.7 32.5 %collective-permute-start.3 = (bf16[256,1536]{1,0:T(8,128)(2,1)}, bf16[256,1536]{1,0:T(8,128)(2,1)}, u32[]{:S(2)}, u32[]{:S(2)}) collective-permute-start(bf16[256,1536]{1,0:T(8,128)(2,1)} %get-tuple-element.160.refs_4_), channel_id=1, source_target_pairs={{0,8},{1,9},{2,10},{3,11},{4,12},{5,13},{6,14},{7,15},{8,0},{9,1},... | collective-permute-start | bytes 2359304 | tf_op jit(solution)/shard_map/ppermute | solution.py:1421
  94.9 176.4 %collective-permute-start.5 = (bf16[1024,2048]{1,0:T(8,128)(2,1)}, bf16[1024,2048]{1,0:T(8,128)(2,1)}, u32[]{:S(2)}, u32[]{:S(2)}) collective-permute-start(bf16[1024,2048]{1,0:T(8,128)(2,1)} %own_grad), channel_id=1, source_target_pairs={{1,4},{3,6},{4,1},{6,3},{9,12},{11,14},{12,9},{14,11},{17,20},{19,... | collective-permute-start | bytes 12582920 | tf_op jit(solution)/shard_map/ppermute | solution.py:1421
  103.6 21.4 %copy-start = (f32[2048]{0:T(1024)}, f32[2048]{0:T(1024)S(1)}, u32[]{:S(2)}) copy-start(f32[2048]{0:T(1024)S(1)} %constant_dynamic-update-slice_fusion.26) | copy-start | bytes 24580
  103.6 21.6 %copy-start.27 = (bf16[256,512]{1,0:T(8,128)(2,1)S(1)}, bf16[256,512]{1,0:T(8,128)(2,1)}, u32[]{:S(2)}) copy-start(bf16[256,512]{1,0:T(8,128)(2,1)} %get-tuple-element.151) | copy-start | bytes 786436
  125.0 5.4 copy-start.1
  127.4 2.9 collective-permute-start.4
  130.4 4.4 copy-start.25
  271.3 33.8 %copy-start.35 = (bf16[1024,2048]{1,0:T(8,128)(2,1)S(1)}, bf16[1024,2048]{1,0:T(8,128)(2,1)}, u32[]{:S(2)}) copy-start(bf16[1024,2048]{1,0:T(8,128)(2,1)} %get-tuple-element.179.rows) | copy-start | bytes 12582916
  305.1 10.4 %copy-start.15 = (bf16[1024,1536]{1,0:T(8,128)(2,1)S(1)}, bf16[1024,1536]{1,0:T(8,128)(2,1)}, u32[]{:S(2)}) copy-start(bf16[1024,1536]{1,0:T(8,128)(2,1)} %get-tuple-element.193.refs_3_) | copy-start | bytes 9437188
  305.1 10.4 %copy-start.26 = (bf16[1024,2048]{1,0:T(8,128)(2,1)S(1)}, bf16[1024,2048]{1,0:T(8,128)(2,1)}, u32[]{:S(2)}) copy-start(bf16[1024,2048]{1,0:T(8,128)(2,1)} %get-tuple-element.192) | copy-start | bytes 12582916
  315.2 10.4 %collective-permute-start.6 = (bf16[1024,3072]{1,0:T(8,128)(2,1)S(1)}, bf16[1024,3072]{1,0:T(8,128)(2,1)}, u32[]{:S(2)}, u32[]{:S(2)}) collective-permute-start(bf16[1024,3072]{1,0:T(8,128)(2,1)S(1)} %convolution_convert_fusion), channel_id=1, source_target_pairs={{0,1},{1,0},{2,3},{3,2},{4,5},{5,4},{6,7},{7,6},{8,9},{9,8},{10,11... | collective-permute-start | bytes 18874376 | tf_op jit(solution)/shard_map/ppermute | solution.py:1421
  325.6 11.3 %collective-permute-start.7 = (bf16[1024,1536]{1,0:T(8,128)(2,1)}, bf16[1024,1536]{1,0:T(8,128)(2,1)}, u32[]{:S(2)}, u32[]{:S(2)}) collective-permute-start(bf16[1024,1536]{1,0:T(8,128)(2,1)} %convolution_convert_fusion.3), channel_id=1, source_target_pairs={{0,1},{1,0},{2,3},{3,2},{4,5},{5,4},{6,7},{7,6},{8,9},{9,8},{10,11... | collective-permute-start | bytes 9437192 | tf_op jit(solution)/shard_map/ppermute | solution.py:1421
  336.8 21.5 %copy-start.4 = (bf16[1024,3072]{1,0:T(8,128)(2,1)}, bf16[1024,3072]{1,0:T(8,128)(2,1)S(1)}, u32[]{:S(2)}) copy-start(bf16[1024,3072]{1,0:T(8,128)(2,1)S(1)} %add_convert_fusion) | copy-start | bytes 18874372
  336.9 21.4 %collective-permute-start.8 = (bf16[128,3072]{1,0:T(8,128)(2,1)S(1)}, bf16[128,3072]{1,0:T(8,128)(2,1)S(1)}, u32[]{:S(2)}, u32[]{:S(2)}) collective-permute-start(bf16[128,3072]{1,0:T(8,128)(2,1)S(1)} %slice_bitcast_fusion.8), channel_id=1, source_target_pairs={{0,8},{1,9},{2,10},{3,11},{4,12},{5,13},{6,14},{7,15},{24,16},{25,... | collective-permute-start | bytes 2359304 | tf_op jit(solution)/shard_map/ppermute | solution.py:1421
  359.2 17.7 %collective-permute-start.9 = (bf16[128,3072]{1,0:T(8,128)(2,1)S(1)}, bf16[128,3072]{1,0:T(8,128)(2,1)S(1)}, u32[]{:S(2)}, u32[]{:S(2)}) collective-permute-start(bf16[128,3072]{1,0:T(8,128)(2,1)S(1)} %slice_bitcast_fusion.7), channel_id=1, source_target_pairs={{0,8},{1,9},{2,10},{3,11},{4,12},{5,13},{6,14},{7,15},{24,16},{25,... | collective-permute-start | bytes 2359304 | tf_op jit(solution)/shard_map/ppermute | solution.py:1421
  376.9 10.9 %copy-start.24 = (bf16[128,3072]{1,0:T(8,128)(2,1)S(1)}, bf16[128,3072]{1,0:T(8,128)(2,1)}, u32[]{:S(2)}) copy-start(bf16[128,3072]{1,0:T(8,128)(2,1)} %copy-done.23) | copy-start | bytes 2359300
  378.1 97.0 %collective-permute-start.10 = (bf16[256,1536]{1,0:T(8,128)(2,1)}, bf16[256,1536]{1,0:T(8,128)(2,1)}, u32[]{:S(2)}, u32[]{:S(2)}) collective-permute-start(bf16[256,1536]{1,0:T(8,128)(2,1)} %get-tuple-element.269), channel_id=1, source_target_pairs={{0,8},{1,9},{2,10},{3,11},{4,12},{5,13},{6,14},{7,15},{24,16},{25,... | collective-permute-start | bytes 2359304 | tf_op jit(solution)/shard_map/ppermute | solution.py:1421
  383.1 92.0 %collective-permute-start.11 = (bf16[256,1536]{1,0:T(8,128)(2,1)}, bf16[256,1536]{1,0:T(8,128)(2,1)}, u32[]{:S(2)}, u32[]{:S(2)}) collective-permute-start(bf16[256,1536]{1,0:T(8,128)(2,1)} %get-tuple-element.268), channel_id=1, source_target_pairs={{0,8},{1,9},{2,10},{3,11},{4,12},{5,13},{6,14},{7,15},{24,16},{25,... | collective-permute-start | bytes 2359304 | tf_op jit(solution)/shard_map/ppermute | solution.py:1421
  475.1 5.3 copy-start.13
  475.1 7.0 copy-start.7
  481.7 35.5 %collective-permute-start.12 = (bf16[256,3072]{1,0:T(8,128)(2,1)}, bf16[256,3072]{1,0:T(8,128)(2,1)}, u32[]{:S(2)}, u32[]{:S(2)}) collective-permute-start(bf16[256,3072]{1,0:T(8,128)(2,1)} %slice_bitcast_fusion), channel_id=1, source_target_pairs={{0,8},{1,9},{2,10},{3,11},{4,12},{5,13},{6,14},{7,15},{8,0},{9,1},... | collective-permute-start | bytes 4718600 | tf_op jit(solution)/shard_map/ppermute | solution.py:1421
  483.7 10.0 %copy-start.31 = (f32[1,2048]{1,0:T(1,128)S(1)}, f32[1,2048]{1,0:T(1,128)}, u32[]{:S(2)}) copy-start(f32[1,2048]{1,0:T(1,128)} %get-tuple-element.209) | copy-start | bytes 24580
  483.7 33.5 %collective-permute-start.13 = (bf16[256,2048]{1,0:T(8,128)(2,1)}, bf16[256,2048]{1,0:T(8,128)(2,1)}, u32[]{:S(2)}, u32[]{:S(2)}) collective-permute-start(bf16[256,2048]{1,0:T(8,128)(2,1)} %get-tuple-element.263), channel_id=1, source_target_pairs={{0,2},{1,3},{2,0},{3,1},{4,6},{5,7},{6,4},{7,5},{8,10},{9,11},{10,... | collective-permute-start | bytes 3145736 | tf_op jit(solution)/shard_map/ppermute | solution.py:1421
  484.9 32.3 %collective-permute-start.14 = (bf16[256,2048]{1,0:T(8,128)(2,1)}, bf16[256,2048]{1,0:T(8,128)(2,1)}, u32[]{:S(2)}, u32[]{:S(2)}) collective-permute-start(bf16[256,2048]{1,0:T(8,128)(2,1)} %get-tuple-element.262), channel_id=1, source_target_pairs={{0,4},{1,5},{2,6},{3,7},{4,0},{5,1},{6,2},{7,3},{8,12},{9,13},{10,... | collective-permute-start | bytes 3145736 | tf_op jit(solution)/shard_map/ppermute | solution.py:1421
  491.4 25.9 %collective-permute-start.15 = (bf16[2,256,1536]{2,1,0:T(8,128)(2,1)}, bf16[2,256,1536]{2,1,0:T(8,128)(2,1)}, u32[]{:S(2)}, u32[]{:S(2)}) collective-permute-start(bf16[2,256,1536]{2,1,0:T(8,128)(2,1)} %add_convert_fusion.3), channel_id=1, source_target_pairs={{8,16},{9,17},{10,18},{11,19},{12,20},{13,21},{14,22},{15,23},{16,... | collective-permute-start | bytes 4718600 | tf_op jit(solution)/shard_map/ppermute | solution.py:1421
  519.1 5.6 copy-start.14
  521.4 40.3 %collective-permute-start.16 = (bf16[1024,512]{1,0:T(8,128)(2,1)}, bf16[1024,512]{1,0:T(8,128)(2,1)}, u32[]{:S(2)}, u32[]{:S(2)}) collective-permute-start(bf16[1024,512]{1,0:T(8,128)(2,1)} %fusion.16), channel_id=1, source_target_pairs={{0,1},{1,0},{2,3},{3,2},{4,5},{5,4},{6,7},{7,6},{8,9},{9,8},{10,11... | collective-permute-start | bytes 3145736 | tf_op jit(solution)/shard_map/ppermute | solution.py:1421
  527.1 38.1 %collective-permute-start.17 = (bf16[2,256,1536]{2,1,0:T(8,128)(2,1)S(1)}, bf16[2,256,1536]{2,1,0:T(8,128)(2,1)S(1)}, u32[]{:S(2)}, u32[]{:S(2)}) collective-permute-start(bf16[2,256,1536]{2,1,0:T(8,128)(2,1)S(1)} %pad_maximum_fusion.1), channel_id=1, source_target_pairs={{1,4},{3,6},{4,1},{6,3},{9,12},{11,14},{12,9},{14,11},{17,20},{19,... | collective-permute-start | bytes 4718600 | tf_op jit(solution)/shard_map/ppermute | solution.py:1421
  532.3 9.9 %copy-start.10 = (bf16[8,256,1024]{2,1,0:T(8,128)(2,1)S(1)}, bf16[8,256,1024]{2,1,0:T(8,128)(2,1)}, u32[]{:S(2)}) copy-start(bf16[8,256,1024]{2,1,0:T(8,128)(2,1)} %get-tuple-element.138) | copy-start | bytes 12582916
  532.4 28.2 %collective-permute-start.18 = (bf16[256,1536]{1,0:T(8,128)(2,1)S(1)}, bf16[256,1536]{1,0:T(8,128)(2,1)S(1)}, u32[]{:S(2)}, u32[]{:S(2)}) collective-permute-start(bf16[256,1536]{1,0:T(8,128)(2,1)S(1)} %slice_bitcast_fusion.1), channel_id=1, source_target_pairs={{0,8},{1,9},{2,10},{3,11},{4,12},{5,13},{6,14},{7,15},{8,0},{9,1},... | collective-permute-start | bytes 2359304 | tf_op jit(solution)/shard_map/ppermute | solution.py:1421
  541.0 13.6 %collective-permute-start.20 = (bf16[128,2048]{1,0:T(8,128)(2,1)S(1)}, bf16[128,2048]{1,0:T(8,128)(2,1)S(1)}, u32[]{:S(2)}, u32[]{:S(2)}) collective-permute-start(bf16[128,2048]{1,0:T(8,128)(2,1)S(1)} %slice.210), channel_id=1, source_target_pairs={{0,2},{1,3},{2,0},{3,1},{4,6},{5,7},{6,4},{7,5},{8,10},{9,11},{10,... | collective-permute-start | bytes 1572872 | tf_op jit(solution)/shard_map/ppermute | solution.py:1421
  542.1 16.9 %collective-permute-start.19 = (bf16[128,2048]{1,0:T(8,128)(2,1)S(1)}, bf16[128,2048]{1,0:T(8,128)(2,1)S(1)}, u32[]{:S(2)}, u32[]{:S(2)}) collective-permute-start(bf16[128,2048]{1,0:T(8,128)(2,1)S(1)} %slice.211), channel_id=1, source_target_pairs={{0,4},{1,5},{2,6},{3,7},{4,0},{5,1},{6,2},{7,3},{8,12},{9,13},{10,... | collective-permute-start | bytes 1572872 | tf_op jit(solution)/shard_map/ppermute | solution.py:1421
  550.1 9.0 %copy-start.5 = (f32[256,2048]{1,0:T(8,128)S(1)}, f32[256,2048]{1,0:T(8,128)}, u32[]{:S(2)}) copy-start(f32[256,2048]{1,0:T(8,128)} %get-tuple-element.196.refs_0_) | copy-start | bytes 6291460
  565.4 112.7 %copy-start.29 = (f32[544]{0:T(1024)S(1)}, f32[544]{0:T(1024)}, u32[]{:S(2)}) copy-start(f32[544]{0:T(1024)} %param.33) | copy-start | bytes 6532
  565.4 112.7 %copy-start.32 = (f32[544]{0:T(1024)S(1)}, f32[544]{0:T(1024)}, u32[]{:S(2)}) copy-start(f32[544]{0:T(1024)} %param.35) | copy-start | bytes 6532
  565.4 112.7 %copy-start.33 = (f32[544]{0:T(1024)S(1)}, f32[544]{0:T(1024)}, u32[]{:S(2)}) copy-start(f32[544]{0:T(1024)} %param.34) | copy-start | bytes 6532
  565.4 113.3 %copy-start.3 = (f32[2,256,1536]{2,1,0:T(8,128)S(1)}, f32[2,256,1536]{2,1,0:T(8,128)}, u32[]{:S(2)}) copy-start(f32[2,256,1536]{2,1,0:T(8,128)} %wide_gate.1) | copy-start | bytes 9437188
  565.4 113.3 %copy-start.12 = (f32[2,256,1536]{2,1,0:T(8,128)S(1)}, f32[2,256,1536]{2,1,0:T(8,128)}, u32[]{:S(2)}) copy-start(f32[2,256,1536]{2,1,0:T(8,128)} %param.29) | copy-start | bytes 9437188
  669.2 30.3 %collective-permute-start.21 = (bf16[1024,2048]{1,0:T(8,128)(2,1)}, bf16[1024,2048]{1,0:T(8,128)(2,1)}, u32[]{:S(2)}, u32[]{:S(2)}) collective-permute-start(bf16[1024,2048]{1,0:T(8,128)(2,1)} %get-tuple-element.237), channel_id=1, source_target_pairs={{0,1},{1,0},{2,3},{3,2},{4,5},{5,4},{6,7},{7,6},{8,9},{9,8},{10,11... | collective-permute-start | bytes 12582920 | tf_op jit(solution)/shard_map/ppermute | solution.py:1421
  671.7 13.3 %collective-permute-start.22 = (bf16[256,1536]{1,0:T(8,128)(2,1)S(1)}, bf16[256,1536]{1,0:T(8,128)(2,1)S(1)}, u32[]{:S(2)}, u32[]{:S(2)}) collective-permute-start(bf16[256,1536]{1,0:T(8,128)(2,1)S(1)} %pad_maximum_fusion.4), channel_id=1, source_target_pairs={{1,4},{3,6},{4,1},{6,3},{9,12},{11,14},{12,9},{14,11},{17,20},{19,... | collective-permute-start | bytes 2359304 | tf_op jit(solution)/shard_map/ppermute | solution.py:1421
  673.6 21.5 %collective-permute-start.23 = (bf16[256,1536]{1,0:T(8,128)(2,1)}, bf16[256,1536]{1,0:T(8,128)(2,1)}, u32[]{:S(2)}, u32[]{:S(2)}) collective-permute-start(bf16[256,1536]{1,0:T(8,128)(2,1)} %fusion.15), channel_id=1, source_target_pairs={{1,4},{3,6},{4,1},{6,3},{9,12},{11,14},{12,9},{14,11},{17,20},{19,... | collective-permute-start | bytes 2359304 | tf_op jit(solution)/shard_map/ppermute | solution.py:1421
  678.7 6.3 copy-start.18
  684.9 4.2 copy-start.17
  686.3 5.5 copy-start.8
  695.1 4.4 copy-start.11
  (12 other events, 29.0 us)
where the time goes:
time: 711 us; the launch traced here: 707 us
  Pallas kernels  488 us (69%)
  matrix products  76.4 us (11%)
  other arithmetic  47.2 us (7%)
  starting transfers between devices  46.5 us (7%)
  waiting for transfers between devices  23.7 us (3%)
  local copies, waits for them, and re-layouts  22.6 us (3%)
    pallas_call x3, Pallas kernels, sum_rows(): pl.pallas_call(functools.partial(kernel, middle, jobs, len(extras), len(o...  326 us
    pallas_call x1, Pallas kernels, opening(): pl.pallas_call(functools.partial(opening_kernel, plan), out_shape=outputs...  84.2 us
    ppermute x24, starting transfers between devices, move(): return lax.ppermute(value, ('dp', 'tensor'), pairs)  46.5 us
    dot_general x6, matrix products, contract_rows(): lax.dot_general(left, right, (((0,), (0,)), ((), ())), preferred_element_...  38.8 us
    pallas_call x1, Pallas kernels, feed_forward(): pl.pallas_call(functools.partial(feed_kernel, plan), grid=(tiles,), out_s...  33.8 us
    dot_general x3, matrix products, contract_cols(): lax.dot_general(left, right, (((1,), (1,)), ((), ())), preferred_element_...  32.3 us
    ppermute x24, waiting for transfers between devices, move(): return lax.ppermute(value, ('dp', 'tensor'), pairs)  23.7 us
    pallas_call x1, Pallas kernels, attention_back(): pl.pallas_call(backward_kernel, out_shape=[jax.ShapeDtypeStruct((total, c...  22.8 us
  transfers between devices with their start and end apart: 24, of which 5 were waited for; matrix products, arithmetic and copies ran while one was open for 16% of the time, Pallas kernels for 38%

commit v1 on v0

--- a/solution.py
+++ b/solution.py
@@ -362,7 +362,7 @@
         self.size = rows // pieces
         self.outputs = [jax.ShapeDtypeStruct((2, rows, columns), parts.dtype)]
         self.scratch = [pltpu.VMEM((2, rows, columns), parts.dtype)] * 2
-        self.count, self.count_local = 3 * pieces, 0
+        self.count, self.count_local = 4 * pieces - 1, 0
         self.in_hbm = False
 
     def peers(self, zone, side, row, core):
@@ -383,8 +383,8 @@
         pieces = [pl.ds(piece * self.size, self.size) for piece in range(self.pieces)]
         self.steps = [(slot, rows) for slot in (0, 1) for rows in pieces]
         self.to_inner = [
-            copies.make(self.parts.at[2, rows], self.inward.at[1, rows], outer_peer)
-            for rows in pieces
+            copies.make(self.parts.at[3 - slot, rows], self.inward.at[slot, rows], outer_peer)
+            for slot, rows in self.steps[1:]
         ]
         self.across = [
             copies.make(self.inward.at[slot, rows], self.crossed.at[slot, rows], inner_peer)
@@ -398,10 +398,9 @@
 
         @pl.when(self.inner)
         def _():
-            for step in range(self.pieces):
-                slot, rows = self.steps[step]
-                self.add(self.inward, slot, rows, self.parts.at[2], self.ready)
-                self.across[step].start()
+            slot, rows = self.steps[0]
+            self.add(self.inward, slot, rows, self.parts.at[2], self.ready)
+            self.across[0].start()
 
     def add(self, target, slot, rows, left, right):
         def some(row, count):
@@ -412,15 +411,15 @@
         for_rows(self.size, some)
 
     def pump(self, steps):
-        steps = [step for step in steps if step < self.pieces]
+        steps = [step for step in steps if step < len(self.to_inner)]
 
         @pl.when(self.inner)
         def _():
             for step in steps:
-                slot, rows = self.steps[self.pieces + step]
+                slot, rows = self.steps[step + 1]
                 self.to_inner[step].wait_recv()
-                self.add(self.inward, slot, rows, self.parts.at[3], self.inward.at[1])
-                self.across[self.pieces + step].start()
+                self.add(self.inward, slot, rows, self.parts.at[2 + slot], self.inward.at[slot])
+                self.across[step + 1].start()
                 self.settle(step)
 
         @pl.when(self.outer)
@@ -438,8 +437,7 @@
     def finish(self):
         @pl.when(self.inner)
         def _():
-            for step in range(self.pieces, len(self.steps)):
-                self.settle(step)
+            self.settle(len(self.steps) - 1)
             for copy in self.across:
                 copy.wait_send()
 
@@ -512,6 +510,36 @@
         self.out[...] = total.astype(jnp.bfloat16)
         for copy in self.over + self.along:
             copy.wait_send()
+
+
+class TurnLate:
+    count, count_local, scratch, in_hbm = 1, 0, [], False
+
+    def __init__(self, values):
+        self.sources = [values]
+        self.outputs = [jax.ShapeDtypeStruct(values.shape, values.dtype)]
+
+    def peers(self, zone, side, row, core):
+        return {}
+
+    def start(self, copies, local_sems, sources, targets, stages):
+        zone, side, row, core = place_here()
+        self.away = side != core
+        self.copy = copies.make(sources[0], targets[0], device(zone, core, row, side))
+
+    def pump(self, steps):
+        pass
+
+    def late(self):
+        @pl.when(self.away)
+        def _():
+            self.copy.start()
+
+    def finish(self):
+        @pl.when(self.away)
+        def _():
+            self.copy.wait_recv()
+            self.copy.wait_send()
 
 
 class PairTree:
@@ -773,6 +801,13 @@
             spot += len(job.scratch)
 
     def pump(steps):
+        if 0 in steps:
+
+            @pl.when(away)
+            def _():
+                for copy in block_side:
+                    copy.start()
+
         for job in jobs:
             job.pump(steps)
 
@@ -815,13 +850,16 @@
 
     @pl.when(away)
     def _():
-        for copy in to_side + block_side:
+        for copy in to_side:
             copy.start()
         for copy in block_over:
             copy.wait_recv()
 
     for copy in to_row:
         copy.start()
+    for job in jobs:
+        if isinstance(job, TurnLate):
+            job.late()
     if gain_sum is not None:
         gain_sum.middle()
 
@@ -1709,26 +1747,17 @@
 
     down_got = plan.core_swap(down_far)
     gate_parts = zone_parts(contract_rows(normed_rows[:, :near_cols], grad_both), gate_got)
-    gate_parts, down_got, grad_both, active, out_grad = fence(
-        gate_parts, down_got, grad_both, active, out_grad
-    )
-
-    half_rows = shard_rows // 2
+    down_parts = zone_parts(contract_rows(out_grad[:, :near_cols], active), down_got)
+    gate_parts, down_parts, grad_both = fence(gate_parts, down_parts, grad_both)
+
     if tree:
-        gate_ready = [plan.inward(gate_parts[3, :half_rows])]
+        gate_ready = plan.inward(gate_parts[3, : shard_rows // 2])
     else:
-        gate_ready = [gate_parts[0]]
+        gate_ready = gate_parts[0]
     post_terms = contract_cols(grad_both, full_gate).astype(low)
-    post_terms, gate_parts, gate_ready, down_got, active, out_grad = fence(
-        post_terms, gate_parts, gate_ready, down_got, active, out_grad
-    )
-    if tree:
-        gate_ready += [plan.inward(gate_parts[3, half_rows:])]
-    down_parts = zone_parts(contract_rows(out_grad[:, :near_cols], active), down_got)
     post_terms, gate_parts, gate_ready, down_parts = fence(
         post_terms, gate_parts, gate_ready, down_parts
     )
-    gate_ready = jnp.concatenate(gate_ready, 0)
 
     if tree:
         down_sums = [plan.inward(down_parts[3]), plan.inward(down_parts[2])]
@@ -1783,14 +1812,14 @@
     else:
         total_down = zone_total(down_parts, down_sums)
     total_gate = zone_total(gate_own, gate_last)
-    summed_gate = plan.turn(jnp.stack([total_gate[:, :units], total_gate[:, units:]]))
+    total_gate = jnp.concatenate([total_gate[:, :units], total_gate[:, units:]], 0)
     out_far = contract_rows(branch_rows[:, near_cols:], attended).astype(low)
     out_got = plan.core_swap(out_far)
     normed_terms = contract_cols(mixed_rows, full_qkv).astype(low)
     out_parts = zone_parts(contract_rows(branch_rows[:, :near_cols], attended), out_got)
     block_own = (hidden + mlp_own + jnp.concatenate(mlp_last, 0).astype(jnp.float32)).astype(low)
-    out_parts, normed_terms, summed_gate, total_down, block_own, normed, grad_mixed = fence(
-        out_parts, normed_terms, summed_gate, total_down, block_own, normed, grad_mixed
+    out_parts, normed_terms, total_gate, total_down, block_own, normed, grad_mixed = fence(
+        out_parts, normed_terms, total_gate, total_down, block_own, normed, grad_mixed
     )
 
     gain_sum = GainSum(plan, gain_terms.shape[1], model_width) if plan.ordered else None
@@ -1802,21 +1831,27 @@
         [own_tokens, grad_hidden, gain_in, block_own] + ([gain_terms] if plan.ordered else []),
         [jax.ShapeDtypeStruct((1, model_width), jnp.float32)],
         2,
-        [BlockGrad(plan, normed, grad_mixed), ZoneBlocks(plan, out_parts, slots)],
+        [
+            BlockGrad(plan, normed, grad_mixed),
+            ZoneBlocks(plan, out_parts, slots),
+            TurnLate(total_gate),
+            TurnLate(total_down),
+        ],
         gain_sum,
     )
     if plan.ordered:
-        summed_gains, total_qkv, out_sent = rest
+        summed_gains, total_qkv, out_sent, got_gate, got_down = rest
     else:
-        total_qkv, out_sent = rest
+        total_qkv, out_sent, got_gate, got_down = rest
         summed_gains = plan.sum_everywhere(
             jnp.concatenate([plan.to_natural(input_gain_grad, 1), gain_terms], 1)
         )
-    mine, summed_gains, total_qkv, out_sent, total_down = fence(
-        mine, summed_gains, total_qkv, out_sent, total_down
-    )
-
-    summed_down = plan.turn(total_down)
+    mine, summed_gains, total_qkv, out_sent, got_gate, got_down = fence(
+        mine, summed_gains, total_qkv, out_sent, got_gate, got_down
+    )
+
+    summed_gate = plan.turned(total_gate, got_gate).reshape(gate_up.shape)
+    summed_down = plan.turned(total_down, got_down)
     other = plan.core_swap(mine)
     input_full, block_out = jnp.where(plan.home, mine, other), jnp.where(plan.home, other, mine)
     if not plan.ordered:

time: 711 us -> 702 us (0.987)
  starting transfers between devices: 46.5 us -> 55 us
    ppermute x24 -> x21, starting transfers between devices: 46.5 us -> 55 us  [move(): return lax.ppermute(value, ('dp', 'tensor'), pairs)]
    ppermute x24 -> x21, waiting for transfers between devices: 23.7 us -> 18.3 us  [move(): return lax.ppermute(value, ('dp', 'tensor'), pairs)]
  transfers between devices with their start and end apart: 24 -> 21, of which waited for: 5 -> 2; matrix products, arithmetic and copies ran while one was open for 16% -> 14% of each run, Pallas kernels for 38% -> 38%
where the time goes in v1:
time: 702 us; the launch traced here: 697 us
  Pallas kernels  484 us (69%)
  matrix products  70.7 us (10%)
  starting transfers between devices  55 us (8%)
  other arithmetic  46.3 us (7%)
  local copies, waits for them, and re-layouts  20.8 us (3%)
  waiting for transfers between devices  18.3 us (3%)
    pallas_call x3, Pallas kernels, sum_rows(): pl.pallas_call(functools.partial(kernel, middle, jobs, len(extras), len(o...  322 us
    pallas_call x1, Pallas kernels, opening(): pl.pallas_call(functools.partial(opening_kernel, plan), out_shape=outputs...  84.2 us
    ppermute x21, starting transfers between devices, move(): return lax.ppermute(value, ('dp', 'tensor'), pairs)  55 us
    dot_general x6, matrix products, contract_rows(): lax.dot_general(left, right, (((0,), (0,)), ((), ())), preferred_element_...  35 us
    pallas_call x1, Pallas kernels, feed_forward(): pl.pallas_call(functools.partial(feed_kernel, plan), grid=(tiles,), out_s...  33.8 us
    dot_general x3, matrix products, contract_cols(): lax.dot_general(left, right, (((1,), (1,)), ((), ())), preferred_element_...  30.5 us
    pallas_call x1, Pallas kernels, attention_back(): pl.pallas_call(backward_kernel, out_shape=[jax.ShapeDtypeStruct((total, c...  22.9 us
    pallas_call x1, Pallas kernels, attention(): pl.pallas_call(forward_kernel, out_shape=[shape(tokens.shape[1]), shape(c...  21.1 us
  transfers between devices with their start and end apart: 21, of which 2 were waited for; matrix products, arithmetic and copies ran while one was open for 14% of the time, Pallas kernels for 38%

profile of v1, /device:TPU:1, one launch (start us, length us, event | category | flops | bytes accessed | tf_op | source)
XLA Modules:
  0.0 697.1 jit_solution(17073377535682623011)
XLA Ops:
  0.7 2.6 reshape.95.wide_qkv
  5.8 84.2 %opening.1 = (bf16[8,256,1024]{2,1,0:T(8,128)(2,1)}, bf16[8,16,128]{2,1,0:T(8,128)(2,1)}, bf16[256,3072]{1,0:T(8,128)(2,1)}, bf16[256,512]{1,0:T(8,128)(2,1)}, b...) custom-call(f32[256,1024]{1,0:T(8,128)} %reshape.95.wide_qkv, ...), custom_call_target="tpu_custom_call" | custom-call | flops 1000000 | bytes 100000 | tf_op jit(solution)/shard_map/opening/pallas_call | solution.py:1109
  90.0 1.3 collective-permute-start
  92.7 2.2 collective-permute-start.3
  94.9 3.7 collective-permute-start.5
  100.5 2.6 fusion.24
  103.6 21.1 %attention.1 = (bf16[1024,2048]{1,0:T(8,128)(2,1)}, f32[1024,1024]{1,0:T(8,128)}, bf16[1024,512]{1,0:T(8,128)(2,1)S(1)}, bf16[1024,256]{1,0:T(8,128)(2,1)S(1)}, ...) custom-call(bf16[1024,2048]{1,0:T(8,128)(2,1)} %get-tuple-element.131.tokens, bf16[2048,1024]{1,0:T(8,128)(2,1)} %bitcast.69, ...), custom_call_target="tpu_custom_call" | custom-call | flops 1000000 | bytes 100000 | tf_op jit(solution)/shard_map/attention/pallas_call | solution.py:1264
  127.5 1.3 constant_dynamic-slice_fusion.10
  130.1 4.4 convolution_convert_fusion.2.terms
  134.4 136.8 %hidden_rows.1 = (bf16[1024,2048]{1,0:T(8,128)(2,1)}, f32[256,2048]{1,0:T(8,128)}, bf16[8,256,3072]{2,1,0:T(8,128)(2,1)}, bf16[8,256,1536]{2,1,0:T(8,128)(2,1)}) custom-call(bf16[1024,2048]{1,0:T(8,128)(2,1)} %convolution_convert_fusion.2.terms, bf16[256,2048]{1,0:T(8,128)(2,1)} %pad_maximum_fusion.1.refs_0_, f32[1,2048]{1,0:T(1,128)} %bitcast.75, ...), custom_call_target="tpu_custom_call" | custom-call | flops 1000000 | bytes 100000 | tf_op jit(solution)/shard_map/hidden_rows/pallas_call | solution.py:923
  271.3 33.8 %feed_forward.1 = (bf16[1024,1536]{1,0:T(8,128)(2,1)}, bf16[1024,3072]{1,0:T(8,128)(2,1)}, bf16[1024,2048]{1,0:T(8,128)(2,1)}) custom-call(bf16[1024,2048]{1,0:T(8,128)(2,1)} %get-tuple-element.173.rows, bf16[1024,2048]{1,0:T(8,128)(2,1)} %own_grad, bf16[1024,2048]{1,0:T(8,128)(2,1)} %collective-permute-done.5.got_grad, bf16[2048,3072]{1,0:T(8,128)(2,1)} %bitcast.78, ...), custom_call_target="tpu_custom_call" | custom-call | flops 19327352832 | bytes 40000000 | tf_op jit(solution)/shard_map/feed_forward/pallas_call | solution.py:1407
  305.1 10.2 %convolution_convert_fusion = bf16[1024,3072]{1,0:T(8,128)(2,1)S(1)} fusion(bf16[1024,3072]{1,0:T(8,128)(2,1)} %get-tuple-element.178, bf16[1024,2048]{1,0:T(8,128)(2,1)S(1)} %copy-done.38), kind=kOutput, calls=%fused_computation.2 | convolution fusion | flops 6445596672 | bytes 14680064 | tf_op jit(solution)/shard_map/dot_general | solution.py:55
  315.5 4.8 convolution_convert_fusion.3
  320.3 5.2 collective-permute-done.6
  325.6 10.1 %add_convert_fusion = bf16[1024,3072]{1,0:T(8,128)(2,1)S(1)} fusion(bf16[1024,3072]{1,0:T(8,128)(2,1)S(1)} %collective-permute-done.6, bf16[1024,3072]{1,0:T(8,128)(2,1)} %get-tuple-element.178, bf16[1024,2048]{1,0:T(8,128)(2,1)} %get-tuple-element.173.rows), kind=kOutput, calls=%fused_computation | convolution fusion | flops 6451888128 | bytes 20971520 | tf_op jit(solution)/shard_map/dot_general | solution.py:55
  335.8 6.3 add_convert_fusion.1
  342.2 1.3 collective-permute-start.8
  343.5 19.8 %convolution_convert_fusion.1.terms = bf16[1024,2048]{1,0:T(8,128)(2,1)} fusion(bf16[1024,3072]{1,0:T(8,128)(2,1)} %get-tuple-element.178, bf16[2048,3072]{1,0:T(8,128)(2,1)} %bitcast.80), kind=kOutput, calls=%fused_computation.8 | convolution fusion | flops 12886999040 | bytes 23068672 | tf_op jit(solution)/shard_map/dot_general | solution.py:61
  363.3 1.5 slice_bitcast_fusion.3
  364.8 2.2 collective-permute-start.9
  367.1 2.2 collective-permute-start.10
  371.7 86.6 %grad_hidden_rows.1 = (bf16[1024,2048]{1,0:T(8,128)(2,1)}, f32[256,2048]{1,0:T(8,128)}, f32[1,2048]{1,0:T(1,128)}, bf16[1024,2048]{1,0:T(8,128)(2,1)}, bf16[2,256,3072]{2,1,0:T(8,128)(2,1)}) custom-call(bf16[1024,2048]{1,0:T(8,128)(2,1)} %convolution_convert_fusion.1.terms, f32[256,2048]{1,0:T(8,128)} %get-tuple-element.182.refs_0_, ...), custom_call_target="tpu_custom_call" | custom-call | flops 1000000 | bytes 100000 | tf_op jit(solution)/shard_map/grad_hidden_rows/pallas_call | solution.py:923
  458.3 5.3 convolution_convert_fusion.5.grad_rows
  463.8 15.5 %collective-permute-start.11 = (bf16[256,3072]{1,0:T(8,128)(2,1)S(1)}, bf16[256,3072]{1,0:T(8,128)(2,1)}, u32[]{:S(2)}, u32[]{:S(2)}) collective-permute-start(bf16[256,3072]{1,0:T(8,128)(2,1)S(1)} %slice_bitcast_fusion), channel_id=1, source_target_pairs={{0,8},{1,9},{2,10},{3,11},{4,12},{5,13},{6,14},{7,15},{8,0},{9,1},... | collective-permute-start | bytes 4718600 | tf_op jit(solution)/shard_map/ppermute | solution.py:1459
  479.3 1.6 fusion.34
  481.7 4.0 collective-permute-start.13
  485.8 2.9 add_convert_fusion.3
  488.7 1.9 collective-permute-start.14
  490.5 22.9 %attention_back.1 = (bf16[1024,1024]{1,0:T(8,128)(2,1)}, bf16[1024,1024]{1,0:T(8,128)(2,1)}, f32[1,128]{1,0:T(1,128)S(1)}, f32[1,128]{1,0:T(1,128)S(1)}) custom-call(bf16[1024,512]{1,0:T(8,128)(2,1)S(1)} %get-tuple-element.135.query, bf16[1024,256]{1,0:T(8,128)(2,1)S(1)} %get-tuple-element.136.key, bf16[1024,256]{1,0:T(8,128)(2,1)S(1)} %get-tuple-element.137.value, ...), custom_call_target="tpu_custom_call" | custom-call | flops 1000000 | bytes 100000 | tf_op jit(solution)/shard_map/attention_back/pallas_call | solution.py:1335
  517.4 3.1 collective-permute-start.15
  520.5 6.3 convolution_convert_fusion.4.terms
  526.8 2.0 fusion.2
  528.9 2.3 slice_add_fusion.1
  532.0 1.8 add_convert_fusion.2
  534.0 9.1 %collective-permute-start.16 = (bf16[256,1536]{1,0:T(8,128)(2,1)S(1)}, bf16[256,1536]{1,0:T(8,128)(2,1)S(1)}, u32[]{:S(2)}, u32[]{:S(2)}) collective-permute-start(bf16[256,1536]{1,0:T(8,128)(2,1)S(1)} %slice_bitcast_fusion.1), channel_id=1, source_target_pairs={{0,8},{1,9},{2,10},{3,11},{4,12},{5,13},{6,14},{7,15},{8,0},{9,1},... | collective-permute-start | bytes 2359304 | tf_op jit(solution)/shard_map/ppermute | solution.py:1459
  544.4 1.5 fusion.4.refs_3_
  545.9 13.0 %collective-permute-done.16 = bf16[256,1536]{1,0:T(8,128)(2,1)S(1)} collective-permute-done((bf16[256,1536]{1,0:T(8,128)(2,1)S(1)}, bf16[256,1536]{1,0:T(8,128)(2,1)S(1)}, u32[]{:S(2)}, u32[]{:S(2)}) %collective-permute-start.16) | collective-permute-done | bytes 786464 | tf_op jit(solution)/shard_map/ppermute | solution.py:1459
  560.0 2.3 add_convert_fusion.4
  562.3 98.7 %grad_input_rows.1 = (bf16[1024,2048]{1,0:T(8,128)(2,1)}, f32[1,2048]{1,0:T(1,128)}, f32[1,4352]{1,0:T(1,128)}, bf16[256,1024]{1,0:T(8,128)(2,1)}, bf16[3,256,51...) custom-call(bf16[1024,2048]{1,0:T(8,128)(2,1)} %convolution_convert_fusion.4.terms, ...), custom_call_target="tpu_custom_call" | custom-call | flops 1000000 | bytes 100000 | tf_op jit(solution)/shard_map/grad_input_rows/pallas_call | solution.py:923
  662.3 1.3 fusion.23
  664.9 3.7 collective-permute-start.20
  670.1 1.6 broadcast_select_fusion.1
  671.8 5.0 multiply_subtract_fusion
  676.8 3.1 multiply_subtract_fusion.1
  681.2 2.8 reshape.107
  684.0 2.8 multiply_subtract_fusion.3
  686.8 3.2 multiply_subtract_fusion.2
  690.0 6.8 select_convert_fusion
  (174 shorter events, 26.5 us)
Async XLA Ops:
  90.0 34.8 %collective-permute-start = (bf16[256,512]{1,0:T(8,128)(2,1)}, bf16[256,512]{1,0:T(8,128)(2,1)S(1)}, u32[]{:S(2)}, u32[]{:S(2)}) collective-permute-start(bf16[256,512]{1,0:T(8,128)(2,1)} %get-tuple-element.145), channel_id=1, source_target_pairs={{0,8},{1,9},{2,10},{3,11},{4,12},{5,13},{6,14},{7,15},{8,0},{9,1},... | collective-permute-start | bytes 786440 | tf_op jit(solution)/shard_map/ppermute | solution.py:1459
  91.4 33.5 %collective-permute-start.1 = (bf16[256,512]{1,0:T(8,128)(2,1)}, bf16[256,512]{1,0:T(8,128)(2,1)}, u32[]{:S(2)}, u32[]{:S(2)}) collective-permute-start(bf16[256,512]{1,0:T(8,128)(2,1)} %get-tuple-element.145), channel_id=1, source_target_pairs={{0,24},{1,25},{2,26},{3,27},{4,28},{5,29},{6,30},{7,31},{8,16},{9,... | collective-permute-start | bytes 786440 | tf_op jit(solution)/shard_map/ppermute | solution.py:1459
  92.6 32.3 %collective-permute-start.2 = (bf16[256,512]{1,0:T(8,128)(2,1)}, bf16[256,512]{1,0:T(8,128)(2,1)}, u32[]{:S(2)}, u32[]{:S(2)}) collective-permute-start(bf16[256,512]{1,0:T(8,128)(2,1)} %get-tuple-element.145), channel_id=1, source_target_pairs={{0,16},{1,17},{2,18},{3,19},{4,20},{5,21},{6,22},{7,23},{8,24},{9,... | collective-permute-start | bytes 786440 | tf_op jit(solution)/shard_map/ppermute | solution.py:1459
  92.7 32.1 %collective-permute-start.3 = (bf16[256,1536]{1,0:T(8,128)(2,1)}, bf16[256,1536]{1,0:T(8,128)(2,1)}, u32[]{:S(2)}, u32[]{:S(2)}) collective-permute-start(bf16[256,1536]{1,0:T(8,128)(2,1)} %get-tuple-element.154.refs_4_), channel_id=1, source_target_pairs={{0,8},{1,9},{2,10},{3,11},{4,12},{5,13},{6,14},{7,15},{8,0},{9,1},... | collective-permute-start | bytes 2359304 | tf_op jit(solution)/shard_map/ppermute | solution.py:1459
  94.9 176.4 %collective-permute-start.5 = (bf16[1024,2048]{1,0:T(8,128)(2,1)}, bf16[1024,2048]{1,0:T(8,128)(2,1)}, u32[]{:S(2)}, u32[]{:S(2)}) collective-permute-start(bf16[1024,2048]{1,0:T(8,128)(2,1)} %own_grad), channel_id=1, source_target_pairs={{1,4},{3,6},{4,1},{6,3},{9,12},{11,14},{12,9},{14,11},{17,20},{19,... | collective-permute-start | bytes 12582920 | tf_op jit(solution)/shard_map/ppermute | solution.py:1459
  103.6 21.1 %copy-start = (f32[2048]{0:T(1024)}, f32[2048]{0:T(1024)S(1)}, u32[]{:S(2)}) copy-start(f32[2048]{0:T(1024)S(1)} %constant_dynamic-update-slice_fusion.26) | copy-start | bytes 24580
  103.6 21.3 %copy-start.30 = (bf16[256,512]{1,0:T(8,128)(2,1)S(1)}, bf16[256,512]{1,0:T(8,128)(2,1)}, u32[]{:S(2)}) copy-start(bf16[256,512]{1,0:T(8,128)(2,1)} %get-tuple-element.145) | copy-start | bytes 786436
  124.7 5.4 copy-start.1
  127.0 2.9 collective-permute-start.4
  271.3 33.8 %copy-start.38 = (bf16[1024,2048]{1,0:T(8,128)(2,1)S(1)}, bf16[1024,2048]{1,0:T(8,128)(2,1)}, u32[]{:S(2)}) copy-start(bf16[1024,2048]{1,0:T(8,128)(2,1)} %get-tuple-element.173.rows) | copy-start | bytes 12582916
  305.0 10.4 %copy-start.19 = (bf16[1024,1536]{1,0:T(8,128)(2,1)S(1)}, bf16[1024,1536]{1,0:T(8,128)(2,1)}, u32[]{:S(2)}) copy-start(bf16[1024,1536]{1,0:T(8,128)(2,1)} %get-tuple-element.176.refs_3_) | copy-start | bytes 9437188
  305.1 10.4 %copy-start.29 = (bf16[1024,2048]{1,0:T(8,128)(2,1)S(1)}, bf16[1024,2048]{1,0:T(8,128)(2,1)}, u32[]{:S(2)}) copy-start(bf16[1024,2048]{1,0:T(8,128)(2,1)} %get-tuple-element.169) | copy-start | bytes 12582916
  315.3 10.2 %collective-permute-start.6 = (bf16[1024,3072]{1,0:T(8,128)(2,1)S(1)}, bf16[1024,3072]{1,0:T(8,128)(2,1)S(1)}, u32[]{:S(2)}, u32[]{:S(2)}) collective-permute-start(bf16[1024,3072]{1,0:T(8,128)(2,1)S(1)} %convolution_convert_fusion), channel_id=1, source_target_pairs={{0,1},{1,0},{2,3},{3,2},{4,5},{5,4},{6,7},{7,6},{8,9},{9,8},{10,11... | collective-permute-start | bytes 18874376 | tf_op jit(solution)/shard_map/ppermute | solution.py:1459
  325.5 10.3 %collective-permute-start.7 = (bf16[1024,1536]{1,0:T(8,128)(2,1)}, bf16[1024,1536]{1,0:T(8,128)(2,1)}, u32[]{:S(2)}, u32[]{:S(2)}) collective-permute-start(bf16[1024,1536]{1,0:T(8,128)(2,1)} %convolution_convert_fusion.3), channel_id=1, source_target_pairs={{0,1},{1,0},{2,3},{3,2},{4,5},{5,4},{6,7},{7,6},{8,9},{9,8},{10,11... | collective-permute-start | bytes 9437192 | tf_op jit(solution)/shard_map/ppermute | solution.py:1459
  335.8 6.3 copy-start.6
  342.1 21.2 %copy-start.7 = (bf16[1024,1536]{1,0:T(8,128)(2,1)}, bf16[1024,1536]{1,0:T(8,128)(2,1)S(1)}, u32[]{:S(2)}) copy-start(bf16[1024,1536]{1,0:T(8,128)(2,1)S(1)} %add_convert_fusion.1) | copy-start | bytes 9437188
  342.2 21.1 %collective-permute-start.8 = (bf16[128,3072]{1,0:T(8,128)(2,1)S(1)}, bf16[128,3072]{1,0:T(8,128)(2,1)S(1)}, u32[]{:S(2)}, u32[]{:S(2)}) collective-permute-start(bf16[128,3072]{1,0:T(8,128)(2,1)S(1)} %slice_bitcast_fusion.5), channel_id=1, source_target_pairs={{0,8},{1,9},{2,10},{3,11},{4,12},{5,13},{6,14},{7,15},{24,16},{25,... | collective-permute-start | bytes 2359304 | tf_op jit(solution)/shard_map/ppermute | solution.py:1459
  364.8 93.5 %collective-permute-start.9 = (bf16[256,1536]{1,0:T(8,128)(2,1)}, bf16[256,1536]{1,0:T(8,128)(2,1)}, u32[]{:S(2)}, u32[]{:S(2)}) collective-permute-start(bf16[256,1536]{1,0:T(8,128)(2,1)} %get-tuple-element.257), channel_id=1, source_target_pairs={{0,8},{1,9},{2,10},{3,11},{4,12},{5,13},{6,14},{7,15},{24,16},{25,... | collective-permute-start | bytes 2359304 | tf_op jit(solution)/shard_map/ppermute | solution.py:1459
  367.1 91.2 %collective-permute-start.10 = (bf16[256,1536]{1,0:T(8,128)(2,1)}, bf16[256,1536]{1,0:T(8,128)(2,1)}, u32[]{:S(2)}, u32[]{:S(2)}) collective-permute-start(bf16[256,1536]{1,0:T(8,128)(2,1)} %get-tuple-element.256), channel_id=1, source_target_pairs={{0,8},{1,9},{2,10},{3,11},{4,12},{5,13},{6,14},{7,15},{24,16},{25,... | collective-permute-start | bytes 2359304 | tf_op jit(solution)/shard_map/ppermute | solution.py:1459
  458.3 5.3 copy-start.18
  458.3 21.0 %copy-start.11 = (bf16[1024,2048]{1,0:T(8,128)(2,1)S(1)}, bf16[1024,2048]{1,0:T(8,128)(2,1)}, u32[]{:S(2)}) copy-start(bf16[1024,2048]{1,0:T(8,128)(2,1)} %get-tuple-element.199) | copy-start | bytes 12582916
  463.7 22.1 %copy-start.8 = (bf16[1024,1536]{1,0:T(8,128)(2,1)S(1)}, bf16[1024,1536]{1,0:T(8,128)(2,1)}, u32[]{:S(2)}) copy-start(bf16[1024,1536]{1,0:T(8,128)(2,1)} %copy-done.7) | copy-start | bytes 9437188
  463.8 50.4 %collective-permute-start.11 = (bf16[256,3072]{1,0:T(8,128)(2,1)S(1)}, bf16[256,3072]{1,0:T(8,128)(2,1)}, u32[]{:S(2)}, u32[]{:S(2)}) collective-permute-start(bf16[256,3072]{1,0:T(8,128)(2,1)S(1)} %slice_bitcast_fusion), channel_id=1, source_target_pairs={{0,8},{1,9},{2,10},{3,11},{4,12},{5,13},{6,14},{7,15},{8,0},{9,1},... | collective-permute-start | bytes 4718600 | tf_op jit(solution)/shard_map/ppermute | solution.py:1459
  480.9 9.6 %copy-start.34 = (f32[1,2048]{1,0:T(1,128)S(1)}, f32[1,2048]{1,0:T(1,128)}, u32[]{:S(2)}) copy-start(f32[1,2048]{1,0:T(1,128)} %get-tuple-element.194) | copy-start | bytes 24580
  480.9 33.3 %collective-permute-start.12 = (bf16[256,2048]{1,0:T(8,128)(2,1)}, bf16[256,2048]{1,0:T(8,128)(2,1)}, u32[]{:S(2)}, u32[]{:S(2)}) collective-permute-start(bf16[256,2048]{1,0:T(8,128)(2,1)} %get-tuple-element.251), channel_id=1, source_target_pairs={{0,2},{1,3},{2,0},{3,1},{4,6},{5,7},{6,4},{7,5},{8,10},{9,11},{10,... | collective-permute-start | bytes 3145736 | tf_op jit(solution)/shard_map/ppermute | solution.py:1459
  481.7 32.5 %collective-permute-start.13 = (bf16[256,2048]{1,0:T(8,128)(2,1)}, bf16[256,2048]{1,0:T(8,128)(2,1)}, u32[]{:S(2)}, u32[]{:S(2)}) collective-permute-start(bf16[256,2048]{1,0:T(8,128)(2,1)} %get-tuple-element.250), channel_id=1, source_target_pairs={{0,4},{1,5},{2,6},{3,7},{4,0},{5,1},{6,2},{7,3},{8,12},{9,13},{10,... | collective-permute-start | bytes 3145736 | tf_op jit(solution)/shard_map/ppermute | solution.py:1459
  488.7 25.5 %collective-permute-start.14 = (bf16[2,256,1536]{2,1,0:T(8,128)(2,1)}, bf16[2,256,1536]{2,1,0:T(8,128)(2,1)}, u32[]{:S(2)}, u32[]{:S(2)}) collective-permute-start(bf16[2,256,1536]{2,1,0:T(8,128)(2,1)} %add_convert_fusion.3), channel_id=1, source_target_pairs={{8,16},{9,17},{10,18},{11,19},{12,20},{13,21},{14,22},{15,23},{16,... | collective-permute-start | bytes 4718600 | tf_op jit(solution)/shard_map/ppermute | solution.py:1459
  516.1 4.4 copy-start.39
  517.4 42.6 %collective-permute-start.15 = (bf16[1024,512]{1,0:T(8,128)(2,1)S(1)}, bf16[1024,512]{1,0:T(8,128)(2,1)S(1)}, u32[]{:S(2)}, u32[]{:S(2)}) collective-permute-start(bf16[1024,512]{1,0:T(8,128)(2,1)S(1)} %fusion.16), channel_id=1, source_target_pairs={{0,1},{1,0},{2,3},{3,2},{4,5},{5,4},{6,7},{7,6},{8,9},{9,8},{10,11... | collective-permute-start | bytes 3145736 | tf_op jit(solution)/shard_map/ppermute | solution.py:1459
  531.2 13.1 %collective-permute-start.18 = (bf16[128,2048]{1,0:T(8,128)(2,1)S(1)}, bf16[128,2048]{1,0:T(8,128)(2,1)S(1)}, u32[]{:S(2)}, u32[]{:S(2)}) collective-permute-start(bf16[128,2048]{1,0:T(8,128)(2,1)S(1)} %slice.203), channel_id=1, source_target_pairs={{0,2},{1,3},{2,0},{3,1},{4,6},{5,7},{6,4},{7,5},{8,10},{9,11},{10,... | collective-permute-start | bytes 1572872 | tf_op jit(solution)/shard_map/ppermute | solution.py:1459
  531.6 12.8 %collective-permute-start.17 = (bf16[128,2048]{1,0:T(8,128)(2,1)S(1)}, bf16[128,2048]{1,0:T(8,128)(2,1)S(1)}, u32[]{:S(2)}, u32[]{:S(2)}) collective-permute-start(bf16[128,2048]{1,0:T(8,128)(2,1)S(1)} %slice.204), channel_id=1, source_target_pairs={{0,4},{1,5},{2,6},{3,7},{4,0},{5,1},{6,2},{7,3},{8,12},{9,13},{10,... | collective-permute-start | bytes 1572872 | tf_op jit(solution)/shard_map/ppermute | solution.py:1459
  533.9 10.4 %copy-start.5 = (f32[256,2048]{1,0:T(8,128)S(1)}, f32[256,2048]{1,0:T(8,128)}, u32[]{:S(2)}) copy-start(f32[256,2048]{1,0:T(8,128)} %get-tuple-element.182.refs_0_) | copy-start | bytes 6291460
  534.0 24.9 %collective-permute-start.16 = (bf16[256,1536]{1,0:T(8,128)(2,1)S(1)}, bf16[256,1536]{1,0:T(8,128)(2,1)S(1)}, u32[]{:S(2)}, u32[]{:S(2)}) collective-permute-start(bf16[256,1536]{1,0:T(8,128)(2,1)S(1)} %slice_bitcast_fusion.1), channel_id=1, source_target_pairs={{0,8},{1,9},{2,10},{3,11},{4,12},{5,13},{6,14},{7,15},{8,0},{9,1},... | collective-permute-start | bytes 2359304 | tf_op jit(solution)/shard_map/ppermute | solution.py:1459
  562.3 107.2 %copy-start.32 = (f32[544]{0:T(1024)S(1)}, f32[544]{0:T(1024)}, u32[]{:S(2)}) copy-start(f32[544]{0:T(1024)} %param.33) | copy-start | bytes 6532
  562.3 107.2 %copy-start.35 = (f32[544]{0:T(1024)S(1)}, f32[544]{0:T(1024)}, u32[]{:S(2)}) copy-start(f32[544]{0:T(1024)} %param.35) | copy-start | bytes 6532
  562.3 107.2 %copy-start.36 = (f32[544]{0:T(1024)S(1)}, f32[544]{0:T(1024)}, u32[]{:S(2)}) copy-start(f32[544]{0:T(1024)} %param.34) | copy-start | bytes 6532
  562.3 109.4 %copy-start.16 = (f32[2,256,1536]{2,1,0:T(8,128)S(1)}, f32[2,256,1536]{2,1,0:T(8,128)}, u32[]{:S(2)}) copy-start(f32[2,256,1536]{2,1,0:T(8,128)} %param.29) | copy-start | bytes 9437188
  562.3 109.4 %copy-start.17 = (f32[2,256,1536]{2,1,0:T(8,128)S(1)}, f32[2,256,1536]{2,1,0:T(8,128)}, u32[]{:S(2)}) copy-start(f32[2,256,1536]{2,1,0:T(8,128)} %param.28) | copy-start | bytes 9437188
  661.1 9.0 %copy-start.3 = (bf16[512,1536]{1,0:T(8,128)(2,1)S(1)}, bf16[512,1536]{1,0:T(8,128)(2,1)}, u32[]{:S(2)}) copy-start(bf16[512,1536]{1,0:T(8,128)(2,1)} %pad_maximum_fusion.refs_8_) | copy-start | bytes 4718596
  661.1 28.9 %collective-permute-start.19 = (bf16[1024,2048]{1,0:T(8,128)(2,1)}, bf16[1024,2048]{1,0:T(8,128)(2,1)}, u32[]{:S(2)}, u32[]{:S(2)}) collective-permute-start(bf16[1024,2048]{1,0:T(8,128)(2,1)} %get-tuple-element.225), channel_id=1, source_target_pairs={{0,1},{1,0},{2,3},{3,2},{4,5},{5,4},{6,7},{7,6},{8,9},{9,8},{10,11... | collective-permute-start | bytes 12582920 | tf_op jit(solution)/shard_map/ppermute | solution.py:1459
  663.7 8.1 %copy-start.4 = (f32[2,256,1536]{2,1,0:T(8,128)S(1)}, f32[2,256,1536]{2,1,0:T(8,128)}, u32[]{:S(2)}) copy-start(f32[2,256,1536]{2,1,0:T(8,128)} %wide_gate.1) | copy-start | bytes 9437188
  664.9 15.0 %collective-permute-start.20 = (bf16[256,1536]{1,0:T(8,128)(2,1)S(1)}, bf16[256,1536]{1,0:T(8,128)(2,1)S(1)}, u32[]{:S(2)}, u32[]{:S(2)}) collective-permute-start(bf16[256,1536]{1,0:T(8,128)(2,1)S(1)} %pad_maximum_fusion.3), channel_id=1, source_target_pairs={{1,4},{3,6},{4,1},{6,3},{9,12},{11,14},{12,9},{14,11},{17,20},{19,... | collective-permute-start | bytes 2359304 | tf_op jit(solution)/shard_map/ppermute | solution.py:1459
  671.7 5.1 copy-start.9
  671.7 5.0 copy-start.10
  671.8 5.0 copy-start.22
  671.8 5.0 copy-start.23
  671.8 5.0 copy-start.27
  681.2 5.5 copy-start.12
  (13 other events, 35.9 us)

commit v2 on v1

--- a/solution.py
+++ b/solution.py
@@ -356,13 +356,13 @@
 
 
 class PairScatter:
-    def __init__(self, parts, ready, pieces):
-        self.sources, self.pieces = [parts, ready], pieces
+    def __init__(self, parts, pieces):
+        self.sources, self.pieces = [parts], pieces
         _, rows, columns = parts.shape
         self.size = rows // pieces
         self.outputs = [jax.ShapeDtypeStruct((2, rows, columns), parts.dtype)]
         self.scratch = [pltpu.VMEM((2, rows, columns), parts.dtype)] * 2
-        self.count, self.count_local = 4 * pieces - 1, 0
+        self.count, self.count_local = 4 * pieces, 0
         self.in_hbm = False
 
     def peers(self, zone, side, row, core):
@@ -373,18 +373,20 @@
 
     def start(self, copies, local_sems, sources, targets, stages):
         zone, side, row, core = place_here()
-        self.parts, self.ready = sources
-        self.out = targets[0]
+        self.parts, self.out = sources[0], targets[0]
         self.inward, self.crossed = stages
         inner_peer = device(flipped(zone, 3), side, row, core)
         outer_peer = device(flipped(zone, 1), side, row, core)
         self.inner = inner_zone(zone) == 1
         self.outer = inner_zone(zone) == 0
-        pieces = [pl.ds(piece * self.size, self.size) for piece in range(self.pieces)]
-        self.steps = [(slot, rows) for slot in (0, 1) for rows in pieces]
+        self.steps = [
+            (slot, pl.ds(piece * self.size, self.size))
+            for piece in range(self.pieces)
+            for slot in (0, 1)
+        ]
         self.to_inner = [
             copies.make(self.parts.at[3 - slot, rows], self.inward.at[slot, rows], outer_peer)
-            for slot, rows in self.steps[1:]
+            for slot, rows in self.steps
         ]
         self.across = [
             copies.make(self.inward.at[slot, rows], self.crossed.at[slot, rows], inner_peer)
@@ -396,12 +398,6 @@
             for copy in self.to_inner[:AHEAD]:
                 copy.start()
 
-        @pl.when(self.inner)
-        def _():
-            slot, rows = self.steps[0]
-            self.add(self.inward, slot, rows, self.parts.at[2], self.ready)
-            self.across[0].start()
-
     def add(self, target, slot, rows, left, right):
         def some(row, count):
             here = pl.ds(rows.start + row, count)
@@ -411,16 +407,17 @@
         for_rows(self.size, some)
 
     def pump(self, steps):
-        steps = [step for step in steps if step < len(self.to_inner)]
+        steps = [step for step in steps if step < len(self.steps)]
 
         @pl.when(self.inner)
         def _():
             for step in steps:
-                slot, rows = self.steps[step + 1]
+                slot, rows = self.steps[step]
                 self.to_inner[step].wait_recv()
                 self.add(self.inward, slot, rows, self.parts.at[2 + slot], self.inward.at[slot])
-                self.across[step + 1].start()
-                self.settle(step)
+                self.across[step].start()
+                if step >= AHEAD:
+                    self.settle(step - AHEAD)
 
         @pl.when(self.outer)
         def _():
@@ -437,7 +434,8 @@
     def finish(self):
         @pl.when(self.inner)
         def _():
-            self.settle(len(self.steps) - 1)
+            for step in range(len(self.steps) - AHEAD, len(self.steps)):
+                self.settle(step)
             for copy in self.across:
                 copy.wait_send()
 
@@ -1734,35 +1732,35 @@
     )
     if not plan.ordered:
         out_grad = plan.to_local(out_grad, 1)
+    down_far = contract_rows(out_grad[:, near_cols:], active).astype(low)
+    down_far, active, grad_both, out_grad, normed_rows = fence(
+        down_far, active, grad_both, out_grad, normed_rows
+    )
+
+    down_got = plan.core_swap(down_far)
     gate_far = contract_rows(normed_rows[:, near_cols:], grad_both).astype(low)
-    gate_far, active, grad_both, out_grad, normed_rows = fence(
-        gate_far, active, grad_both, out_grad, normed_rows
+    down_parts = zone_parts(contract_rows(out_grad[:, :near_cols], active), down_got)
+    gate_far, down_parts, grad_both, normed_rows = fence(
+        gate_far, down_parts, grad_both, normed_rows
     )
 
     gate_got = plan.core_swap(gate_far)
-    down_far = contract_rows(out_grad[:, near_cols:], active).astype(low)
-    gate_got, down_far, active, grad_both, normed_rows = fence(
-        gate_got, down_far, active, grad_both, normed_rows
-    )
-
-    down_got = plan.core_swap(down_far)
-    gate_parts = zone_parts(contract_rows(normed_rows[:, :near_cols], grad_both), gate_got)
-    down_parts = zone_parts(contract_rows(out_grad[:, :near_cols], active), down_got)
-    gate_parts, down_parts, grad_both = fence(gate_parts, down_parts, grad_both)
-
     if tree:
-        gate_ready = plan.inward(gate_parts[3, : shard_rows // 2])
-    else:
-        gate_ready = gate_parts[0]
-    post_terms = contract_cols(grad_both, full_gate).astype(low)
-    post_terms, gate_parts, gate_ready, down_parts = fence(
-        post_terms, gate_parts, gate_ready, down_parts
-    )
-
-    if tree:
-        down_sums = [plan.inward(down_parts[3]), plan.inward(down_parts[2])]
+        down_sums = [plan.inward(down_parts[3])]
     else:
         down_sums = plan.to_zones(down_parts, slots)
+    post_terms = contract_cols(grad_both, full_gate).astype(low)
+    post_terms, gate_got, down_parts, down_sums, grad_both, normed_rows = fence(
+        post_terms, gate_got, down_parts, down_sums, grad_both, normed_rows
+    )
+
+    if tree:
+        down_sums += [plan.inward(down_parts[2])]
+    gate_parts = zone_parts(contract_rows(normed_rows[:, :near_cols], grad_both), gate_got)
+    post_terms, gate_parts, down_parts, down_sums = fence(
+        post_terms, gate_parts, down_parts, down_sums
+    )
+
     eighth = tok_rows // 8
     own_grad = jnp.concatenate([out_grad[:eighth], out_grad[2 * eighth : 3 * eighth]], 0)
     branch_rows, grad_hidden, post_gain_grad, mlp_terms, gate_sums = sum_rows(
@@ -1778,7 +1776,7 @@
         1,
         [
             SideDot(active, full_down),
-            PairScatter(gate_parts, gate_ready, 2) if tree else ZoneBlocks(plan, gate_parts, slots),
+            PairScatter(gate_parts, 2) if tree else ZoneBlocks(plan, gate_parts, slots),
         ],
     )
     branch_rows, grad_hidden, post_gain_grad, gate_sums, mlp_terms, down_parts, down_sums = fence(
@@ -1812,7 +1810,7 @@
     else:
         total_down = zone_total(down_parts, down_sums)
     total_gate = zone_total(gate_own, gate_last)
-    total_gate = jnp.concatenate([total_gate[:, :units], total_gate[:, units:]], 0)
+    total_gate = jnp.stack([total_gate[:, :units], total_gate[:, units:]])
     out_far = contract_rows(branch_rows[:, near_cols:], attended).astype(low)
     out_got = plan.core_swap(out_far)
     normed_terms = contract_cols(mixed_rows, full_qkv).astype(low)
@@ -1834,23 +1832,22 @@
         [
             BlockGrad(plan, normed, grad_mixed),
             ZoneBlocks(plan, out_parts, slots),
-            TurnLate(total_gate),
             TurnLate(total_down),
         ],
         gain_sum,
     )
     if plan.ordered:
-        summed_gains, total_qkv, out_sent, got_gate, got_down = rest
+        summed_gains, total_qkv, out_sent, got_down = rest
     else:
-        total_qkv, out_sent, got_gate, got_down = rest
+        total_qkv, out_sent, got_down = rest
         summed_gains = plan.sum_everywhere(
             jnp.concatenate([plan.to_natural(input_gain_grad, 1), gain_terms], 1)
         )
-    mine, summed_gains, total_qkv, out_sent, got_gate, got_down = fence(
-        mine, summed_gains, total_qkv, out_sent, got_gate, got_down
-    )
-
-    summed_gate = plan.turned(total_gate, got_gate).reshape(gate_up.shape)
+    mine, summed_gains, total_qkv, out_sent, total_gate, got_down = fence(
+        mine, summed_gains, total_qkv, out_sent, total_gate, got_down
+    )
+
+    summed_gate = plan.turn(total_gate)
     summed_down = plan.turned(total_down, got_down)
     other = plan.core_swap(mine)
     input_full, block_out = jnp.where(plan.home, mine, other), jnp.where(plan.home, other, mine)

time: 702 us -> 702 us (level)
  transfers between devices with their start and end apart: 21 -> 21, of which waited for: 2 -> 4; matrix products, arithmetic and copies ran while one was open for 14% -> 14% of each run, Pallas kernels for 38% -> 26%
where the time goes in v2:
time: 702 us; the launch traced here: 698 us
  Pallas kernels  487 us (69%)
  matrix products  71.5 us (10%)
  starting transfers between devices  58.5 us (8%)
  other arithmetic  46.2 us (7%)
  local copies, waits for them, and re-layouts  18.7 us (3%)
  waiting for transfers between devices  13.8 us (2%)
    pallas_call x3, Pallas kernels, sum_rows(): pl.pallas_call(functools.partial(kernel, middle, jobs, len(extras), len(o...  324 us
    pallas_call x1, Pallas kernels, opening(): pl.pallas_call(functools.partial(opening_kernel, plan), out_shape=outputs...  84.2 us
    ppermute x21, starting transfers between devices, move(): return lax.ppermute(value, ('dp', 'tensor'), pairs)  58.5 us
    dot_general x6, matrix products, contract_rows(): lax.dot_general(left, right, (((0,), (0,)), ((), ())), preferred_element_...  36 us
    pallas_call x1, Pallas kernels, feed_forward(): pl.pallas_call(functools.partial(feed_kernel, plan), grid=(tiles,), out_s...  33.9 us
    dot_general x3, matrix products, contract_cols(): lax.dot_general(left, right, (((1,), (1,)), ((), ())), preferred_element_...  30.2 us
    pallas_call x1, Pallas kernels, attention_back(): pl.pallas_call(backward_kernel, out_shape=[jax.ShapeDtypeStruct((total, c...  23.2 us
    pallas_call x1, Pallas kernels, attention(): pl.pallas_call(forward_kernel, out_shape=[shape(tokens.shape[1]), shape(c...  21.4 us
  transfers between devices with their start and end apart: 21, of which 4 were waited for; matrix products, arithmetic and copies ran while one was open for 14% of the time, Pallas kernels for 26%

profile of v2, /device:TPU:1, one launch (start us, length us, event | category | flops | bytes accessed | tf_op | source)
XLA Modules:
  0.0 697.7 jit_solution(11118048535471518664)
XLA Ops:
  3.2 2.6 reshape.92.wide_qkv
  5.8 84.2 %opening.1 = (bf16[8,256,1024]{2,1,0:T(8,128)(2,1)}, bf16[8,16,128]{2,1,0:T(8,128)(2,1)}, bf16[256,3072]{1,0:T(8,128)(2,1)}, bf16[256,512]{1,0:T(8,128)(2,1)}, b...) custom-call(f32[256,1024]{1,0:T(8,128)} %reshape.92.wide_qkv, ...), custom_call_target="tpu_custom_call" | custom-call | flops 1000000 | bytes 100000 | tf_op jit(solution)/shard_map/opening/pallas_call | solution.py:1107
  91.4 2.1 collective-permute-start.1
  93.4 1.5 collective-permute-start.3
  94.9 3.7 collective-permute-start.5
  100.5 2.6 fusion.27
  103.6 21.4 %attention.1 = (bf16[1024,2048]{1,0:T(8,128)(2,1)}, f32[1024,1024]{1,0:T(8,128)}, bf16[1024,512]{1,0:T(8,128)(2,1)S(1)}, bf16[1024,256]{1,0:T(8,128)(2,1)S(1)}, ...) custom-call(bf16[1024,2048]{1,0:T(8,128)(2,1)} %get-tuple-element.133.tokens, bf16[2048,1024]{1,0:T(8,128)(2,1)} %bitcast.68, ...), custom_call_target="tpu_custom_call" | custom-call | flops 1000000 | bytes 100000 | tf_op jit(solution)/shard_map/attention/pallas_call | solution.py:1262
  130.5 4.4 convolution_convert_fusion.2.terms
  134.8 136.4 %hidden_rows.1 = (bf16[1024,2048]{1,0:T(8,128)(2,1)}, f32[256,2048]{1,0:T(8,128)}, bf16[8,256,3072]{2,1,0:T(8,128)(2,1)}, bf16[8,256,1536]{2,1,0:T(8,128)(2,1)}) custom-call(bf16[1024,2048]{1,0:T(8,128)(2,1)} %convolution_convert_fusion.2.terms, bf16[256,2048]{1,0:T(8,128)(2,1)} %pad_maximum_fusion.1.refs_0_, f32[1,2048]{1,0:T(1,128)} %bitcast.76, ...), custom_call_target="tpu_custom_call" | custom-call | flops 1000000 | bytes 100000 | tf_op jit(solution)/shard_map/hidden_rows/pallas_call | solution.py:921
  271.2 33.9 %feed_forward.1 = (bf16[1024,1536]{1,0:T(8,128)(2,1)}, bf16[1024,3072]{1,0:T(8,128)(2,1)}, bf16[1024,2048]{1,0:T(8,128)(2,1)}) custom-call(bf16[1024,2048]{1,0:T(8,128)(2,1)} %get-tuple-element.180.rows, bf16[1024,2048]{1,0:T(8,128)(2,1)} %own_grad, bf16[1024,2048]{1,0:T(8,128)(2,1)} %collective-permute-done.5.got_grad, bf16[2048,3072]{1,0:T(8,128)(2,1)} %bitcast.79, ...), custom_call_target="tpu_custom_call" | custom-call | flops 19327352832 | bytes 40000000 | tf_op jit(solution)/shard_map/feed_forward/pallas_call | solution.py:1405
  305.1 6.1 convolution_convert_fusion.3
  311.6 8.9 %convolution_convert_fusion = bf16[1024,3072]{1,0:T(8,128)(2,1)} fusion(bf16[1024,3072]{1,0:T(8,128)(2,1)S(1)} %copy-done.38, bf16[1024,2048]{1,0:T(8,128)(2,1)S(1)} %copy-done.35), kind=kOutput, calls=%fused_computation.2 | convolution fusion | flops 6445596672 | bytes 14680064 | tf_op jit(solution)/shard_map/dot_general | solution.py:55
  320.5 4.9 add_convert_fusion.1
  328.4 1.6 collective-permute-start.8
  330.0 19.6 %convolution_convert_fusion.1.terms = bf16[1024,2048]{1,0:T(8,128)(2,1)} fusion(bf16[1024,3072]{1,0:T(8,128)(2,1)} %get-tuple-element.181, bf16[2048,3072]{1,0:T(8,128)(2,1)} %bitcast.81), kind=kOutput, calls=%fused_computation.7 | convolution fusion | flops 12886999040 | bytes 23068672 | tf_op jit(solution)/shard_map/dot_general | solution.py:61
  349.6 1.6 collective-permute-start.9
  351.2 12.5 %add_convert_fusion = bf16[1024,3072]{1,0:T(8,128)(2,1)} fusion(bf16[1024,3072]{1,0:T(8,128)(2,1)} %collective-permute-done.7, bf16[1024,3072]{1,0:T(8,128)(2,1)} %get-tuple-element.181, bf16[1024,2048]{1,0:T(8,128)(2,1)S(1)} %copy-done.36), kind=kOutput, calls=%fused_computation | convolution fusion | flops 6451888128 | bytes 20971520 | tf_op jit(solution)/shard_map/dot_general | solution.py:55
  363.7 3.7 collective-permute-done.9
  367.4 87.7 %grad_hidden_rows.1 = (bf16[1024,2048]{1,0:T(8,128)(2,1)}, f32[256,2048]{1,0:T(8,128)}, f32[1,2048]{1,0:T(1,128)}, bf16[1024,2048]{1,0:T(8,128)(2,1)}, bf16[2,256,3072]{2,1,0:T(8,128)(2,1)}) custom-call(bf16[1024,2048]{1,0:T(8,128)(2,1)} %convolution_convert_fusion.1.terms, f32[256,2048]{1,0:T(8,128)} %get-tuple-element.186.refs_0_, ...), custom_call_target="tpu_custom_call" | custom-call | flops 1000000 | bytes 100000 | tf_op jit(solution)/shard_map/grad_hidden_rows/pallas_call | solution.py:921
  455.1 5.3 convolution_convert_fusion.5.grad_rows
  461.7 20.3 %collective-permute-start.10 = (bf16[256,3072]{1,0:T(8,128)(2,1)}, bf16[256,3072]{1,0:T(8,128)(2,1)}, u32[]{:S(2)}, u32[]{:S(2)}) collective-permute-start(bf16[256,3072]{1,0:T(8,128)(2,1)} %slice_bitcast_fusion), channel_id=1, source_target_pairs={{0,8},{1,9},{2,10},{3,11},{4,12},{5,13},{6,14},{7,15},{8,0},{9,1},... | collective-permute-start | bytes 4718600 | tf_op jit(solution)/shard_map/ppermute | solution.py:1457
  482.0 1.5 add_convert_fusion.3
  483.5 2.0 collective-permute-start.13
  485.5 1.6 fusion.37
  487.1 2.3 collective-permute-start.12
  490.1 23.2 %attention_back.1 = (bf16[1024,1024]{1,0:T(8,128)(2,1)}, bf16[1024,1024]{1,0:T(8,128)(2,1)}, f32[1,128]{1,0:T(1,128)S(1)}, f32[1,128]{1,0:T(1,128)S(1)}) custom-call(bf16[1024,512]{1,0:T(8,128)(2,1)S(1)} %get-tuple-element.137.query, bf16[1024,256]{1,0:T(8,128)(2,1)S(1)} %get-tuple-element.138.key, bf16[1024,256]{1,0:T(8,128)(2,1)S(1)} %get-tuple-element.139.value, ...), custom_call_target="tpu_custom_call" | custom-call | flops 1000000 | bytes 100000 | tf_op jit(solution)/shard_map/attention_back/pallas_call | solution.py:1333
  514.0 2.1 slice_add_fusion.1
  516.5 1.9 add_convert_fusion.2
  518.6 4.9 collective-permute-start.15
  523.5 6.2 convolution_convert_fusion.4.terms
  529.8 2.1 fusion.2
  532.1 4.1 collective-permute-start.16
  537.5 4.2 collective-permute-start.14
  541.9 2.8 collective-permute-done.16
  544.7 1.5 fusion.4.refs_3_
  547.3 2.3 add_convert_fusion.4
  549.5 100.4 %grad_input_rows.1 = (bf16[1024,2048]{1,0:T(8,128)(2,1)}, f32[1,2048]{1,0:T(1,128)}, f32[1,4352]{1,0:T(1,128)}, bf16[256,1024]{1,0:T(8,128)(2,1)}, bf16[3,256,51...) custom-call(bf16[1024,2048]{1,0:T(8,128)(2,1)} %convolution_convert_fusion.4.terms, ...), custom_call_target="tpu_custom_call" | custom-call | flops 1000000 | bytes 100000 | tf_op jit(solution)/shard_map/grad_input_rows/pallas_call | solution.py:921
  649.9 1.8 collective-permute-start.18
  654.1 3.1 collective-permute-start.19
  657.2 2.7 collective-permute-start.20
  660.8 4.3 multiply_subtract_fusion.1
  665.7 1.8 collective-permute-done.19
  668.7 2.7 reshape.104
  671.4 2.9 multiply_subtract_fusion.3
  674.4 4.6 multiply_subtract_fusion.2
  678.9 5.5 collective-permute-done.20
  684.4 6.2 multiply_subtract_fusion
  690.6 6.9 select_convert_fusion
  (171 shorter events, 25.4 us)
Async XLA Ops:
  90.0 35.2 %collective-permute-start.2 = (bf16[256,512]{1,0:T(8,128)(2,1)}, bf16[256,512]{1,0:T(8,128)(2,1)S(1)}, u32[]{:S(2)}, u32[]{:S(2)}) collective-permute-start(bf16[256,512]{1,0:T(8,128)(2,1)} %get-tuple-element.147), channel_id=1, source_target_pairs={{0,16},{1,17},{2,18},{3,19},{4,20},{5,21},{6,22},{7,23},{8,24},{9,... | collective-permute-start | bytes 786440 | tf_op jit(solution)/shard_map/ppermute | solution.py:1457
  91.4 33.8 %collective-permute-start.1 = (bf16[256,512]{1,0:T(8,128)(2,1)}, bf16[256,512]{1,0:T(8,128)(2,1)}, u32[]{:S(2)}, u32[]{:S(2)}) collective-permute-start(bf16[256,512]{1,0:T(8,128)(2,1)} %get-tuple-element.147), channel_id=1, source_target_pairs={{0,24},{1,25},{2,26},{3,27},{4,28},{5,29},{6,30},{7,31},{8,16},{9,... | collective-permute-start | bytes 786440 | tf_op jit(solution)/shard_map/ppermute | solution.py:1457
  93.4 31.8 %collective-permute-start = (bf16[256,512]{1,0:T(8,128)(2,1)}, bf16[256,512]{1,0:T(8,128)(2,1)}, u32[]{:S(2)}, u32[]{:S(2)}) collective-permute-start(bf16[256,512]{1,0:T(8,128)(2,1)} %get-tuple-element.147), channel_id=1, source_target_pairs={{0,8},{1,9},{2,10},{3,11},{4,12},{5,13},{6,14},{7,15},{8,0},{9,1},... | collective-permute-start | bytes 786440 | tf_op jit(solution)/shard_map/ppermute | solution.py:1457
  93.4 31.8 %collective-permute-start.3 = (bf16[256,1536]{1,0:T(8,128)(2,1)}, bf16[256,1536]{1,0:T(8,128)(2,1)}, u32[]{:S(2)}, u32[]{:S(2)}) collective-permute-start(bf16[256,1536]{1,0:T(8,128)(2,1)} %get-tuple-element.156.refs_4_), channel_id=1, source_target_pairs={{0,8},{1,9},{2,10},{3,11},{4,12},{5,13},{6,14},{7,15},{8,0},{9,1},... | collective-permute-start | bytes 2359304 | tf_op jit(solution)/shard_map/ppermute | solution.py:1457
  94.9 176.3 %collective-permute-start.5 = (bf16[1024,2048]{1,0:T(8,128)(2,1)}, bf16[1024,2048]{1,0:T(8,128)(2,1)}, u32[]{:S(2)}, u32[]{:S(2)}) collective-permute-start(bf16[1024,2048]{1,0:T(8,128)(2,1)} %own_grad), channel_id=1, source_target_pairs={{1,4},{3,6},{4,1},{6,3},{9,12},{11,14},{12,9},{14,11},{17,20},{19,... | collective-permute-start | bytes 12582920 | tf_op jit(solution)/shard_map/ppermute | solution.py:1457
  103.6 21.4 %copy-start = (f32[2048]{0:T(1024)}, f32[2048]{0:T(1024)S(1)}, u32[]{:S(2)}) copy-start(f32[2048]{0:T(1024)S(1)} %constant_dynamic-update-slice_fusion.26) | copy-start | bytes 24580
  103.6 21.6 %copy-start.27 = (bf16[256,512]{1,0:T(8,128)(2,1)S(1)}, bf16[256,512]{1,0:T(8,128)(2,1)}, u32[]{:S(2)}) copy-start(bf16[256,512]{1,0:T(8,128)(2,1)} %get-tuple-element.147) | copy-start | bytes 786436
  127.4 2.9 collective-permute-start.4
  305.1 6.4 copy-start.35
  305.1 6.4 copy-start.38
  311.3 9.2 %copy-start.16 = (bf16[1024,1536]{1,0:T(8,128)(2,1)S(1)}, bf16[1024,1536]{1,0:T(8,128)(2,1)}, u32[]{:S(2)}) copy-start(bf16[1024,1536]{1,0:T(8,128)(2,1)} %get-tuple-element.173.refs_3_) | copy-start | bytes 9437188
  311.3 9.2 %copy-start.26 = (bf16[1024,2048]{1,0:T(8,128)(2,1)S(1)}, bf16[1024,2048]{1,0:T(8,128)(2,1)}, u32[]{:S(2)}) copy-start(bf16[1024,2048]{1,0:T(8,128)(2,1)} %get-tuple-element.172) | copy-start | bytes 12582916
  311.3 9.2 %collective-permute-start.6 = (bf16[1024,1536]{1,0:T(8,128)(2,1)S(1)}, bf16[1024,1536]{1,0:T(8,128)(2,1)S(1)}, u32[]{:S(2)}, u32[]{:S(2)}) collective-permute-start(bf16[1024,1536]{1,0:T(8,128)(2,1)S(1)} %convolution_convert_fusion.3), channel_id=1, source_target_pairs={{0,1},{1,0},{2,3},{3,2},{4,5},{5,4},{6,7},{7,6},{8,9},{9,8},{10,11... | collective-permute-start | bytes 9437192 | tf_op jit(solution)/shard_map/ppermute | solution.py:1457
  325.4 24.2 %collective-permute-start.7 = (bf16[1024,3072]{1,0:T(8,128)(2,1)}, bf16[1024,3072]{1,0:T(8,128)(2,1)}, u32[]{:S(2)}, u32[]{:S(2)}) collective-permute-start(bf16[1024,3072]{1,0:T(8,128)(2,1)} %convolution_convert_fusion), channel_id=1, source_target_pairs={{0,1},{1,0},{2,3},{3,2},{4,5},{5,4},{6,7},{7,6},{8,9},{9,8},{10,11... | collective-permute-start | bytes 18874376 | tf_op jit(solution)/shard_map/ppermute | solution.py:1457
  328.4 22.9 %copy-start.36 = (bf16[1024,2048]{1,0:T(8,128)(2,1)S(1)}, bf16[1024,2048]{1,0:T(8,128)(2,1)}, u32[]{:S(2)}) copy-start(bf16[1024,2048]{1,0:T(8,128)(2,1)} %get-tuple-element.180.rows) | copy-start | bytes 12582916
  328.4 21.2 %collective-permute-start.8 = (bf16[256,1536]{1,0:T(8,128)(2,1)S(1)}, bf16[256,1536]{1,0:T(8,128)(2,1)S(1)}, u32[]{:S(2)}, u32[]{:S(2)}) collective-permute-start(bf16[256,1536]{1,0:T(8,128)(2,1)S(1)} %slice_bitcast_fusion.6), channel_id=1, source_target_pairs={{0,8},{1,9},{2,10},{3,11},{4,12},{5,13},{6,14},{7,15},{24,16},{25,... | collective-permute-start | bytes 2359304 | tf_op jit(solution)/shard_map/ppermute | solution.py:1457
  349.6 14.2 %copy-start.21 = (bf16[256,1536]{1,0:T(8,128)(2,1)}, bf16[256,1536]{1,0:T(8,128)(2,1)S(1)}, u32[]{:S(2)}) copy-start(bf16[256,1536]{1,0:T(8,128)(2,1)S(1)} %collective-permute-done.8) | copy-start | bytes 2359300
  349.6 17.8 %collective-permute-start.9 = (bf16[256,1536]{1,0:T(8,128)(2,1)S(1)}, bf16[256,1536]{1,0:T(8,128)(2,1)S(1)}, u32[]{:S(2)}, u32[]{:S(2)}) collective-permute-start(bf16[256,1536]{1,0:T(8,128)(2,1)S(1)} %slice_bitcast_fusion.5), channel_id=1, source_target_pairs={{0,8},{1,9},{2,10},{3,11},{4,12},{5,13},{6,14},{7,15},{24,16},{25,... | collective-permute-start | bytes 2359304 | tf_op jit(solution)/shard_map/ppermute | solution.py:1457
  367.4 87.7 %copy-start.23 = (bf16[256,1536]{1,0:T(8,128)(2,1)}, bf16[256,1536]{1,0:T(8,128)(2,1)S(1)}, u32[]{:S(2)}) copy-start(bf16[256,1536]{1,0:T(8,128)(2,1)S(1)} %collective-permute-done.9) | copy-start | bytes 2359300
  460.4 21.6 %copy-start.22 = (bf16[256,1536]{1,0:T(8,128)(2,1)S(1)}, bf16[256,1536]{1,0:T(8,128)(2,1)}, u32[]{:S(2)}) copy-start(bf16[256,1536]{1,0:T(8,128)(2,1)} %copy-done.21) | copy-start | bytes 2359300
  460.4 21.5 %copy-start.24 = (bf16[256,1536]{1,0:T(8,128)(2,1)S(1)}, bf16[256,1536]{1,0:T(8,128)(2,1)}, u32[]{:S(2)}) copy-start(bf16[256,1536]{1,0:T(8,128)(2,1)} %copy-done.23) | copy-start | bytes 2359300
  461.7 23.8 %copy-start.8 = (bf16[1024,2048]{1,0:T(8,128)(2,1)S(1)}, bf16[1024,2048]{1,0:T(8,128)(2,1)}, u32[]{:S(2)}) copy-start(bf16[1024,2048]{1,0:T(8,128)(2,1)} %get-tuple-element.204) | copy-start | bytes 12582916
  461.7 52.3 %collective-permute-start.10 = (bf16[256,3072]{1,0:T(8,128)(2,1)}, bf16[256,3072]{1,0:T(8,128)(2,1)}, u32[]{:S(2)}, u32[]{:S(2)}) collective-permute-start(bf16[256,3072]{1,0:T(8,128)(2,1)} %slice_bitcast_fusion), channel_id=1, source_target_pairs={{0,8},{1,9},{2,10},{3,11},{4,12},{5,13},{6,14},{7,15},{8,0},{9,1},... | collective-permute-start | bytes 4718600 | tf_op jit(solution)/shard_map/ppermute | solution.py:1457
  483.5 6.6 copy-start.31
  483.5 30.5 %collective-permute-start.13 = (bf16[2,256,1536]{2,1,0:T(8,128)(2,1)}, bf16[2,256,1536]{2,1,0:T(8,128)(2,1)}, u32[]{:S(2)}, u32[]{:S(2)}) collective-permute-start(bf16[2,256,1536]{2,1,0:T(8,128)(2,1)} %add_convert_fusion.3), channel_id=1, source_target_pairs={{8,16},{9,17},{10,18},{11,19},{12,20},{13,21},{14,22},{15,23},{16,... | collective-permute-start | bytes 4718600 | tf_op jit(solution)/shard_map/ppermute | solution.py:1457
  487.1 27.0 %collective-permute-start.12 = (bf16[256,2048]{1,0:T(8,128)(2,1)}, bf16[256,2048]{1,0:T(8,128)(2,1)}, u32[]{:S(2)}, u32[]{:S(2)}) collective-permute-start(bf16[256,2048]{1,0:T(8,128)(2,1)} %get-tuple-element.254), channel_id=1, source_target_pairs={{0,4},{1,5},{2,6},{3,7},{4,0},{5,1},{6,2},{7,3},{8,12},{9,13},{10,... | collective-permute-start | bytes 3145736 | tf_op jit(solution)/shard_map/ppermute | solution.py:1457
  489.4 24.6 %collective-permute-start.11 = (bf16[256,2048]{1,0:T(8,128)(2,1)}, bf16[256,2048]{1,0:T(8,128)(2,1)}, u32[]{:S(2)}, u32[]{:S(2)}) collective-permute-start(bf16[256,2048]{1,0:T(8,128)(2,1)} %get-tuple-element.255), channel_id=1, source_target_pairs={{0,2},{1,3},{2,0},{3,1},{4,6},{5,7},{6,4},{7,5},{8,10},{9,11},{10,... | collective-permute-start | bytes 3145736 | tf_op jit(solution)/shard_map/ppermute | solution.py:1457
  516.5 7.0 copy-start.11
  516.5 7.0 copy-start.37
  518.5 11.2 %copy-start.15 = (bf16[2,256,3072]{2,1,0:T(8,128)(2,1)S(1)}, bf16[2,256,3072]{2,1,0:T(8,128)(2,1)}, u32[]{:S(2)}) copy-start(bf16[2,256,3072]{2,1,0:T(8,128)(2,1)} %get-tuple-element.203) | copy-start | bytes 9437188
  518.6 27.6 %collective-permute-start.15 = (bf16[256,1536]{1,0:T(8,128)(2,1)S(1)}, bf16[256,1536]{1,0:T(8,128)(2,1)S(1)}, u32[]{:S(2)}, u32[]{:S(2)}) collective-permute-start(bf16[256,1536]{1,0:T(8,128)(2,1)S(1)} %slice_bitcast_fusion.1), channel_id=1, source_target_pairs={{0,8},{1,9},{2,10},{3,11},{4,12},{5,13},{6,14},{7,15},{8,0},{9,1},... | collective-permute-start | bytes 2359304 | tf_op jit(solution)/shard_map/ppermute | solution.py:1457
  529.7 6.5 copy-start.2
  529.7 6.5 copy-start.34
  532.0 9.8 %collective-permute-start.17 = (bf16[128,2048]{1,0:T(8,128)(2,1)S(1)}, bf16[128,2048]{1,0:T(8,128)(2,1)S(1)}, u32[]{:S(2)}, u32[]{:S(2)}) collective-permute-start(bf16[128,2048]{1,0:T(8,128)(2,1)S(1)} %slice.202), channel_id=1, source_target_pairs={{0,2},{1,3},{2,0},{3,1},{4,6},{5,7},{6,4},{7,5},{8,10},{9,11},{10,... | collective-permute-start | bytes 1572872 | tf_op jit(solution)/shard_map/ppermute | solution.py:1457
  532.1 12.6 %collective-permute-start.16 = (bf16[128,2048]{1,0:T(8,128)(2,1)S(1)}, bf16[128,2048]{1,0:T(8,128)(2,1)S(1)}, u32[]{:S(2)}, u32[]{:S(2)}) collective-permute-start(bf16[128,2048]{1,0:T(8,128)(2,1)S(1)} %slice.203), channel_id=1, source_target_pairs={{0,4},{1,5},{2,6},{3,7},{4,0},{5,1},{6,2},{7,3},{8,12},{9,13},{10,... | collective-permute-start | bytes 1572872 | tf_op jit(solution)/shard_map/ppermute | solution.py:1457
  537.5 7.1 %copy-start.4 = (f32[256,2048]{1,0:T(8,128)S(1)}, f32[256,2048]{1,0:T(8,128)}, u32[]{:S(2)}) copy-start(f32[256,2048]{1,0:T(8,128)} %get-tuple-element.186.refs_0_) | copy-start | bytes 6291460
  537.5 9.7 %collective-permute-start.14 = (bf16[1024,512]{1,0:T(8,128)(2,1)S(1)}, bf16[1024,512]{1,0:T(8,128)(2,1)S(1)}, u32[]{:S(2)}, u32[]{:S(2)}) collective-permute-start(bf16[1024,512]{1,0:T(8,128)(2,1)S(1)} %fusion.19), channel_id=1, source_target_pairs={{0,1},{1,0},{2,3},{3,2},{4,5},{5,4},{6,7},{7,6},{8,9},{9,8},{10,11... | collective-permute-start | bytes 3145736 | tf_op jit(solution)/shard_map/ppermute | solution.py:1457
  549.5 111.2 %copy-start.18 = (f32[256,1536]{1,0:T(8,128)S(1)}, f32[256,1536]{1,0:T(8,128)}, u32[]{:S(2)}) copy-start(f32[256,1536]{1,0:T(8,128)} %param.32) | copy-start | bytes 4718596
  549.5 111.2 %copy-start.19 = (f32[256,1536]{1,0:T(8,128)S(1)}, f32[256,1536]{1,0:T(8,128)}, u32[]{:S(2)}) copy-start(f32[256,1536]{1,0:T(8,128)} %param.31) | copy-start | bytes 4718596
  649.9 10.8 %copy-start.5 = (bf16[256,1536]{1,0:T(8,128)(2,1)S(1)}, bf16[256,1536]{1,0:T(8,128)(2,1)}, u32[]{:S(2)}) copy-start(bf16[256,1536]{1,0:T(8,128)(2,1)} %fusion.18.refs_8_) | copy-start | bytes 2359300
  649.9 10.8 %copy-start.7 = (f32[256,1536]{1,0:T(8,128)S(1)}, f32[256,1536]{1,0:T(8,128)}, u32[]{:S(2)}) copy-start(f32[256,1536]{1,0:T(8,128)} %wide_down.1) | copy-start | bytes 4718596
  649.9 40.7 %collective-permute-start.18 = (bf16[1024,2048]{1,0:T(8,128)(2,1)}, bf16[1024,2048]{1,0:T(8,128)(2,1)}, u32[]{:S(2)}, u32[]{:S(2)}) collective-permute-start(bf16[1024,2048]{1,0:T(8,128)(2,1)} %get-tuple-element.229), channel_id=1, source_target_pairs={{0,1},{1,0},{2,3},{3,2},{4,5},{5,4},{6,7},{7,6},{8,9},{9,8},{10,11... | collective-permute-start | bytes 12582920 | tf_op jit(solution)/shard_map/ppermute | solution.py:1457
  654.1 13.3 %collective-permute-start.19 = (bf16[256,1536]{1,0:T(8,128)(2,1)S(1)}, bf16[256,1536]{1,0:T(8,128)(2,1)S(1)}, u32[]{:S(2)}, u32[]{:S(2)}) collective-permute-start(bf16[256,1536]{1,0:T(8,128)(2,1)S(1)} %pad_maximum_fusion.3), channel_id=1, source_target_pairs={{1,4},{3,6},{4,1},{6,3},{9,12},{11,14},{12,9},{14,11},{17,20},{19,... | collective-permute-start | bytes 2359304 | tf_op jit(solution)/shard_map/ppermute | solution.py:1457
  657.2 27.1 %collective-permute-start.20 = (bf16[2,256,1536]{2,1,0:T(8,128)(2,1)S(1)}, bf16[2,256,1536]{2,1,0:T(8,128)(2,1)}, u32[]{:S(2)}, u32[]{:S(2)}) collective-permute-start(bf16[2,256,1536]{2,1,0:T(8,128)(2,1)S(1)} %pad_maximum_fusion), channel_id=1, source_target_pairs={{1,4},{3,6},{4,1},{6,3},{9,12},{11,14},{12,9},{14,11},{17,20},{19,... | collective-permute-start | bytes 4718600 | tf_op jit(solution)/shard_map/ppermute | solution.py:1457
  660.8 6.7 copy-start.17
  674.3 10.1 %copy-start.3 = (f32[2,256,1536]{2,1,0:T(8,128)S(1)}, f32[2,256,1536]{2,1,0:T(8,128)}, u32[]{:S(2)}) copy-start(f32[2,256,1536]{2,1,0:T(8,128)} %wide_gate.1) | copy-start | bytes 9437188
  674.3 10.0 %copy-start.13 = (f32[2,256,1536]{2,1,0:T(8,128)S(1)}, f32[2,256,1536]{2,1,0:T(8,128)}, u32[]{:S(2)}) copy-start(f32[2,256,1536]{2,1,0:T(8,128)} %param.29) | copy-start | bytes 9437188
  678.9 11.7 %copy-start.12 = (bf16[1024,2048]{1,0:T(8,128)(2,1)S(1)}, bf16[1024,2048]{1,0:T(8,128)(2,1)}, u32[]{:S(2)}) copy-start(bf16[1024,2048]{1,0:T(8,128)(2,1)} %get-tuple-element.229) | copy-start | bytes 12582916
  (12 other events, 42.5 us)

commit v3 on v2

--- a/solution.py
+++ b/solution.py
@@ -362,7 +362,7 @@
         self.size = rows // pieces
         self.outputs = [jax.ShapeDtypeStruct((2, rows, columns), parts.dtype)]
         self.scratch = [pltpu.VMEM((2, rows, columns), parts.dtype)] * 2
-        self.count, self.count_local = 4 * pieces, 0
+        self.count, self.count_local = 6 * pieces, 0
         self.in_hbm = False
 
     def peers(self, zone, side, row, core):
@@ -380,9 +380,9 @@
         self.inner = inner_zone(zone) == 1
         self.outer = inner_zone(zone) == 0
         self.steps = [
-            (slot, pl.ds(piece * self.size, self.size))
-            for piece in range(self.pieces)
-            for slot in (0, 1)
+            (slot, pl.ds(piece * size, size))
+            for slot, size in ((0, self.size), (1, self.size // 2))
+            for piece in range(self.parts.shape[1] // size)
         ]
         self.to_inner = [
             copies.make(self.parts.at[3 - slot, rows], self.inward.at[slot, rows], outer_peer)
@@ -404,7 +404,7 @@
             both = left[here, :].astype(jnp.float32) + right[here, :].astype(jnp.float32)
             target.at[slot][here, :] = both.astype(jnp.bfloat16)
 
-        for_rows(self.size, some)
+        for_rows(rows.size, some)
 
     def pump(self, steps):
         steps = [step for step in steps if step < len(self.steps)]
@@ -475,7 +475,7 @@
         self.out = targets[0]
         self.far, self.got, self.parts, self.arrived = stages
         core_peer = device(zone, side, row, 1 - core)
-        self.order = list(range(1, self.zones)) + [0]
+        self.order = list(range(2, self.zones)) + [1, 0]
         self.over = [
             copies.make(self.far.at[slot], self.got.at[slot], core_peer)
             for slot in range(self.zones)
@@ -872,14 +872,17 @@
     def _():
         for copy in block_side:
             copy.wait_recv()
-        for copy in to_side + block_side:
-            copy.wait_send()
 
     for copy in pass_row:
         copy.start()
     for copy in to_row + pass_row:
         copy.wait_recv()
         copy.wait_send()
+    @pl.when(away)
+    def _():
+        for copy in to_side + block_side:
+            copy.wait_send()
+
     natural, local = block_columns(plan, full.shape[1], side)
 
     def some(start, count):
@@ -1810,7 +1813,7 @@
     else:
         total_down = zone_total(down_parts, down_sums)
     total_gate = zone_total(gate_own, gate_last)
-    total_gate = jnp.stack([total_gate[:, :units], total_gate[:, units:]])
+    total_gate = jnp.concatenate([total_gate[:, :units], total_gate[:, units:]], 0)
     out_far = contract_rows(branch_rows[:, near_cols:], attended).astype(low)
     out_got = plan.core_swap(out_far)
     normed_terms = contract_cols(mixed_rows, full_qkv).astype(low)
@@ -1832,22 +1835,23 @@
         [
             BlockGrad(plan, normed, grad_mixed),
             ZoneBlocks(plan, out_parts, slots),
+            TurnLate(total_gate),
             TurnLate(total_down),
         ],
         gain_sum,
     )
     if plan.ordered:
-        summed_gains, total_qkv, out_sent, got_down = rest
+        summed_gains, total_qkv, out_sent, got_gate, got_down = rest
     else:
-        total_qkv, out_sent, got_down = rest
+        total_qkv, out_sent, got_gate, got_down = rest
         summed_gains = plan.sum_everywhere(
             jnp.concatenate([plan.to_natural(input_gain_grad, 1), gain_terms], 1)
         )
-    mine, summed_gains, total_qkv, out_sent, total_gate, got_down = fence(
-        mine, summed_gains, total_qkv, out_sent, total_gate, got_down
-    )
-
-    summed_gate = plan.turn(total_gate)
+    mine, summed_gains, total_qkv, out_sent, got_gate, got_down = fence(
+        mine, summed_gains, total_qkv, out_sent, got_gate, got_down
+    )
+
+    summed_gate = plan.turned(total_gate, got_gate).reshape(gate_up.shape)
     summed_down = plan.turned(total_down, got_down)
     other = plan.core_swap(mine)
     input_full, block_out = jnp.where(plan.home, mine, other), jnp.where(plan.home, other, mine)

time: 702 us -> 685 us (0.976)
  waiting for transfers between devices: 13.8 us -> 3.74 us
    ppermute x21 -> x20, waiting for transfers between devices: 13.8 us -> 3.74 us  [move(): return lax.ppermute(value, ('dp', 'tensor'), pairs)]
    ppermute x21 -> x20, starting transfers between devices: 58.5 us -> 53.7 us  [move(): return lax.ppermute(value, ('dp', 'tensor'), pairs)]
  transfers between devices with their start and end apart: 21 -> 20, of which waited for: 4 -> 1; matrix products, arithmetic and copies ran while one was open for 14% -> 14% of each run, Pallas kernels for 26% -> 27%
where the time goes in v3:
time: 685 us; the launch traced here: 681 us
  Pallas kernels  486 us (71%)
  matrix products  71.5 us (10%)
  starting transfers between devices  53.7 us (8%)
  other arithmetic  45.2 us (7%)
  local copies, waits for them, and re-layouts  18.9 us (3%)
    pallas_call x3, Pallas kernels, sum_rows(): pl.pallas_call(functools.partial(kernel, middle, jobs, len(extras), len(o...  323 us
    pallas_call x1, Pallas kernels, opening(): pl.pallas_call(functools.partial(opening_kernel, plan), out_shape=outputs...  84.1 us
    ppermute x20, starting transfers between devices, move(): return lax.ppermute(value, ('dp', 'tensor'), pairs)  53.7 us
    dot_general x6, matrix products, contract_rows(): lax.dot_general(left, right, (((0,), (0,)), ((), ())), preferred_element_...  36 us
    pallas_call x1, Pallas kernels, feed_forward(): pl.pallas_call(functools.partial(feed_kernel, plan), grid=(tiles,), out_s...  33.8 us
    dot_general x3, matrix products, contract_cols(): lax.dot_general(left, right, (((1,), (1,)), ((), ())), preferred_element_...  30.2 us
    pallas_call x1, Pallas kernels, attention_back(): pl.pallas_call(backward_kernel, out_shape=[jax.ShapeDtypeStruct((total, c...  23.2 us
    pallas_call x1, Pallas kernels, attention(): pl.pallas_call(forward_kernel, out_shape=[shape(tokens.shape[1]), shape(c...  21.4 us
  transfers between devices with their start and end apart: 20, of which 1 were waited for; matrix products, arithmetic and copies ran while one was open for 14% of the time, Pallas kernels for 27%

profile of v3, /device:TPU:1, one launch (start us, length us, event | category | flops | bytes accessed | tf_op | source)
XLA Modules:
  0.0 680.8 jit_solution(6641793447104429429)
XLA Ops:
  3.2 2.6 reshape.95.wide_qkv
  5.8 84.1 %opening.1 = (bf16[8,256,1024]{2,1,0:T(8,128)(2,1)}, bf16[8,16,128]{2,1,0:T(8,128)(2,1)}, bf16[256,3072]{1,0:T(8,128)(2,1)}, bf16[256,512]{1,0:T(8,128)(2,1)}, b...) custom-call(f32[256,1024]{1,0:T(8,128)} %reshape.95.wide_qkv, ...), custom_call_target="tpu_custom_call" | custom-call | flops 1000000 | bytes 100000 | tf_op jit(solution)/shard_map/opening/pallas_call | solution.py:1110
  90.0 1.4 collective-permute-start.2
  91.3 2.1 collective-permute-start.1
  93.4 1.5 collective-permute-start.3
  94.8 3.7 collective-permute-start.5
  100.4 2.6 fusion.27
  103.5 21.4 %attention.1 = (bf16[1024,2048]{1,0:T(8,128)(2,1)}, f32[1024,1024]{1,0:T(8,128)}, bf16[1024,512]{1,0:T(8,128)(2,1)S(1)}, bf16[1024,256]{1,0:T(8,128)(2,1)S(1)}, ...) custom-call(bf16[1024,2048]{1,0:T(8,128)(2,1)} %get-tuple-element.134.tokens, bf16[2048,1024]{1,0:T(8,128)(2,1)} %bitcast.67, ...), custom_call_target="tpu_custom_call" | custom-call | flops 1000000 | bytes 100000 | tf_op jit(solution)/shard_map/attention/pallas_call | solution.py:1265
  127.8 1.3 constant_dynamic-slice_fusion.10
  130.4 4.4 convolution_convert_fusion.2.terms
  134.8 136.4 %hidden_rows.1 = (bf16[1024,2048]{1,0:T(8,128)(2,1)}, f32[256,2048]{1,0:T(8,128)}, bf16[8,256,3072]{2,1,0:T(8,128)(2,1)}, bf16[8,256,1536]{2,1,0:T(8,128)(2,1)}) custom-call(bf16[1024,2048]{1,0:T(8,128)(2,1)} %convolution_convert_fusion.2.terms, bf16[256,2048]{1,0:T(8,128)(2,1)} %pad_maximum_fusion.1.refs_0_, f32[1,2048]{1,0:T(1,128)} %bitcast.75, ...), custom_call_target="tpu_custom_call" | custom-call | flops 1000000 | bytes 100000 | tf_op jit(solution)/shard_map/hidden_rows/pallas_call | solution.py:924
  271.2 33.8 %feed_forward.1 = (bf16[1024,1536]{1,0:T(8,128)(2,1)}, bf16[1024,3072]{1,0:T(8,128)(2,1)}, bf16[1024,2048]{1,0:T(8,128)(2,1)}) custom-call(bf16[1024,2048]{1,0:T(8,128)(2,1)} %get-tuple-element.181.rows, bf16[1024,2048]{1,0:T(8,128)(2,1)} %own_grad, bf16[1024,2048]{1,0:T(8,128)(2,1)} %collective-permute-done.5.got_grad, bf16[2048,3072]{1,0:T(8,128)(2,1)} %bitcast.78, ...), custom_call_target="tpu_custom_call" | custom-call | flops 19327352832 | bytes 40000000 | tf_op jit(solution)/shard_map/feed_forward/pallas_call | solution.py:1408
  305.0 6.1 convolution_convert_fusion.3
  311.4 8.9 %convolution_convert_fusion = bf16[1024,3072]{1,0:T(8,128)(2,1)} fusion(bf16[1024,3072]{1,0:T(8,128)(2,1)S(1)} %copy-done.43, bf16[1024,2048]{1,0:T(8,128)(2,1)S(1)} %copy-done.40), kind=kOutput, calls=%fused_computation.2 | convolution fusion | flops 6445596672 | bytes 14680064 | tf_op jit(solution)/shard_map/dot_general | solution.py:55
  320.3 4.9 add_convert_fusion.1
  325.6 1.4 fusion.38
  328.2 1.6 collective-permute-start.8
  329.8 19.6 %convolution_convert_fusion.1.terms = bf16[1024,2048]{1,0:T(8,128)(2,1)} fusion(bf16[1024,3072]{1,0:T(8,128)(2,1)} %get-tuple-element.182, bf16[2048,3072]{1,0:T(8,128)(2,1)} %bitcast.80), kind=kOutput, calls=%fused_computation.8 | convolution fusion | flops 12886999040 | bytes 23068672 | tf_op jit(solution)/shard_map/dot_general | solution.py:61
  349.5 1.6 collective-permute-start.9
  351.1 12.5 %add_convert_fusion = bf16[1024,3072]{1,0:T(8,128)(2,1)} fusion(bf16[1024,3072]{1,0:T(8,128)(2,1)} %collective-permute-done.7, bf16[1024,3072]{1,0:T(8,128)(2,1)} %get-tuple-element.182, bf16[1024,2048]{1,0:T(8,128)(2,1)S(1)} %copy-done.41), kind=kOutput, calls=%fused_computation | convolution fusion | flops 6451888128 | bytes 20971520 | tf_op jit(solution)/shard_map/dot_general | solution.py:55
  363.5 3.7 collective-permute-done.9
  367.2 85.6 %grad_hidden_rows.1 = (bf16[1024,2048]{1,0:T(8,128)(2,1)}, f32[256,2048]{1,0:T(8,128)}, f32[1,2048]{1,0:T(1,128)}, bf16[1024,2048]{1,0:T(8,128)(2,1)}, bf16[2,256,3072]{2,1,0:T(8,128)(2,1)}) custom-call(bf16[1024,2048]{1,0:T(8,128)(2,1)} %convolution_convert_fusion.1.terms, f32[256,2048]{1,0:T(8,128)} %get-tuple-element.187.refs_0_, ...), custom_call_target="tpu_custom_call" | custom-call | flops 1000000 | bytes 100000 | tf_op jit(solution)/shard_map/grad_hidden_rows/pallas_call | solution.py:924
  452.8 5.3 convolution_convert_fusion.5.grad_rows
  459.4 19.3 %collective-permute-start.10 = (bf16[256,3072]{1,0:T(8,128)(2,1)}, bf16[256,3072]{1,0:T(8,128)(2,1)}, u32[]{:S(2)}, u32[]{:S(2)}) collective-permute-start(bf16[256,3072]{1,0:T(8,128)(2,1)} %slice_bitcast_fusion), channel_id=1, source_target_pairs={{0,8},{1,9},{2,10},{3,11},{4,12},{5,13},{6,14},{7,15},{8,0},{9,1},... | collective-permute-start | bytes 4718600 | tf_op jit(solution)/shard_map/ppermute | solution.py:1460
  478.8 1.5 add_convert_fusion.3
  480.3 2.0 collective-permute-start.13
  482.2 1.6 fusion.37
  484.1 1.6 collective-permute-start.11
  485.7 23.2 %attention_back.1 = (bf16[1024,1024]{1,0:T(8,128)(2,1)}, bf16[1024,1024]{1,0:T(8,128)(2,1)}, f32[1,128]{1,0:T(1,128)S(1)}, f32[1,128]{1,0:T(1,128)S(1)}) custom-call(bf16[1024,512]{1,0:T(8,128)(2,1)S(1)} %get-tuple-element.138.query, bf16[1024,256]{1,0:T(8,128)(2,1)S(1)} %get-tuple-element.139.key, bf16[1024,256]{1,0:T(8,128)(2,1)S(1)} %get-tuple-element.140.value, ...), custom_call_target="tpu_custom_call" | custom-call | flops 1000000 | bytes 100000 | tf_op jit(solution)/shard_map/attention_back/pallas_call | solution.py:1336
  509.7 2.1 slice_add_fusion.1
  512.1 1.9 add_convert_fusion.2
  514.1 2.8 collective-permute-start.15
  516.9 6.2 convolution_convert_fusion.4.terms
  523.2 2.1 fusion.2
  525.7 2.1 collective-permute-start.16
  529.1 8.2 %collective-permute-start.14 = (bf16[1024,512]{1,0:T(8,128)(2,1)S(1)}, bf16[1024,512]{1,0:T(8,128)(2,1)S(1)}, u32[]{:S(2)}, u32[]{:S(2)}) collective-permute-start(bf16[1024,512]{1,0:T(8,128)(2,1)S(1)} %fusion.19), channel_id=1, source_target_pairs={{0,1},{1,0},{2,3},{3,2},{4,5},{5,4},{6,7},{7,6},{8,9},{9,8},{10,11... | collective-permute-start | bytes 3145736 | tf_op jit(solution)/shard_map/ppermute | solution.py:1460
  538.6 1.5 fusion.4.refs_3_
  541.2 2.3 add_convert_fusion.4
  543.4 101.4 %grad_input_rows.1 = (bf16[1024,2048]{1,0:T(8,128)(2,1)}, f32[1,2048]{1,0:T(1,128)}, f32[1,4352]{1,0:T(1,128)}, bf16[256,1024]{1,0:T(8,128)(2,1)}, bf16[3,256,51...) custom-call(bf16[1024,2048]{1,0:T(8,128)(2,1)} %convolution_convert_fusion.4.terms, ...), custom_call_target="tpu_custom_call" | custom-call | flops 1000000 | bytes 100000 | tf_op jit(solution)/shard_map/grad_input_rows/pallas_call | solution.py:924
  644.9 1.4 fusion.26
  647.6 4.7 collective-permute-start.19
  653.8 1.6 broadcast_select_fusion.1
  655.5 5.0 multiply_subtract_fusion
  660.6 3.1 multiply_subtract_fusion.1
  665.0 2.8 reshape.107
  667.8 2.8 multiply_subtract_fusion.3
  670.6 3.2 multiply_subtract_fusion.2
  673.7 6.8 %select_convert_fusion = (f32[1024,2048]{1,0:T(8,128)}, bf16[1024,2048]{1,0:T(8,128)(2,1)}) fusion(bf16[1024,2048]{1,0:T(8,128)(2,1)S(1)} %copy-done.13, bf16[1024,2048]{1,0:T(8,128)(2,1)} %collective-permute-done.18, pred[]{:T(512)S(6)} %eq.9), kind=kLoop, calls=%fused_computation.6 | loop fusion | flops 6291456 | bytes 20971520 | tf_op jit(solution)/shard_map/convert_element_type | solution.py:1869
  (180 shorter events, 21.2 us)
Async XLA Ops:
  90.0 35.2 %collective-permute-start.2 = (bf16[256,512]{1,0:T(8,128)(2,1)}, bf16[256,512]{1,0:T(8,128)(2,1)S(1)}, u32[]{:S(2)}, u32[]{:S(2)}) collective-permute-start(bf16[256,512]{1,0:T(8,128)(2,1)} %get-tuple-element.148), channel_id=1, source_target_pairs={{0,16},{1,17},{2,18},{3,19},{4,20},{5,21},{6,22},{7,23},{8,24},{9,... | collective-permute-start | bytes 786440 | tf_op jit(solution)/shard_map/ppermute | solution.py:1460
  91.3 33.9 %collective-permute-start.1 = (bf16[256,512]{1,0:T(8,128)(2,1)}, bf16[256,512]{1,0:T(8,128)(2,1)}, u32[]{:S(2)}, u32[]{:S(2)}) collective-permute-start(bf16[256,512]{1,0:T(8,128)(2,1)} %get-tuple-element.148), channel_id=1, source_target_pairs={{0,24},{1,25},{2,26},{3,27},{4,28},{5,29},{6,30},{7,31},{8,16},{9,... | collective-permute-start | bytes 786440 | tf_op jit(solution)/shard_map/ppermute | solution.py:1460
  93.4 31.8 %collective-permute-start = (bf16[256,512]{1,0:T(8,128)(2,1)}, bf16[256,512]{1,0:T(8,128)(2,1)}, u32[]{:S(2)}, u32[]{:S(2)}) collective-permute-start(bf16[256,512]{1,0:T(8,128)(2,1)} %get-tuple-element.148), channel_id=1, source_target_pairs={{0,8},{1,9},{2,10},{3,11},{4,12},{5,13},{6,14},{7,15},{8,0},{9,1},... | collective-permute-start | bytes 786440 | tf_op jit(solution)/shard_map/ppermute | solution.py:1460
  93.4 31.8 %collective-permute-start.3 = (bf16[256,1536]{1,0:T(8,128)(2,1)}, bf16[256,1536]{1,0:T(8,128)(2,1)}, u32[]{:S(2)}, u32[]{:S(2)}) collective-permute-start(bf16[256,1536]{1,0:T(8,128)(2,1)} %get-tuple-element.157.refs_4_), channel_id=1, source_target_pairs={{0,8},{1,9},{2,10},{3,11},{4,12},{5,13},{6,14},{7,15},{8,0},{9,1},... | collective-permute-start | bytes 2359304 | tf_op jit(solution)/shard_map/ppermute | solution.py:1460
  94.8 176.3 %collective-permute-start.5 = (bf16[1024,2048]{1,0:T(8,128)(2,1)}, bf16[1024,2048]{1,0:T(8,128)(2,1)}, u32[]{:S(2)}, u32[]{:S(2)}) collective-permute-start(bf16[1024,2048]{1,0:T(8,128)(2,1)} %own_grad), channel_id=1, source_target_pairs={{1,4},{3,6},{4,1},{6,3},{9,12},{11,14},{12,9},{14,11},{17,20},{19,... | collective-permute-start | bytes 12582920 | tf_op jit(solution)/shard_map/ppermute | solution.py:1460
  103.5 21.5 %copy-start = (f32[2048]{0:T(1024)}, f32[2048]{0:T(1024)S(1)}, u32[]{:S(2)}) copy-start(f32[2048]{0:T(1024)S(1)} %constant_dynamic-update-slice_fusion.26) | copy-start | bytes 24580
  103.5 21.6 %copy-start.32 = (bf16[256,512]{1,0:T(8,128)(2,1)S(1)}, bf16[256,512]{1,0:T(8,128)(2,1)}, u32[]{:S(2)}) copy-start(bf16[256,512]{1,0:T(8,128)(2,1)} %get-tuple-element.148) | copy-start | bytes 786436
  125.0 5.4 copy-start.1
  127.3 2.9 collective-permute-start.4
  305.0 6.4 copy-start.40
  305.0 6.4 copy-start.43
  311.1 9.2 %copy-start.18 = (bf16[1024,1536]{1,0:T(8,128)(2,1)S(1)}, bf16[1024,1536]{1,0:T(8,128)(2,1)}, u32[]{:S(2)}) copy-start(bf16[1024,1536]{1,0:T(8,128)(2,1)} %get-tuple-element.174.refs_3_) | copy-start | bytes 9437188
  311.2 9.2 %copy-start.31 = (bf16[1024,2048]{1,0:T(8,128)(2,1)S(1)}, bf16[1024,2048]{1,0:T(8,128)(2,1)}, u32[]{:S(2)}) copy-start(bf16[1024,2048]{1,0:T(8,128)(2,1)} %get-tuple-element.173) | copy-start | bytes 12582916
  311.2 9.1 %collective-permute-start.6 = (bf16[1024,1536]{1,0:T(8,128)(2,1)S(1)}, bf16[1024,1536]{1,0:T(8,128)(2,1)S(1)}, u32[]{:S(2)}, u32[]{:S(2)}) collective-permute-start(bf16[1024,1536]{1,0:T(8,128)(2,1)S(1)} %convolution_convert_fusion.3), channel_id=1, source_target_pairs={{0,1},{1,0},{2,3},{3,2},{4,5},{5,4},{6,7},{7,6},{8,9},{9,8},{10,11... | collective-permute-start | bytes 9437192 | tf_op jit(solution)/shard_map/ppermute | solution.py:1460
  325.2 24.2 %collective-permute-start.7 = (bf16[1024,3072]{1,0:T(8,128)(2,1)}, bf16[1024,3072]{1,0:T(8,128)(2,1)}, u32[]{:S(2)}, u32[]{:S(2)}) collective-permute-start(bf16[1024,3072]{1,0:T(8,128)(2,1)} %convolution_convert_fusion), channel_id=1, source_target_pairs={{0,1},{1,0},{2,3},{3,2},{4,5},{5,4},{6,7},{7,6},{8,9},{9,8},{10,11... | collective-permute-start | bytes 18874376 | tf_op jit(solution)/shard_map/ppermute | solution.py:1460
  328.2 22.9 %copy-start.41 = (bf16[1024,2048]{1,0:T(8,128)(2,1)S(1)}, bf16[1024,2048]{1,0:T(8,128)(2,1)}, u32[]{:S(2)}) copy-start(bf16[1024,2048]{1,0:T(8,128)(2,1)} %get-tuple-element.181.rows) | copy-start | bytes 12582916
  328.2 21.2 %collective-permute-start.8 = (bf16[256,1536]{1,0:T(8,128)(2,1)S(1)}, bf16[256,1536]{1,0:T(8,128)(2,1)S(1)}, u32[]{:S(2)}, u32[]{:S(2)}) collective-permute-start(bf16[256,1536]{1,0:T(8,128)(2,1)S(1)} %slice_bitcast_fusion.4), channel_id=1, source_target_pairs={{0,8},{1,9},{2,10},{3,11},{4,12},{5,13},{6,14},{7,15},{24,16},{25,... | collective-permute-start | bytes 2359304 | tf_op jit(solution)/shard_map/ppermute | solution.py:1460
  349.4 14.2 %copy-start.25 = (bf16[256,1536]{1,0:T(8,128)(2,1)}, bf16[256,1536]{1,0:T(8,128)(2,1)S(1)}, u32[]{:S(2)}) copy-start(bf16[256,1536]{1,0:T(8,128)(2,1)S(1)} %collective-permute-done.8) | copy-start | bytes 2359300
  349.5 17.8 %collective-permute-start.9 = (bf16[256,1536]{1,0:T(8,128)(2,1)S(1)}, bf16[256,1536]{1,0:T(8,128)(2,1)S(1)}, u32[]{:S(2)}, u32[]{:S(2)}) collective-permute-start(bf16[256,1536]{1,0:T(8,128)(2,1)S(1)} %slice_bitcast_fusion.3), channel_id=1, source_target_pairs={{0,8},{1,9},{2,10},{3,11},{4,12},{5,13},{6,14},{7,15},{24,16},{25,... | collective-permute-start | bytes 2359304 | tf_op jit(solution)/shard_map/ppermute | solution.py:1460
  367.2 85.6 %copy-start.27 = (bf16[256,1536]{1,0:T(8,128)(2,1)}, bf16[256,1536]{1,0:T(8,128)(2,1)S(1)}, u32[]{:S(2)}) copy-start(bf16[256,1536]{1,0:T(8,128)(2,1)S(1)} %collective-permute-done.9) | copy-start | bytes 2359300
  452.8 5.3 copy-start.16
  458.2 20.6 %copy-start.26 = (bf16[256,1536]{1,0:T(8,128)(2,1)S(1)}, bf16[256,1536]{1,0:T(8,128)(2,1)}, u32[]{:S(2)}) copy-start(bf16[256,1536]{1,0:T(8,128)(2,1)} %copy-done.25) | copy-start | bytes 2359300
  458.2 20.6 %copy-start.28 = (bf16[256,1536]{1,0:T(8,128)(2,1)S(1)}, bf16[256,1536]{1,0:T(8,128)(2,1)}, u32[]{:S(2)}) copy-start(bf16[256,1536]{1,0:T(8,128)(2,1)} %copy-done.27) | copy-start | bytes 2359300
  459.4 22.8 %copy-start.9 = (bf16[1024,2048]{1,0:T(8,128)(2,1)S(1)}, bf16[1024,2048]{1,0:T(8,128)(2,1)}, u32[]{:S(2)}) copy-start(bf16[1024,2048]{1,0:T(8,128)(2,1)} %get-tuple-element.205) | copy-start | bytes 12582916
  459.4 50.2 %collective-permute-start.10 = (bf16[256,3072]{1,0:T(8,128)(2,1)}, bf16[256,3072]{1,0:T(8,128)(2,1)}, u32[]{:S(2)}, u32[]{:S(2)}) collective-permute-start(bf16[256,3072]{1,0:T(8,128)(2,1)} %slice_bitcast_fusion), channel_id=1, source_target_pairs={{0,8},{1,9},{2,10},{3,11},{4,12},{5,13},{6,14},{7,15},{8,0},{9,1},... | collective-permute-start | bytes 4718600 | tf_op jit(solution)/shard_map/ppermute | solution.py:1460
  480.3 5.4 copy-start.36
  480.3 29.4 %collective-permute-start.13 = (bf16[2,256,1536]{2,1,0:T(8,128)(2,1)}, bf16[2,256,1536]{2,1,0:T(8,128)(2,1)}, u32[]{:S(2)}, u32[]{:S(2)}) collective-permute-start(bf16[2,256,1536]{2,1,0:T(8,128)(2,1)} %add_convert_fusion.3), channel_id=1, source_target_pairs={{8,16},{9,17},{10,18},{11,19},{12,20},{13,21},{14,22},{15,23},{16,... | collective-permute-start | bytes 4718600 | tf_op jit(solution)/shard_map/ppermute | solution.py:1460
  483.8 25.8 %collective-permute-start.12 = (bf16[256,2048]{1,0:T(8,128)(2,1)}, bf16[256,2048]{1,0:T(8,128)(2,1)}, u32[]{:S(2)}, u32[]{:S(2)}) collective-permute-start(bf16[256,2048]{1,0:T(8,128)(2,1)} %get-tuple-element.256), channel_id=1, source_target_pairs={{0,4},{1,5},{2,6},{3,7},{4,0},{5,1},{6,2},{7,3},{8,12},{9,13},{10,... | collective-permute-start | bytes 3145736 | tf_op jit(solution)/shard_map/ppermute | solution.py:1460
  484.1 25.5 %collective-permute-start.11 = (bf16[256,2048]{1,0:T(8,128)(2,1)}, bf16[256,2048]{1,0:T(8,128)(2,1)}, u32[]{:S(2)}, u32[]{:S(2)}) collective-permute-start(bf16[256,2048]{1,0:T(8,128)(2,1)} %get-tuple-element.257), channel_id=1, source_target_pairs={{0,2},{1,3},{2,0},{3,1},{4,6},{5,7},{6,4},{7,5},{8,10},{9,11},{10,... | collective-permute-start | bytes 3145736 | tf_op jit(solution)/shard_map/ppermute | solution.py:1460
  514.1 9.0 %copy-start.17 = (bf16[2,256,3072]{2,1,0:T(8,128)(2,1)S(1)}, bf16[2,256,3072]{2,1,0:T(8,128)(2,1)}, u32[]{:S(2)}) copy-start(bf16[2,256,3072]{2,1,0:T(8,128)(2,1)} %get-tuple-element.204) | copy-start | bytes 9437188
  514.1 26.0 %collective-permute-start.15 = (bf16[256,1536]{1,0:T(8,128)(2,1)S(1)}, bf16[256,1536]{1,0:T(8,128)(2,1)S(1)}, u32[]{:S(2)}, u32[]{:S(2)}) collective-permute-start(bf16[256,1536]{1,0:T(8,128)(2,1)S(1)} %slice_bitcast_fusion.1), channel_id=1, source_target_pairs={{0,8},{1,9},{2,10},{3,11},{4,12},{5,13},{6,14},{7,15},{8,0},{9,1},... | collective-permute-start | bytes 2359304 | tf_op jit(solution)/shard_map/ppermute | solution.py:1460
  525.4 13.1 %collective-permute-start.17 = (bf16[128,2048]{1,0:T(8,128)(2,1)S(1)}, bf16[128,2048]{1,0:T(8,128)(2,1)S(1)}, u32[]{:S(2)}, u32[]{:S(2)}) collective-permute-start(bf16[128,2048]{1,0:T(8,128)(2,1)S(1)} %slice.200), channel_id=1, source_target_pairs={{0,2},{1,3},{2,0},{3,1},{4,6},{5,7},{6,4},{7,5},{8,10},{9,11},{10,... | collective-permute-start | bytes 1572872 | tf_op jit(solution)/shard_map/ppermute | solution.py:1460
  525.7 12.8 %collective-permute-start.16 = (bf16[128,2048]{1,0:T(8,128)(2,1)S(1)}, bf16[128,2048]{1,0:T(8,128)(2,1)S(1)}, u32[]{:S(2)}, u32[]{:S(2)}) collective-permute-start(bf16[128,2048]{1,0:T(8,128)(2,1)S(1)} %slice.201), channel_id=1, source_target_pairs={{0,4},{1,5},{2,6},{3,7},{4,0},{5,1},{6,2},{7,3},{8,12},{9,13},{10,... | collective-permute-start | bytes 1572872 | tf_op jit(solution)/shard_map/ppermute | solution.py:1460
  529.1 9.5 %copy-start.5 = (f32[256,2048]{1,0:T(8,128)S(1)}, f32[256,2048]{1,0:T(8,128)}, u32[]{:S(2)}) copy-start(f32[256,2048]{1,0:T(8,128)} %get-tuple-element.187.refs_0_) | copy-start | bytes 6291460
  529.1 12.0 %collective-permute-start.14 = (bf16[1024,512]{1,0:T(8,128)(2,1)S(1)}, bf16[1024,512]{1,0:T(8,128)(2,1)S(1)}, u32[]{:S(2)}, u32[]{:S(2)}) collective-permute-start(bf16[1024,512]{1,0:T(8,128)(2,1)S(1)} %fusion.19), channel_id=1, source_target_pairs={{0,1},{1,0},{2,3},{3,2},{4,5},{5,4},{6,7},{7,6},{8,9},{9,8},{10,11... | collective-permute-start | bytes 3145736 | tf_op jit(solution)/shard_map/ppermute | solution.py:1460
  543.4 109.7 %copy-start.34 = (f32[544]{0:T(1024)S(1)}, f32[544]{0:T(1024)}, u32[]{:S(2)}) copy-start(f32[544]{0:T(1024)} %param.33) | copy-start | bytes 6532
  543.4 109.7 %copy-start.37 = (f32[544]{0:T(1024)S(1)}, f32[544]{0:T(1024)}, u32[]{:S(2)}) copy-start(f32[544]{0:T(1024)} %param.35) | copy-start | bytes 6532
  543.4 109.8 %copy-start.38 = (f32[544]{0:T(1024)S(1)}, f32[544]{0:T(1024)}, u32[]{:S(2)}) copy-start(f32[544]{0:T(1024)} %param.34) | copy-start | bytes 6532
  543.4 112.0 %copy-start.14 = (f32[2,256,1536]{2,1,0:T(8,128)S(1)}, f32[2,256,1536]{2,1,0:T(8,128)}, u32[]{:S(2)}) copy-start(f32[2,256,1536]{2,1,0:T(8,128)} %param.29) | copy-start | bytes 9437188
  543.4 112.0 %copy-start.15 = (f32[2,256,1536]{2,1,0:T(8,128)S(1)}, f32[2,256,1536]{2,1,0:T(8,128)}, u32[]{:S(2)}) copy-start(f32[2,256,1536]{2,1,0:T(8,128)} %param.28) | copy-start | bytes 9437188
  644.9 8.9 %copy-start.3 = (bf16[512,1536]{1,0:T(8,128)(2,1)S(1)}, bf16[512,1536]{1,0:T(8,128)(2,1)}, u32[]{:S(2)}) copy-start(bf16[512,1536]{1,0:T(8,128)(2,1)} %pad_maximum_fusion.refs_8_) | copy-start | bytes 4718596
  646.3 9.1 %copy-start.4 = (f32[2,256,1536]{2,1,0:T(8,128)S(1)}, f32[2,256,1536]{2,1,0:T(8,128)}, u32[]{:S(2)}) copy-start(f32[2,256,1536]{2,1,0:T(8,128)} %wide_gate.1) | copy-start | bytes 9437188
  647.6 16.1 %collective-permute-start.19 = (bf16[256,1536]{1,0:T(8,128)(2,1)S(1)}, bf16[256,1536]{1,0:T(8,128)(2,1)S(1)}, u32[]{:S(2)}, u32[]{:S(2)}) collective-permute-start(bf16[256,1536]{1,0:T(8,128)(2,1)S(1)} %pad_maximum_fusion.3), channel_id=1, source_target_pairs={{1,4},{3,6},{4,1},{6,3},{9,12},{11,14},{12,9},{14,11},{17,20},{19,... | collective-permute-start | bytes 2359304 | tf_op jit(solution)/shard_map/ppermute | solution.py:1460
  652.3 21.4 %collective-permute-start.18 = (bf16[1024,2048]{1,0:T(8,128)(2,1)}, bf16[1024,2048]{1,0:T(8,128)(2,1)}, u32[]{:S(2)}, u32[]{:S(2)}) collective-permute-start(bf16[1024,2048]{1,0:T(8,128)(2,1)} %get-tuple-element.231), channel_id=1, source_target_pairs={{0,1},{1,0},{2,3},{3,2},{4,5},{5,4},{6,7},{7,6},{8,9},{9,8},{10,11... | collective-permute-start | bytes 12582920 | tf_op jit(solution)/shard_map/ppermute | solution.py:1460
  655.5 5.1 copy-start.7
  655.5 5.1 copy-start.8
  655.5 5.1 copy-start.29
  665.0 5.5 copy-start.10
  (16 other events, 57.8 us)

commit v4 on v3

--- a/solution.py
+++ b/solution.py
@@ -317,6 +317,12 @@
             copy.wait_recv()
 
 
+def due(point, early, total):
+    if 0 in point:
+        return range(early)
+    return range(early, early + 1) if 1 in point else range(early + 1, total)
+
+
 def inner_zone(zone):
     return lax.rem(lax.div(zone + 1, 2), 2)
 
@@ -356,13 +362,12 @@
 
 
 class PairScatter:
-    def __init__(self, parts, pieces):
-        self.sources, self.pieces = [parts], pieces
+    def __init__(self, parts):
+        self.sources = [parts]
         _, rows, columns = parts.shape
-        self.size = rows // pieces
         self.outputs = [jax.ShapeDtypeStruct((2, rows, columns), parts.dtype)]
         self.scratch = [pltpu.VMEM((2, rows, columns), parts.dtype)] * 2
-        self.count, self.count_local = 6 * pieces, 0
+        self.count, self.count_local = 14, 0
         self.in_hbm = False
 
     def peers(self, zone, side, row, core):
@@ -379,10 +384,12 @@
         outer_peer = device(flipped(zone, 1), side, row, core)
         self.inner = inner_zone(zone) == 1
         self.outer = inner_zone(zone) == 0
+        rows = self.parts.shape[1]
+        cuts = ((0, (rows // 4, rows // 4, rows // 2)), (1, (rows // 4,) * 4))
         self.steps = [
-            (slot, pl.ds(piece * size, size))
-            for slot, size in ((0, self.size), (1, self.size // 2))
-            for piece in range(self.parts.shape[1] // size)
+            (slot, pl.ds(sum(sizes[:place]), size))
+            for slot, sizes in cuts
+            for place, size in enumerate(sizes)
         ]
         self.to_inner = [
             copies.make(self.parts.at[3 - slot, rows], self.inward.at[slot, rows], outer_peer)
@@ -407,7 +414,7 @@
         for_rows(rows.size, some)
 
     def pump(self, steps):
-        steps = [step for step in steps if step < len(self.steps)]
+        steps = due(steps, 2, len(self.steps))
 
         @pl.when(self.inner)
         def _():
@@ -541,10 +548,15 @@
 
 
 class PairTree:
-    def __init__(self, pairs, pieces):
+    def __init__(self, pairs):
+        halves_of = [own.shape[0] // 2 for own, *_ in pairs]
+        self.cuts = [
+            (size // 2, size // 2, size) if weight == 0 else (size, size)
+            for weight, size in enumerate(halves_of)
+        ]
+        pieces = [len(cut) for cut in self.cuts]
         self.pairs = [len(pair) for pair in pairs]
         self.sources = [shard for pair in pairs for shard in pair]
-        self.pieces = pieces
         self.outputs = [
             jax.ShapeDtypeStruct((8,) + own.shape, own.dtype) for own, *_ in pairs
         ]
@@ -578,9 +590,8 @@
             if len(pair) == 1:
                 pair.append(late_stages.pop(0))
                 self.partners.append(copies.start(pair[0], pair[1], outer_peer))
-            size = pair[0].shape[0] // self.pieces[weight]
-            for piece in range(self.pieces[weight]):
-                rows = pl.ds(piece * size, size)
+            for place, size in enumerate(self.cuts[weight]):
+                rows = pl.ds(sum(self.cuts[weight][:place]), size)
                 for slot in (0, 1):
                     here = landing.at[slot, rows]
                     self.across.append(copies.make(pair[slot].at[rows], here, inner_peer))
@@ -614,7 +625,8 @@
         self.place[swapped].start()
 
     def pump(self, steps):
-        steps = [step for step in steps if step < len(self.across)]
+        middle = 1 in steps
+        steps = due(steps, 3, len(self.across))
 
         @pl.when(self.inner)
         def _():
@@ -632,10 +644,10 @@
                 if step > 0:
                     self.arrive(step - 1)
 
-        for copy in self.partners if 1 in steps else []:
+        for copy in self.partners if middle else []:
             copy.wait_recv()
             copy.wait_send()
-        for copy in self.later if 1 in steps else []:
+        for copy in self.later if middle else []:
             copy.start()
 
     def finish(self):
@@ -1700,7 +1712,7 @@
     full_out = jnp.concatenate([near_out, far_out], 0)
     branch_terms = contract_cols(attended, full_out).astype(low)
     pairs = [(turned_gate, partner_gate), (turned_down, partner_down)]
-    jobs = [PairTree(pairs, (2, 2))] if tree else []
+    jobs = [PairTree(pairs)] if tree else []
     normed_rows, hidden, *gathered = sum_rows(
         plan,
         spread_kernel,
@@ -1779,7 +1791,7 @@
         1,
         [
             SideDot(active, full_down),
-            PairScatter(gate_parts, 2) if tree else ZoneBlocks(plan, gate_parts, slots),
+            PairScatter(gate_parts) if tree else ZoneBlocks(plan, gate_parts, slots),
         ],
     )
     branch_rows, grad_hidden, post_gain_grad, gate_sums, mlp_terms, down_parts, down_sums = fence(

time: 685 us -> 685 us (level)
  no operation moved by 1% of the time
where the time goes in v4:
time: 685 us; the launch traced here: 681 us
  Pallas kernels  486 us (71%)
  matrix products  71.5 us (10%)
  starting transfers between devices  53.9 us (8%)
  other arithmetic  45.2 us (7%)
  local copies, waits for them, and re-layouts  18.9 us (3%)
    pallas_call x3, Pallas kernels, sum_rows(): pl.pallas_call(functools.partial(kernel, middle, jobs, len(extras), len(o...  323 us
    pallas_call x1, Pallas kernels, opening(): pl.pallas_call(functools.partial(opening_kernel, plan), out_shape=outputs...  84.1 us
    ppermute x20, starting transfers between devices, move(): return lax.ppermute(value, ('dp', 'tensor'), pairs)  53.9 us
    dot_general x6, matrix products, contract_rows(): lax.dot_general(left, right, (((0,), (0,)), ((), ())), preferred_element_...  36 us
    pallas_call x1, Pallas kernels, feed_forward(): pl.pallas_call(functools.partial(feed_kernel, plan), grid=(tiles,), out_s...  33.8 us
    dot_general x3, matrix products, contract_cols(): lax.dot_general(left, right, (((1,), (1,)), ((), ())), preferred_element_...  30.2 us
    pallas_call x1, Pallas kernels, attention_back(): pl.pallas_call(backward_kernel, out_shape=[jax.ShapeDtypeStruct((total, c...  23.2 us
    pallas_call x1, Pallas kernels, attention(): pl.pallas_call(forward_kernel, out_shape=[shape(tokens.shape[1]), shape(c...  21.4 us
  transfers between devices with their start and end apart: 20, of which 1 were waited for; matrix products, arithmetic and copies ran while one was open for 14% of the time, Pallas kernels for 27%

profile of v4, /device:TPU:1, one launch (start us, length us, event | category | flops | bytes accessed | tf_op | source)
XLA Modules:
  0.0 681.0 jit_solution(16489960285958836825)
XLA Ops:
  3.2 2.6 reshape.95.wide_qkv
  5.8 84.1 %opening.1 = (bf16[8,256,1024]{2,1,0:T(8,128)(2,1)}, bf16[8,16,128]{2,1,0:T(8,128)(2,1)}, bf16[256,3072]{1,0:T(8,128)(2,1)}, bf16[256,512]{1,0:T(8,128)(2,1)}, b...) custom-call(f32[256,1024]{1,0:T(8,128)} %reshape.95.wide_qkv, ...), custom_call_target="tpu_custom_call" | custom-call | flops 1000000 | bytes 100000 | tf_op jit(solution)/shard_map/opening/pallas_call | solution.py:1122
  90.0 1.4 collective-permute-start.2
  91.3 2.1 collective-permute-start.1
  93.4 1.5 collective-permute-start.3
  94.8 3.7 collective-permute-start.5
  100.4 2.6 fusion.27
  103.5 21.4 %attention.1 = (bf16[1024,2048]{1,0:T(8,128)(2,1)}, f32[1024,1024]{1,0:T(8,128)}, bf16[1024,512]{1,0:T(8,128)(2,1)S(1)}, bf16[1024,256]{1,0:T(8,128)(2,1)S(1)}, ...) custom-call(bf16[1024,2048]{1,0:T(8,128)(2,1)} %get-tuple-element.134.tokens, bf16[2048,1024]{1,0:T(8,128)(2,1)} %bitcast.67, ...), custom_call_target="tpu_custom_call" | custom-call | flops 1000000 | bytes 100000 | tf_op jit(solution)/shard_map/attention/pallas_call | solution.py:1277
  127.8 1.3 constant_dynamic-slice_fusion.10
  130.4 4.4 convolution_convert_fusion.2.terms
  134.8 135.9 %hidden_rows.1 = (bf16[1024,2048]{1,0:T(8,128)(2,1)}, f32[256,2048]{1,0:T(8,128)}, bf16[8,256,3072]{2,1,0:T(8,128)(2,1)}, bf16[8,256,1536]{2,1,0:T(8,128)(2,1)}) custom-call(bf16[1024,2048]{1,0:T(8,128)(2,1)} %convolution_convert_fusion.2.terms, bf16[256,2048]{1,0:T(8,128)(2,1)} %pad_maximum_fusion.1.refs_0_, f32[1,2048]{1,0:T(1,128)} %bitcast.75, ...), custom_call_target="tpu_custom_call" | custom-call | flops 1000000 | bytes 100000 | tf_op jit(solution)/shard_map/hidden_rows/pallas_call | solution.py:936
  270.8 33.8 %feed_forward.1 = (bf16[1024,1536]{1,0:T(8,128)(2,1)}, bf16[1024,3072]{1,0:T(8,128)(2,1)}, bf16[1024,2048]{1,0:T(8,128)(2,1)}) custom-call(bf16[1024,2048]{1,0:T(8,128)(2,1)} %get-tuple-element.181.rows, bf16[1024,2048]{1,0:T(8,128)(2,1)} %own_grad, bf16[1024,2048]{1,0:T(8,128)(2,1)} %collective-permute-done.5.got_grad, bf16[2048,3072]{1,0:T(8,128)(2,1)} %bitcast.78, ...), custom_call_target="tpu_custom_call" | custom-call | flops 19327352832 | bytes 40000000 | tf_op jit(solution)/shard_map/feed_forward/pallas_call | solution.py:1420
  304.6 6.1 convolution_convert_fusion.3
  311.0 8.9 %convolution_convert_fusion = bf16[1024,3072]{1,0:T(8,128)(2,1)} fusion(bf16[1024,3072]{1,0:T(8,128)(2,1)S(1)} %copy-done.43, bf16[1024,2048]{1,0:T(8,128)(2,1)S(1)} %copy-done.40), kind=kOutput, calls=%fused_computation.2 | convolution fusion | flops 6445596672 | bytes 14680064 | tf_op jit(solution)/shard_map/dot_general | solution.py:55
  319.9 4.9 add_convert_fusion.1
  325.2 1.4 fusion.38
  327.8 1.6 collective-permute-start.8
  329.4 19.6 %convolution_convert_fusion.1.terms = bf16[1024,2048]{1,0:T(8,128)(2,1)} fusion(bf16[1024,3072]{1,0:T(8,128)(2,1)} %get-tuple-element.182, bf16[2048,3072]{1,0:T(8,128)(2,1)} %bitcast.80), kind=kOutput, calls=%fused_computation.8 | convolution fusion | flops 12886999040 | bytes 23068672 | tf_op jit(solution)/shard_map/dot_general | solution.py:61
  349.0 1.6 collective-permute-start.9
  350.7 12.5 %add_convert_fusion = bf16[1024,3072]{1,0:T(8,128)(2,1)} fusion(bf16[1024,3072]{1,0:T(8,128)(2,1)} %collective-permute-done.7, bf16[1024,3072]{1,0:T(8,128)(2,1)} %get-tuple-element.182, bf16[1024,2048]{1,0:T(8,128)(2,1)S(1)} %copy-done.41), kind=kOutput, calls=%fused_computation | convolution fusion | flops 6451888128 | bytes 20971520 | tf_op jit(solution)/shard_map/dot_general | solution.py:55
  363.1 3.7 collective-permute-done.9
  366.8 86.1 %grad_hidden_rows.1 = (bf16[1024,2048]{1,0:T(8,128)(2,1)}, f32[256,2048]{1,0:T(8,128)}, f32[1,2048]{1,0:T(1,128)}, bf16[1024,2048]{1,0:T(8,128)(2,1)}, bf16[2,256,3072]{2,1,0:T(8,128)(2,1)}) custom-call(bf16[1024,2048]{1,0:T(8,128)(2,1)} %convolution_convert_fusion.1.terms, f32[256,2048]{1,0:T(8,128)} %get-tuple-element.187.refs_0_, ...), custom_call_target="tpu_custom_call" | custom-call | flops 1000000 | bytes 100000 | tf_op jit(solution)/shard_map/grad_hidden_rows/pallas_call | solution.py:936
  452.9 5.3 convolution_convert_fusion.5.grad_rows
  459.5 19.3 %collective-permute-start.10 = (bf16[256,3072]{1,0:T(8,128)(2,1)}, bf16[256,3072]{1,0:T(8,128)(2,1)}, u32[]{:S(2)}, u32[]{:S(2)}) collective-permute-start(bf16[256,3072]{1,0:T(8,128)(2,1)} %slice_bitcast_fusion), channel_id=1, source_target_pairs={{0,8},{1,9},{2,10},{3,11},{4,12},{5,13},{6,14},{7,15},{8,0},{9,1},... | collective-permute-start | bytes 4718600 | tf_op jit(solution)/shard_map/ppermute | solution.py:1472
  478.9 1.5 add_convert_fusion.3
  480.4 2.0 collective-permute-start.13
  482.3 1.6 fusion.37
  484.2 1.6 collective-permute-start.11
  485.9 23.2 %attention_back.1 = (bf16[1024,1024]{1,0:T(8,128)(2,1)}, bf16[1024,1024]{1,0:T(8,128)(2,1)}, f32[1,128]{1,0:T(1,128)S(1)}, f32[1,128]{1,0:T(1,128)S(1)}) custom-call(bf16[1024,512]{1,0:T(8,128)(2,1)S(1)} %get-tuple-element.138.query, bf16[1024,256]{1,0:T(8,128)(2,1)S(1)} %get-tuple-element.139.key, bf16[1024,256]{1,0:T(8,128)(2,1)S(1)} %get-tuple-element.140.value, ...), custom_call_target="tpu_custom_call" | custom-call | flops 1000000 | bytes 100000 | tf_op jit(solution)/shard_map/attention_back/pallas_call | solution.py:1348
  509.8 2.1 slice_add_fusion.1
  512.3 1.9 add_convert_fusion.2
  514.3 2.6 collective-permute-start.15
  517.0 6.2 convolution_convert_fusion.4.terms
  523.2 2.1 fusion.2
  526.0 2.0 collective-permute-start.16
  529.3 8.2 %collective-permute-start.14 = (bf16[1024,512]{1,0:T(8,128)(2,1)S(1)}, bf16[1024,512]{1,0:T(8,128)(2,1)S(1)}, u32[]{:S(2)}, u32[]{:S(2)}) collective-permute-start(bf16[1024,512]{1,0:T(8,128)(2,1)S(1)} %fusion.19), channel_id=1, source_target_pairs={{0,1},{1,0},{2,3},{3,2},{4,5},{5,4},{6,7},{7,6},{8,9},{9,8},{10,11... | collective-permute-start | bytes 3145736 | tf_op jit(solution)/shard_map/ppermute | solution.py:1472
  538.8 1.5 fusion.4.refs_3_
  541.4 2.3 add_convert_fusion.4
  543.6 101.3 %grad_input_rows.1 = (bf16[1024,2048]{1,0:T(8,128)(2,1)}, f32[1,2048]{1,0:T(1,128)}, f32[1,4352]{1,0:T(1,128)}, bf16[256,1024]{1,0:T(8,128)(2,1)}, bf16[3,256,51...) custom-call(bf16[1024,2048]{1,0:T(8,128)(2,1)} %convolution_convert_fusion.4.terms, ...), custom_call_target="tpu_custom_call" | custom-call | flops 1000000 | bytes 100000 | tf_op jit(solution)/shard_map/grad_input_rows/pallas_call | solution.py:936
  645.0 1.4 fusion.26
  647.7 4.8 collective-permute-start.19
  654.0 1.6 broadcast_select_fusion.1
  655.7 5.0 multiply_subtract_fusion
  660.8 3.1 multiply_subtract_fusion.1
  665.2 2.8 reshape.107
  667.9 2.8 multiply_subtract_fusion.3
  670.7 3.2 multiply_subtract_fusion.2
  673.9 6.8 %select_convert_fusion = (f32[1024,2048]{1,0:T(8,128)}, bf16[1024,2048]{1,0:T(8,128)(2,1)}) fusion(bf16[1024,2048]{1,0:T(8,128)(2,1)S(1)} %copy-done.13, bf16[1024,2048]{1,0:T(8,128)(2,1)} %collective-permute-done.18, pred[]{:T(512)S(6)} %eq.9), kind=kLoop, calls=%fused_computation.6 | loop fusion | flops 6291456 | bytes 20971520 | tf_op jit(solution)/shard_map/convert_element_type | solution.py:1881
  (180 shorter events, 21.5 us)
Async XLA Ops:
  90.0 35.2 %collective-permute-start.2 = (bf16[256,512]{1,0:T(8,128)(2,1)}, bf16[256,512]{1,0:T(8,128)(2,1)S(1)}, u32[]{:S(2)}, u32[]{:S(2)}) collective-permute-start(bf16[256,512]{1,0:T(8,128)(2,1)} %get-tuple-element.148), channel_id=1, source_target_pairs={{0,16},{1,17},{2,18},{3,19},{4,20},{5,21},{6,22},{7,23},{8,24},{9,... | collective-permute-start | bytes 786440 | tf_op jit(solution)/shard_map/ppermute | solution.py:1472
  91.3 33.9 %collective-permute-start.1 = (bf16[256,512]{1,0:T(8,128)(2,1)}, bf16[256,512]{1,0:T(8,128)(2,1)}, u32[]{:S(2)}, u32[]{:S(2)}) collective-permute-start(bf16[256,512]{1,0:T(8,128)(2,1)} %get-tuple-element.148), channel_id=1, source_target_pairs={{0,24},{1,25},{2,26},{3,27},{4,28},{5,29},{6,30},{7,31},{8,16},{9,... | collective-permute-start | bytes 786440 | tf_op jit(solution)/shard_map/ppermute | solution.py:1472
  93.4 31.8 %collective-permute-start = (bf16[256,512]{1,0:T(8,128)(2,1)}, bf16[256,512]{1,0:T(8,128)(2,1)}, u32[]{:S(2)}, u32[]{:S(2)}) collective-permute-start(bf16[256,512]{1,0:T(8,128)(2,1)} %get-tuple-element.148), channel_id=1, source_target_pairs={{0,8},{1,9},{2,10},{3,11},{4,12},{5,13},{6,14},{7,15},{8,0},{9,1},... | collective-permute-start | bytes 786440 | tf_op jit(solution)/shard_map/ppermute | solution.py:1472
  93.4 31.8 %collective-permute-start.3 = (bf16[256,1536]{1,0:T(8,128)(2,1)}, bf16[256,1536]{1,0:T(8,128)(2,1)}, u32[]{:S(2)}, u32[]{:S(2)}) collective-permute-start(bf16[256,1536]{1,0:T(8,128)(2,1)} %get-tuple-element.157.refs_4_), channel_id=1, source_target_pairs={{0,8},{1,9},{2,10},{3,11},{4,12},{5,13},{6,14},{7,15},{8,0},{9,1},... | collective-permute-start | bytes 2359304 | tf_op jit(solution)/shard_map/ppermute | solution.py:1472
  94.8 175.9 %collective-permute-start.5 = (bf16[1024,2048]{1,0:T(8,128)(2,1)}, bf16[1024,2048]{1,0:T(8,128)(2,1)}, u32[]{:S(2)}, u32[]{:S(2)}) collective-permute-start(bf16[1024,2048]{1,0:T(8,128)(2,1)} %own_grad), channel_id=1, source_target_pairs={{1,4},{3,6},{4,1},{6,3},{9,12},{11,14},{12,9},{14,11},{17,20},{19,... | collective-permute-start | bytes 12582920 | tf_op jit(solution)/shard_map/ppermute | solution.py:1472
  103.5 21.5 %copy-start = (f32[2048]{0:T(1024)}, f32[2048]{0:T(1024)S(1)}, u32[]{:S(2)}) copy-start(f32[2048]{0:T(1024)S(1)} %constant_dynamic-update-slice_fusion.26) | copy-start | bytes 24580
  103.5 21.6 %copy-start.32 = (bf16[256,512]{1,0:T(8,128)(2,1)S(1)}, bf16[256,512]{1,0:T(8,128)(2,1)}, u32[]{:S(2)}) copy-start(bf16[256,512]{1,0:T(8,128)(2,1)} %get-tuple-element.148) | copy-start | bytes 786436
  125.0 5.4 copy-start.1
  127.3 2.9 collective-permute-start.4
  304.6 6.4 copy-start.40
  304.6 6.4 copy-start.43
  310.7 9.2 %copy-start.18 = (bf16[1024,1536]{1,0:T(8,128)(2,1)S(1)}, bf16[1024,1536]{1,0:T(8,128)(2,1)}, u32[]{:S(2)}) copy-start(bf16[1024,1536]{1,0:T(8,128)(2,1)} %get-tuple-element.174.refs_3_) | copy-start | bytes 9437188
  310.8 9.2 %copy-start.31 = (bf16[1024,2048]{1,0:T(8,128)(2,1)S(1)}, bf16[1024,2048]{1,0:T(8,128)(2,1)}, u32[]{:S(2)}) copy-start(bf16[1024,2048]{1,0:T(8,128)(2,1)} %get-tuple-element.173) | copy-start | bytes 12582916
  310.8 9.1 %collective-permute-start.6 = (bf16[1024,1536]{1,0:T(8,128)(2,1)S(1)}, bf16[1024,1536]{1,0:T(8,128)(2,1)S(1)}, u32[]{:S(2)}, u32[]{:S(2)}) collective-permute-start(bf16[1024,1536]{1,0:T(8,128)(2,1)S(1)} %convolution_convert_fusion.3), channel_id=1, source_target_pairs={{0,1},{1,0},{2,3},{3,2},{4,5},{5,4},{6,7},{7,6},{8,9},{9,8},{10,11... | collective-permute-start | bytes 9437192 | tf_op jit(solution)/shard_map/ppermute | solution.py:1472
  324.8 24.1 %collective-permute-start.7 = (bf16[1024,3072]{1,0:T(8,128)(2,1)}, bf16[1024,3072]{1,0:T(8,128)(2,1)}, u32[]{:S(2)}, u32[]{:S(2)}) collective-permute-start(bf16[1024,3072]{1,0:T(8,128)(2,1)} %convolution_convert_fusion), channel_id=1, source_target_pairs={{0,1},{1,0},{2,3},{3,2},{4,5},{5,4},{6,7},{7,6},{8,9},{9,8},{10,11... | collective-permute-start | bytes 18874376 | tf_op jit(solution)/shard_map/ppermute | solution.py:1472
  327.8 22.9 %copy-start.41 = (bf16[1024,2048]{1,0:T(8,128)(2,1)S(1)}, bf16[1024,2048]{1,0:T(8,128)(2,1)}, u32[]{:S(2)}) copy-start(bf16[1024,2048]{1,0:T(8,128)(2,1)} %get-tuple-element.181.rows) | copy-start | bytes 12582916
  327.8 21.2 %collective-permute-start.8 = (bf16[256,1536]{1,0:T(8,128)(2,1)S(1)}, bf16[256,1536]{1,0:T(8,128)(2,1)S(1)}, u32[]{:S(2)}, u32[]{:S(2)}) collective-permute-start(bf16[256,1536]{1,0:T(8,128)(2,1)S(1)} %slice_bitcast_fusion.4), channel_id=1, source_target_pairs={{0,8},{1,9},{2,10},{3,11},{4,12},{5,13},{6,14},{7,15},{24,16},{25,... | collective-permute-start | bytes 2359304 | tf_op jit(solution)/shard_map/ppermute | solution.py:1472
  349.0 14.2 %copy-start.25 = (bf16[256,1536]{1,0:T(8,128)(2,1)}, bf16[256,1536]{1,0:T(8,128)(2,1)S(1)}, u32[]{:S(2)}) copy-start(bf16[256,1536]{1,0:T(8,128)(2,1)S(1)} %collective-permute-done.8) | copy-start | bytes 2359300
  349.0 17.8 %collective-permute-start.9 = (bf16[256,1536]{1,0:T(8,128)(2,1)S(1)}, bf16[256,1536]{1,0:T(8,128)(2,1)S(1)}, u32[]{:S(2)}, u32[]{:S(2)}) collective-permute-start(bf16[256,1536]{1,0:T(8,128)(2,1)S(1)} %slice_bitcast_fusion.3), channel_id=1, source_target_pairs={{0,8},{1,9},{2,10},{3,11},{4,12},{5,13},{6,14},{7,15},{24,16},{25,... | collective-permute-start | bytes 2359304 | tf_op jit(solution)/shard_map/ppermute | solution.py:1472
  366.8 86.1 %copy-start.27 = (bf16[256,1536]{1,0:T(8,128)(2,1)}, bf16[256,1536]{1,0:T(8,128)(2,1)S(1)}, u32[]{:S(2)}) copy-start(bf16[256,1536]{1,0:T(8,128)(2,1)S(1)} %collective-permute-done.9) | copy-start | bytes 2359300
  452.9 5.3 copy-start.16
  458.3 20.6 %copy-start.26 = (bf16[256,1536]{1,0:T(8,128)(2,1)S(1)}, bf16[256,1536]{1,0:T(8,128)(2,1)}, u32[]{:S(2)}) copy-start(bf16[256,1536]{1,0:T(8,128)(2,1)} %copy-done.25) | copy-start | bytes 2359300
  458.3 20.6 %copy-start.28 = (bf16[256,1536]{1,0:T(8,128)(2,1)S(1)}, bf16[256,1536]{1,0:T(8,128)(2,1)}, u32[]{:S(2)}) copy-start(bf16[256,1536]{1,0:T(8,128)(2,1)} %copy-done.27) | copy-start | bytes 2359300
  459.5 22.8 %copy-start.9 = (bf16[1024,2048]{1,0:T(8,128)(2,1)S(1)}, bf16[1024,2048]{1,0:T(8,128)(2,1)}, u32[]{:S(2)}) copy-start(bf16[1024,2048]{1,0:T(8,128)(2,1)} %get-tuple-element.205) | copy-start | bytes 12582916
  459.5 50.3 %collective-permute-start.10 = (bf16[256,3072]{1,0:T(8,128)(2,1)}, bf16[256,3072]{1,0:T(8,128)(2,1)}, u32[]{:S(2)}, u32[]{:S(2)}) collective-permute-start(bf16[256,3072]{1,0:T(8,128)(2,1)} %slice_bitcast_fusion), channel_id=1, source_target_pairs={{0,8},{1,9},{2,10},{3,11},{4,12},{5,13},{6,14},{7,15},{8,0},{9,1},... | collective-permute-start | bytes 4718600 | tf_op jit(solution)/shard_map/ppermute | solution.py:1472
  480.4 5.5 copy-start.36
  480.4 29.4 %collective-permute-start.13 = (bf16[2,256,1536]{2,1,0:T(8,128)(2,1)}, bf16[2,256,1536]{2,1,0:T(8,128)(2,1)}, u32[]{:S(2)}, u32[]{:S(2)}) collective-permute-start(bf16[2,256,1536]{2,1,0:T(8,128)(2,1)} %add_convert_fusion.3), channel_id=1, source_target_pairs={{8,16},{9,17},{10,18},{11,19},{12,20},{13,21},{14,22},{15,23},{16,... | collective-permute-start | bytes 4718600 | tf_op jit(solution)/shard_map/ppermute | solution.py:1472
  483.9 25.9 %collective-permute-start.12 = (bf16[256,2048]{1,0:T(8,128)(2,1)}, bf16[256,2048]{1,0:T(8,128)(2,1)}, u32[]{:S(2)}, u32[]{:S(2)}) collective-permute-start(bf16[256,2048]{1,0:T(8,128)(2,1)} %get-tuple-element.256), channel_id=1, source_target_pairs={{0,4},{1,5},{2,6},{3,7},{4,0},{5,1},{6,2},{7,3},{8,12},{9,13},{10,... | collective-permute-start | bytes 3145736 | tf_op jit(solution)/shard_map/ppermute | solution.py:1472
  484.2 25.6 %collective-permute-start.11 = (bf16[256,2048]{1,0:T(8,128)(2,1)}, bf16[256,2048]{1,0:T(8,128)(2,1)}, u32[]{:S(2)}, u32[]{:S(2)}) collective-permute-start(bf16[256,2048]{1,0:T(8,128)(2,1)} %get-tuple-element.257), channel_id=1, source_target_pairs={{0,2},{1,3},{2,0},{3,1},{4,6},{5,7},{6,4},{7,5},{8,10},{9,11},{10,... | collective-permute-start | bytes 3145736 | tf_op jit(solution)/shard_map/ppermute | solution.py:1472
  514.3 8.9 %copy-start.17 = (bf16[2,256,3072]{2,1,0:T(8,128)(2,1)S(1)}, bf16[2,256,3072]{2,1,0:T(8,128)(2,1)}, u32[]{:S(2)}) copy-start(bf16[2,256,3072]{2,1,0:T(8,128)(2,1)} %get-tuple-element.204) | copy-start | bytes 9437188
  514.3 26.0 %collective-permute-start.15 = (bf16[256,1536]{1,0:T(8,128)(2,1)S(1)}, bf16[256,1536]{1,0:T(8,128)(2,1)S(1)}, u32[]{:S(2)}, u32[]{:S(2)}) collective-permute-start(bf16[256,1536]{1,0:T(8,128)(2,1)S(1)} %slice_bitcast_fusion.1), channel_id=1, source_target_pairs={{0,8},{1,9},{2,10},{3,11},{4,12},{5,13},{6,14},{7,15},{8,0},{9,1},... | collective-permute-start | bytes 2359304 | tf_op jit(solution)/shard_map/ppermute | solution.py:1472
  525.5 13.2 %collective-permute-start.17 = (bf16[128,2048]{1,0:T(8,128)(2,1)S(1)}, bf16[128,2048]{1,0:T(8,128)(2,1)S(1)}, u32[]{:S(2)}, u32[]{:S(2)}) collective-permute-start(bf16[128,2048]{1,0:T(8,128)(2,1)S(1)} %slice.200), channel_id=1, source_target_pairs={{0,2},{1,3},{2,0},{3,1},{4,6},{5,7},{6,4},{7,5},{8,10},{9,11},{10,... | collective-permute-start | bytes 1572872 | tf_op jit(solution)/shard_map/ppermute | solution.py:1472
  526.0 12.7 %collective-permute-start.16 = (bf16[128,2048]{1,0:T(8,128)(2,1)S(1)}, bf16[128,2048]{1,0:T(8,128)(2,1)S(1)}, u32[]{:S(2)}, u32[]{:S(2)}) collective-permute-start(bf16[128,2048]{1,0:T(8,128)(2,1)S(1)} %slice.201), channel_id=1, source_target_pairs={{0,4},{1,5},{2,6},{3,7},{4,0},{5,1},{6,2},{7,3},{8,12},{9,13},{10,... | collective-permute-start | bytes 1572872 | tf_op jit(solution)/shard_map/ppermute | solution.py:1472
  529.3 9.5 %copy-start.5 = (f32[256,2048]{1,0:T(8,128)S(1)}, f32[256,2048]{1,0:T(8,128)}, u32[]{:S(2)}) copy-start(f32[256,2048]{1,0:T(8,128)} %get-tuple-element.187.refs_0_) | copy-start | bytes 6291460
  529.3 12.0 %collective-permute-start.14 = (bf16[1024,512]{1,0:T(8,128)(2,1)S(1)}, bf16[1024,512]{1,0:T(8,128)(2,1)S(1)}, u32[]{:S(2)}, u32[]{:S(2)}) collective-permute-start(bf16[1024,512]{1,0:T(8,128)(2,1)S(1)} %fusion.19), channel_id=1, source_target_pairs={{0,1},{1,0},{2,3},{3,2},{4,5},{5,4},{6,7},{7,6},{8,9},{9,8},{10,11... | collective-permute-start | bytes 3145736 | tf_op jit(solution)/shard_map/ppermute | solution.py:1472
  543.6 109.7 %copy-start.34 = (f32[544]{0:T(1024)S(1)}, f32[544]{0:T(1024)}, u32[]{:S(2)}) copy-start(f32[544]{0:T(1024)} %param.33) | copy-start | bytes 6532
  543.6 109.7 %copy-start.37 = (f32[544]{0:T(1024)S(1)}, f32[544]{0:T(1024)}, u32[]{:S(2)}) copy-start(f32[544]{0:T(1024)} %param.35) | copy-start | bytes 6532
  543.6 109.7 %copy-start.38 = (f32[544]{0:T(1024)S(1)}, f32[544]{0:T(1024)}, u32[]{:S(2)}) copy-start(f32[544]{0:T(1024)} %param.34) | copy-start | bytes 6532
  543.6 112.0 %copy-start.14 = (f32[2,256,1536]{2,1,0:T(8,128)S(1)}, f32[2,256,1536]{2,1,0:T(8,128)}, u32[]{:S(2)}) copy-start(f32[2,256,1536]{2,1,0:T(8,128)} %param.29) | copy-start | bytes 9437188
  543.6 112.0 %copy-start.15 = (f32[2,256,1536]{2,1,0:T(8,128)S(1)}, f32[2,256,1536]{2,1,0:T(8,128)}, u32[]{:S(2)}) copy-start(f32[2,256,1536]{2,1,0:T(8,128)} %param.28) | copy-start | bytes 9437188
  644.9 9.0 %copy-start.3 = (bf16[512,1536]{1,0:T(8,128)(2,1)S(1)}, bf16[512,1536]{1,0:T(8,128)(2,1)}, u32[]{:S(2)}) copy-start(bf16[512,1536]{1,0:T(8,128)(2,1)} %pad_maximum_fusion.refs_8_) | copy-start | bytes 4718596
  646.4 9.2 %copy-start.4 = (f32[2,256,1536]{2,1,0:T(8,128)S(1)}, f32[2,256,1536]{2,1,0:T(8,128)}, u32[]{:S(2)}) copy-start(f32[2,256,1536]{2,1,0:T(8,128)} %wide_gate.1) | copy-start | bytes 9437188
  647.7 16.2 %collective-permute-start.19 = (bf16[256,1536]{1,0:T(8,128)(2,1)S(1)}, bf16[256,1536]{1,0:T(8,128)(2,1)S(1)}, u32[]{:S(2)}, u32[]{:S(2)}) collective-permute-start(bf16[256,1536]{1,0:T(8,128)(2,1)S(1)} %pad_maximum_fusion.3), channel_id=1, source_target_pairs={{1,4},{3,6},{4,1},{6,3},{9,12},{11,14},{12,9},{14,11},{17,20},{19,... | collective-permute-start | bytes 2359304 | tf_op jit(solution)/shard_map/ppermute | solution.py:1472
  652.5 21.4 %collective-permute-start.18 = (bf16[1024,2048]{1,0:T(8,128)(2,1)}, bf16[1024,2048]{1,0:T(8,128)(2,1)}, u32[]{:S(2)}, u32[]{:S(2)}) collective-permute-start(bf16[1024,2048]{1,0:T(8,128)(2,1)} %get-tuple-element.231), channel_id=1, source_target_pairs={{0,1},{1,0},{2,3},{3,2},{4,5},{5,4},{6,7},{7,6},{8,9},{9,8},{10,11... | collective-permute-start | bytes 12582920 | tf_op jit(solution)/shard_map/ppermute | solution.py:1472
  655.6 5.1 copy-start.7
  655.6 5.1 copy-start.8
  655.7 5.1 copy-start.29
  665.1 5.5 copy-start.10
  (16 other events, 57.8 us)

commit v5 on v4

--- a/solution.py
+++ b/solution.py
@@ -1778,7 +1778,7 @@
 
     eighth = tok_rows // 8
     own_grad = jnp.concatenate([out_grad[:eighth], out_grad[2 * eighth : 3 * eighth]], 0)
-    branch_rows, grad_hidden, post_gain_grad, mlp_terms, gate_sums = sum_rows(
+    branch_rows, grad_hidden, post_gain_grad, gate_sums, mlp_terms = sum_rows(
         plan,
         spread_kernel,
         grad_hidden_rows,
@@ -1790,8 +1790,8 @@
         ],
         1,
         [
+            PairScatter(gate_parts) if tree else ZoneBlocks(plan, gate_parts, slots),
             SideDot(active, full_down),
-            PairScatter(gate_parts) if tree else ZoneBlocks(plan, gate_parts, slots),
         ],
     )
     branch_rows, grad_hidden, post_gain_grad, gate_sums, mlp_terms, down_parts, down_sums = fence(
@@ -1845,17 +1845,17 @@
         [jax.ShapeDtypeStruct((1, model_width), jnp.float32)],
         2,
         [
+            ZoneBlocks(plan, out_parts, slots),
             BlockGrad(plan, normed, grad_mixed),
-            ZoneBlocks(plan, out_parts, slots),
             TurnLate(total_gate),
             TurnLate(total_down),
         ],
         gain_sum,
     )
     if plan.ordered:
-        summed_gains, total_qkv, out_sent, got_gate, got_down = rest
+        summed_gains, out_sent, total_qkv, got_gate, got_down = rest
     else:
-        total_qkv, out_sent, got_gate, got_down = rest
+        out_sent, total_qkv, got_gate, got_down = rest
         summed_gains = plan.sum_everywhere(
             jnp.concatenate([plan.to_natural(input_gain_grad, 1), gain_terms], 1)
         )

time: 685 us -> 685 us (level)
  no operation moved by 1% of the time
where the time goes in v5:
time: 685 us; the launch traced here: 681 us
  Pallas kernels  486 us (71%)
  matrix products  71.5 us (10%)
  starting transfers between devices  53.9 us (8%)
  other arithmetic  45.2 us (7%)
  local copies, waits for them, and re-layouts  18.9 us (3%)
    pallas_call x3, Pallas kernels, sum_rows(): pl.pallas_call(functools.partial(kernel, middle, jobs, len(extras), len(o...  323 us
    pallas_call x1, Pallas kernels, opening(): pl.pallas_call(functools.partial(opening_kernel, plan), out_shape=outputs...  84.1 us
    ppermute x20, starting transfers between devices, move(): return lax.ppermute(value, ('dp', 'tensor'), pairs)  53.9 us
    dot_general x6, matrix products, contract_rows(): lax.dot_general(left, right, (((0,), (0,)), ((), ())), preferred_element_...  36 us
    pallas_call x1, Pallas kernels, feed_forward(): pl.pallas_call(functools.partial(feed_kernel, plan), grid=(tiles,), out_s...  33.8 us
    dot_general x3, matrix products, contract_cols(): lax.dot_general(left, right, (((1,), (1,)), ((), ())), preferred_element_...  30.2 us
    pallas_call x1, Pallas kernels, attention_back(): pl.pallas_call(backward_kernel, out_shape=[jax.ShapeDtypeStruct((total, c...  23.2 us
    pallas_call x1, Pallas kernels, attention(): pl.pallas_call(forward_kernel, out_shape=[shape(tokens.shape[1]), shape(c...  21.4 us
  transfers between devices with their start and end apart: 20, of which 1 were waited for; matrix products, arithmetic and copies ran while one was open for 14% of the time, Pallas kernels for 27%

profile of v5, /device:TPU:1, one launch (start us, length us, event | category | flops | bytes accessed | tf_op | source)
XLA Modules:
  0.0 680.9 jit_solution(12821866526478634641)
XLA Ops:
  3.2 2.6 reshape.95.wide_qkv
  5.8 84.1 %opening.1 = (bf16[8,256,1024]{2,1,0:T(8,128)(2,1)}, bf16[8,16,128]{2,1,0:T(8,128)(2,1)}, bf16[256,3072]{1,0:T(8,128)(2,1)}, bf16[256,512]{1,0:T(8,128)(2,1)}, b...) custom-call(f32[256,1024]{1,0:T(8,128)} %reshape.95.wide_qkv, ...), custom_call_target="tpu_custom_call" | custom-call | flops 1000000 | bytes 100000 | tf_op jit(solution)/shard_map/opening/pallas_call | solution.py:1122
  90.0 1.4 collective-permute-start.2
  91.3 2.1 collective-permute-start.1
  93.4 1.5 collective-permute-start.3
  94.8 3.7 collective-permute-start.5
  100.4 2.6 fusion.27
  103.5 21.4 %attention.1 = (bf16[1024,2048]{1,0:T(8,128)(2,1)}, f32[1024,1024]{1,0:T(8,128)}, bf16[1024,512]{1,0:T(8,128)(2,1)S(1)}, bf16[1024,256]{1,0:T(8,128)(2,1)S(1)}, ...) custom-call(bf16[1024,2048]{1,0:T(8,128)(2,1)} %get-tuple-element.134.tokens, bf16[2048,1024]{1,0:T(8,128)(2,1)} %bitcast.67, ...), custom_call_target="tpu_custom_call" | custom-call | flops 1000000 | bytes 100000 | tf_op jit(solution)/shard_map/attention/pallas_call | solution.py:1277
  127.8 1.3 constant_dynamic-slice_fusion.10
  130.4 4.4 convolution_convert_fusion.2.terms
  134.8 135.9 %hidden_rows.1 = (bf16[1024,2048]{1,0:T(8,128)(2,1)}, f32[256,2048]{1,0:T(8,128)}, bf16[8,256,3072]{2,1,0:T(8,128)(2,1)}, bf16[8,256,1536]{2,1,0:T(8,128)(2,1)}) custom-call(bf16[1024,2048]{1,0:T(8,128)(2,1)} %convolution_convert_fusion.2.terms, bf16[256,2048]{1,0:T(8,128)(2,1)} %pad_maximum_fusion.1.refs_0_, f32[1,2048]{1,0:T(1,128)} %bitcast.75, ...), custom_call_target="tpu_custom_call" | custom-call | flops 1000000 | bytes 100000 | tf_op jit(solution)/shard_map/hidden_rows/pallas_call | solution.py:936
  270.8 33.8 %feed_forward.1 = (bf16[1024,1536]{1,0:T(8,128)(2,1)}, bf16[1024,3072]{1,0:T(8,128)(2,1)}, bf16[1024,2048]{1,0:T(8,128)(2,1)}) custom-call(bf16[1024,2048]{1,0:T(8,128)(2,1)} %get-tuple-element.181.rows, bf16[1024,2048]{1,0:T(8,128)(2,1)} %own_grad, bf16[1024,2048]{1,0:T(8,128)(2,1)} %collective-permute-done.5.got_grad, bf16[2048,3072]{1,0:T(8,128)(2,1)} %bitcast.78, ...), custom_call_target="tpu_custom_call" | custom-call | flops 19327352832 | bytes 40000000 | tf_op jit(solution)/shard_map/feed_forward/pallas_call | solution.py:1420
  304.6 6.1 convolution_convert_fusion.3
  311.0 8.9 %convolution_convert_fusion = bf16[1024,3072]{1,0:T(8,128)(2,1)} fusion(bf16[1024,3072]{1,0:T(8,128)(2,1)S(1)} %copy-done.43, bf16[1024,2048]{1,0:T(8,128)(2,1)S(1)} %copy-done.40), kind=kOutput, calls=%fused_computation.2 | convolution fusion | flops 6445596672 | bytes 14680064 | tf_op jit(solution)/shard_map/dot_general | solution.py:55
  319.9 4.9 add_convert_fusion.1
  325.2 1.4 fusion.38
  327.8 1.6 collective-permute-start.8
  329.4 19.6 %convolution_convert_fusion.1.terms = bf16[1024,2048]{1,0:T(8,128)(2,1)} fusion(bf16[1024,3072]{1,0:T(8,128)(2,1)} %get-tuple-element.182, bf16[2048,3072]{1,0:T(8,128)(2,1)} %bitcast.80), kind=kOutput, calls=%fused_computation.8 | convolution fusion | flops 12886999040 | bytes 23068672 | tf_op jit(solution)/shard_map/dot_general | solution.py:61
  349.0 1.6 collective-permute-start.9
  350.7 12.5 %add_convert_fusion = bf16[1024,3072]{1,0:T(8,128)(2,1)} fusion(bf16[1024,3072]{1,0:T(8,128)(2,1)} %collective-permute-done.7, bf16[1024,3072]{1,0:T(8,128)(2,1)} %get-tuple-element.182, bf16[1024,2048]{1,0:T(8,128)(2,1)S(1)} %copy-done.41), kind=kOutput, calls=%fused_computation | convolution fusion | flops 6451888128 | bytes 20971520 | tf_op jit(solution)/shard_map/dot_general | solution.py:55
  363.1 3.7 collective-permute-done.9
  366.8 85.9 %grad_hidden_rows.1 = (bf16[1024,2048]{1,0:T(8,128)(2,1)}, f32[256,2048]{1,0:T(8,128)}, f32[1,2048]{1,0:T(1,128)}, bf16[2,256,3072]{2,1,0:T(8,128)(2,1)}, bf16[1024,2048]{1,0:T(8,128)(2,1)}) custom-call(bf16[1024,2048]{1,0:T(8,128)(2,1)} %convolution_convert_fusion.1.terms, f32[256,2048]{1,0:T(8,128)} %get-tuple-element.187.refs_0_, ...), custom_call_target="tpu_custom_call" | custom-call | flops 1000000 | bytes 100000 | tf_op jit(solution)/shard_map/grad_hidden_rows/pallas_call | solution.py:936
  452.8 5.3 convolution_convert_fusion.5.grad_rows
  459.4 19.3 %collective-permute-start.10 = (bf16[256,3072]{1,0:T(8,128)(2,1)}, bf16[256,3072]{1,0:T(8,128)(2,1)}, u32[]{:S(2)}, u32[]{:S(2)}) collective-permute-start(bf16[256,3072]{1,0:T(8,128)(2,1)} %slice_bitcast_fusion), channel_id=1, source_target_pairs={{0,8},{1,9},{2,10},{3,11},{4,12},{5,13},{6,14},{7,15},{8,0},{9,1},... | collective-permute-start | bytes 4718600 | tf_op jit(solution)/shard_map/ppermute | solution.py:1472
  478.7 1.5 add_convert_fusion.3
  480.2 2.0 collective-permute-start.13
  482.2 1.6 fusion.37
  484.1 1.7 collective-permute-start.11
  485.7 23.2 %attention_back.1 = (bf16[1024,1024]{1,0:T(8,128)(2,1)}, bf16[1024,1024]{1,0:T(8,128)(2,1)}, f32[1,128]{1,0:T(1,128)S(1)}, f32[1,128]{1,0:T(1,128)S(1)}) custom-call(bf16[1024,512]{1,0:T(8,128)(2,1)S(1)} %get-tuple-element.138.query, bf16[1024,256]{1,0:T(8,128)(2,1)S(1)} %get-tuple-element.139.key, bf16[1024,256]{1,0:T(8,128)(2,1)S(1)} %get-tuple-element.140.value, ...), custom_call_target="tpu_custom_call" | custom-call | flops 1000000 | bytes 100000 | tf_op jit(solution)/shard_map/attention_back/pallas_call | solution.py:1348
  509.7 2.1 slice_add_fusion.1
  512.2 1.9 add_convert_fusion.2
  514.2 2.6 collective-permute-start.15
  516.8 6.2 convolution_convert_fusion.4.terms
  523.0 2.1 fusion.2
  525.9 2.0 collective-permute-start.16
  529.2 8.2 %collective-permute-start.14 = (bf16[1024,512]{1,0:T(8,128)(2,1)S(1)}, bf16[1024,512]{1,0:T(8,128)(2,1)S(1)}, u32[]{:S(2)}, u32[]{:S(2)}) collective-permute-start(bf16[1024,512]{1,0:T(8,128)(2,1)S(1)} %fusion.19), channel_id=1, source_target_pairs={{0,1},{1,0},{2,3},{3,2},{4,5},{5,4},{6,7},{7,6},{8,9},{9,8},{10,11... | collective-permute-start | bytes 3145736 | tf_op jit(solution)/shard_map/ppermute | solution.py:1472
  538.6 1.5 fusion.4.refs_3_
  541.2 2.3 add_convert_fusion.4
  543.5 101.3 %grad_input_rows.1 = (bf16[1024,2048]{1,0:T(8,128)(2,1)}, f32[1,2048]{1,0:T(1,128)}, f32[1,4352]{1,0:T(1,128)}, bf16[3,256,512]{2,1,0:T(8,128)(2,1)}, bf16[256,1...) custom-call(bf16[1024,2048]{1,0:T(8,128)(2,1)} %convolution_convert_fusion.4.terms, ...), custom_call_target="tpu_custom_call" | custom-call | flops 1000000 | bytes 100000 | tf_op jit(solution)/shard_map/grad_input_rows/pallas_call | solution.py:936
  644.8 1.4 fusion.26
  647.5 4.8 collective-permute-start.19
  653.8 1.6 broadcast_select_fusion.1
  655.6 5.0 multiply_subtract_fusion
  660.6 3.1 multiply_subtract_fusion.1
  665.0 2.8 reshape.107
  667.8 2.8 multiply_subtract_fusion.3
  670.6 3.2 multiply_subtract_fusion.2
  673.8 6.8 %select_convert_fusion = (f32[1024,2048]{1,0:T(8,128)}, bf16[1024,2048]{1,0:T(8,128)(2,1)}) fusion(bf16[1024,2048]{1,0:T(8,128)(2,1)S(1)} %copy-done.13, bf16[1024,2048]{1,0:T(8,128)(2,1)} %collective-permute-done.18, pred[]{:T(512)S(6)} %eq.9), kind=kLoop, calls=%fused_computation.6 | loop fusion | flops 6291456 | bytes 20971520 | tf_op jit(solution)/shard_map/convert_element_type | solution.py:1881
  (180 shorter events, 21.6 us)
Async XLA Ops:
  90.0 35.2 %collective-permute-start.2 = (bf16[256,512]{1,0:T(8,128)(2,1)}, bf16[256,512]{1,0:T(8,128)(2,1)S(1)}, u32[]{:S(2)}, u32[]{:S(2)}) collective-permute-start(bf16[256,512]{1,0:T(8,128)(2,1)} %get-tuple-element.148), channel_id=1, source_target_pairs={{0,16},{1,17},{2,18},{3,19},{4,20},{5,21},{6,22},{7,23},{8,24},{9,... | collective-permute-start | bytes 786440 | tf_op jit(solution)/shard_map/ppermute | solution.py:1472
  91.3 33.9 %collective-permute-start.1 = (bf16[256,512]{1,0:T(8,128)(2,1)}, bf16[256,512]{1,0:T(8,128)(2,1)}, u32[]{:S(2)}, u32[]{:S(2)}) collective-permute-start(bf16[256,512]{1,0:T(8,128)(2,1)} %get-tuple-element.148), channel_id=1, source_target_pairs={{0,24},{1,25},{2,26},{3,27},{4,28},{5,29},{6,30},{7,31},{8,16},{9,... | collective-permute-start | bytes 786440 | tf_op jit(solution)/shard_map/ppermute | solution.py:1472
  93.4 31.8 %collective-permute-start = (bf16[256,512]{1,0:T(8,128)(2,1)}, bf16[256,512]{1,0:T(8,128)(2,1)}, u32[]{:S(2)}, u32[]{:S(2)}) collective-permute-start(bf16[256,512]{1,0:T(8,128)(2,1)} %get-tuple-element.148), channel_id=1, source_target_pairs={{0,8},{1,9},{2,10},{3,11},{4,12},{5,13},{6,14},{7,15},{8,0},{9,1},... | collective-permute-start | bytes 786440 | tf_op jit(solution)/shard_map/ppermute | solution.py:1472
  93.4 31.8 %collective-permute-start.3 = (bf16[256,1536]{1,0:T(8,128)(2,1)}, bf16[256,1536]{1,0:T(8,128)(2,1)}, u32[]{:S(2)}, u32[]{:S(2)}) collective-permute-start(bf16[256,1536]{1,0:T(8,128)(2,1)} %get-tuple-element.157.refs_4_), channel_id=1, source_target_pairs={{0,8},{1,9},{2,10},{3,11},{4,12},{5,13},{6,14},{7,15},{8,0},{9,1},... | collective-permute-start | bytes 2359304 | tf_op jit(solution)/shard_map/ppermute | solution.py:1472
  94.8 175.9 %collective-permute-start.5 = (bf16[1024,2048]{1,0:T(8,128)(2,1)}, bf16[1024,2048]{1,0:T(8,128)(2,1)}, u32[]{:S(2)}, u32[]{:S(2)}) collective-permute-start(bf16[1024,2048]{1,0:T(8,128)(2,1)} %own_grad), channel_id=1, source_target_pairs={{1,4},{3,6},{4,1},{6,3},{9,12},{11,14},{12,9},{14,11},{17,20},{19,... | collective-permute-start | bytes 12582920 | tf_op jit(solution)/shard_map/ppermute | solution.py:1472
  103.5 21.5 %copy-start = (f32[2048]{0:T(1024)}, f32[2048]{0:T(1024)S(1)}, u32[]{:S(2)}) copy-start(f32[2048]{0:T(1024)S(1)} %constant_dynamic-update-slice_fusion.26) | copy-start | bytes 24580
  103.5 21.6 %copy-start.32 = (bf16[256,512]{1,0:T(8,128)(2,1)S(1)}, bf16[256,512]{1,0:T(8,128)(2,1)}, u32[]{:S(2)}) copy-start(bf16[256,512]{1,0:T(8,128)(2,1)} %get-tuple-element.148) | copy-start | bytes 786436
  125.0 5.4 copy-start.1
  127.3 2.9 collective-permute-start.4
  304.6 6.4 copy-start.40
  304.6 6.4 copy-start.43
  310.7 9.2 %copy-start.18 = (bf16[1024,1536]{1,0:T(8,128)(2,1)S(1)}, bf16[1024,1536]{1,0:T(8,128)(2,1)}, u32[]{:S(2)}) copy-start(bf16[1024,1536]{1,0:T(8,128)(2,1)} %get-tuple-element.174.refs_4_) | copy-start | bytes 9437188
  310.8 9.2 %copy-start.31 = (bf16[1024,2048]{1,0:T(8,128)(2,1)S(1)}, bf16[1024,2048]{1,0:T(8,128)(2,1)}, u32[]{:S(2)}) copy-start(bf16[1024,2048]{1,0:T(8,128)(2,1)} %get-tuple-element.173) | copy-start | bytes 12582916
  310.8 9.1 %collective-permute-start.6 = (bf16[1024,1536]{1,0:T(8,128)(2,1)S(1)}, bf16[1024,1536]{1,0:T(8,128)(2,1)S(1)}, u32[]{:S(2)}, u32[]{:S(2)}) collective-permute-start(bf16[1024,1536]{1,0:T(8,128)(2,1)S(1)} %convolution_convert_fusion.3), channel_id=1, source_target_pairs={{0,1},{1,0},{2,3},{3,2},{4,5},{5,4},{6,7},{7,6},{8,9},{9,8},{10,11... | collective-permute-start | bytes 9437192 | tf_op jit(solution)/shard_map/ppermute | solution.py:1472
  324.8 24.1 %collective-permute-start.7 = (bf16[1024,3072]{1,0:T(8,128)(2,1)}, bf16[1024,3072]{1,0:T(8,128)(2,1)}, u32[]{:S(2)}, u32[]{:S(2)}) collective-permute-start(bf16[1024,3072]{1,0:T(8,128)(2,1)} %convolution_convert_fusion), channel_id=1, source_target_pairs={{0,1},{1,0},{2,3},{3,2},{4,5},{5,4},{6,7},{7,6},{8,9},{9,8},{10,11... | collective-permute-start | bytes 18874376 | tf_op jit(solution)/shard_map/ppermute | solution.py:1472
  327.8 22.9 %copy-start.41 = (bf16[1024,2048]{1,0:T(8,128)(2,1)S(1)}, bf16[1024,2048]{1,0:T(8,128)(2,1)}, u32[]{:S(2)}) copy-start(bf16[1024,2048]{1,0:T(8,128)(2,1)} %get-tuple-element.181.rows) | copy-start | bytes 12582916
  327.8 21.2 %collective-permute-start.8 = (bf16[256,1536]{1,0:T(8,128)(2,1)S(1)}, bf16[256,1536]{1,0:T(8,128)(2,1)S(1)}, u32[]{:S(2)}, u32[]{:S(2)}) collective-permute-start(bf16[256,1536]{1,0:T(8,128)(2,1)S(1)} %slice_bitcast_fusion.4), channel_id=1, source_target_pairs={{0,8},{1,9},{2,10},{3,11},{4,12},{5,13},{6,14},{7,15},{24,16},{25,... | collective-permute-start | bytes 2359304 | tf_op jit(solution)/shard_map/ppermute | solution.py:1472
  349.0 14.2 %copy-start.25 = (bf16[256,1536]{1,0:T(8,128)(2,1)}, bf16[256,1536]{1,0:T(8,128)(2,1)S(1)}, u32[]{:S(2)}) copy-start(bf16[256,1536]{1,0:T(8,128)(2,1)S(1)} %collective-permute-done.8) | copy-start | bytes 2359300
  349.0 17.8 %collective-permute-start.9 = (bf16[256,1536]{1,0:T(8,128)(2,1)S(1)}, bf16[256,1536]{1,0:T(8,128)(2,1)S(1)}, u32[]{:S(2)}, u32[]{:S(2)}) collective-permute-start(bf16[256,1536]{1,0:T(8,128)(2,1)S(1)} %slice_bitcast_fusion.3), channel_id=1, source_target_pairs={{0,8},{1,9},{2,10},{3,11},{4,12},{5,13},{6,14},{7,15},{24,16},{25,... | collective-permute-start | bytes 2359304 | tf_op jit(solution)/shard_map/ppermute | solution.py:1472
  366.8 86.0 %copy-start.27 = (bf16[256,1536]{1,0:T(8,128)(2,1)}, bf16[256,1536]{1,0:T(8,128)(2,1)S(1)}, u32[]{:S(2)}) copy-start(bf16[256,1536]{1,0:T(8,128)(2,1)S(1)} %collective-permute-done.9) | copy-start | bytes 2359300
  452.8 5.4 copy-start.16
  458.1 20.5 %copy-start.26 = (bf16[256,1536]{1,0:T(8,128)(2,1)S(1)}, bf16[256,1536]{1,0:T(8,128)(2,1)}, u32[]{:S(2)}) copy-start(bf16[256,1536]{1,0:T(8,128)(2,1)} %copy-done.25) | copy-start | bytes 2359300
  458.2 20.5 %copy-start.28 = (bf16[256,1536]{1,0:T(8,128)(2,1)S(1)}, bf16[256,1536]{1,0:T(8,128)(2,1)}, u32[]{:S(2)}) copy-start(bf16[256,1536]{1,0:T(8,128)(2,1)} %copy-done.27) | copy-start | bytes 2359300
  459.4 22.8 %copy-start.9 = (bf16[1024,2048]{1,0:T(8,128)(2,1)S(1)}, bf16[1024,2048]{1,0:T(8,128)(2,1)}, u32[]{:S(2)}) copy-start(bf16[1024,2048]{1,0:T(8,128)(2,1)} %get-tuple-element.205) | copy-start | bytes 12582916
  459.4 50.3 %collective-permute-start.10 = (bf16[256,3072]{1,0:T(8,128)(2,1)}, bf16[256,3072]{1,0:T(8,128)(2,1)}, u32[]{:S(2)}, u32[]{:S(2)}) collective-permute-start(bf16[256,3072]{1,0:T(8,128)(2,1)} %slice_bitcast_fusion), channel_id=1, source_target_pairs={{0,8},{1,9},{2,10},{3,11},{4,12},{5,13},{6,14},{7,15},{8,0},{9,1},... | collective-permute-start | bytes 4718600 | tf_op jit(solution)/shard_map/ppermute | solution.py:1472
  480.2 5.5 copy-start.36
  480.2 29.5 %collective-permute-start.13 = (bf16[2,256,1536]{2,1,0:T(8,128)(2,1)}, bf16[2,256,1536]{2,1,0:T(8,128)(2,1)}, u32[]{:S(2)}, u32[]{:S(2)}) collective-permute-start(bf16[2,256,1536]{2,1,0:T(8,128)(2,1)} %add_convert_fusion.3), channel_id=1, source_target_pairs={{8,16},{9,17},{10,18},{11,19},{12,20},{13,21},{14,22},{15,23},{16,... | collective-permute-start | bytes 4718600 | tf_op jit(solution)/shard_map/ppermute | solution.py:1472
  483.7 25.9 %collective-permute-start.12 = (bf16[256,2048]{1,0:T(8,128)(2,1)}, bf16[256,2048]{1,0:T(8,128)(2,1)}, u32[]{:S(2)}, u32[]{:S(2)}) collective-permute-start(bf16[256,2048]{1,0:T(8,128)(2,1)} %get-tuple-element.256), channel_id=1, source_target_pairs={{0,4},{1,5},{2,6},{3,7},{4,0},{5,1},{6,2},{7,3},{8,12},{9,13},{10,... | collective-permute-start | bytes 3145736 | tf_op jit(solution)/shard_map/ppermute | solution.py:1472
  484.1 25.6 %collective-permute-start.11 = (bf16[256,2048]{1,0:T(8,128)(2,1)}, bf16[256,2048]{1,0:T(8,128)(2,1)}, u32[]{:S(2)}, u32[]{:S(2)}) collective-permute-start(bf16[256,2048]{1,0:T(8,128)(2,1)} %get-tuple-element.257), channel_id=1, source_target_pairs={{0,2},{1,3},{2,0},{3,1},{4,6},{5,7},{6,4},{7,5},{8,10},{9,11},{10,... | collective-permute-start | bytes 3145736 | tf_op jit(solution)/shard_map/ppermute | solution.py:1472
  514.2 8.8 %copy-start.17 = (bf16[2,256,3072]{2,1,0:T(8,128)(2,1)S(1)}, bf16[2,256,3072]{2,1,0:T(8,128)(2,1)}, u32[]{:S(2)}) copy-start(bf16[2,256,3072]{2,1,0:T(8,128)(2,1)} %get-tuple-element.204) | copy-start | bytes 9437188
  514.2 26.0 %collective-permute-start.15 = (bf16[256,1536]{1,0:T(8,128)(2,1)S(1)}, bf16[256,1536]{1,0:T(8,128)(2,1)S(1)}, u32[]{:S(2)}, u32[]{:S(2)}) collective-permute-start(bf16[256,1536]{1,0:T(8,128)(2,1)S(1)} %slice_bitcast_fusion.1), channel_id=1, source_target_pairs={{0,8},{1,9},{2,10},{3,11},{4,12},{5,13},{6,14},{7,15},{8,0},{9,1},... | collective-permute-start | bytes 2359304 | tf_op jit(solution)/shard_map/ppermute | solution.py:1472
  525.3 13.3 %collective-permute-start.17 = (bf16[128,2048]{1,0:T(8,128)(2,1)S(1)}, bf16[128,2048]{1,0:T(8,128)(2,1)S(1)}, u32[]{:S(2)}, u32[]{:S(2)}) collective-permute-start(bf16[128,2048]{1,0:T(8,128)(2,1)S(1)} %slice.200), channel_id=1, source_target_pairs={{0,2},{1,3},{2,0},{3,1},{4,6},{5,7},{6,4},{7,5},{8,10},{9,11},{10,... | collective-permute-start | bytes 1572872 | tf_op jit(solution)/shard_map/ppermute | solution.py:1472
  525.9 12.7 %collective-permute-start.16 = (bf16[128,2048]{1,0:T(8,128)(2,1)S(1)}, bf16[128,2048]{1,0:T(8,128)(2,1)S(1)}, u32[]{:S(2)}, u32[]{:S(2)}) collective-permute-start(bf16[128,2048]{1,0:T(8,128)(2,1)S(1)} %slice.201), channel_id=1, source_target_pairs={{0,4},{1,5},{2,6},{3,7},{4,0},{5,1},{6,2},{7,3},{8,12},{9,13},{10,... | collective-permute-start | bytes 1572872 | tf_op jit(solution)/shard_map/ppermute | solution.py:1472
  529.2 9.4 %copy-start.5 = (f32[256,2048]{1,0:T(8,128)S(1)}, f32[256,2048]{1,0:T(8,128)}, u32[]{:S(2)}) copy-start(f32[256,2048]{1,0:T(8,128)} %get-tuple-element.187.refs_0_) | copy-start | bytes 6291460
  529.2 12.0 %collective-permute-start.14 = (bf16[1024,512]{1,0:T(8,128)(2,1)S(1)}, bf16[1024,512]{1,0:T(8,128)(2,1)S(1)}, u32[]{:S(2)}, u32[]{:S(2)}) collective-permute-start(bf16[1024,512]{1,0:T(8,128)(2,1)S(1)} %fusion.19), channel_id=1, source_target_pairs={{0,1},{1,0},{2,3},{3,2},{4,5},{5,4},{6,7},{7,6},{8,9},{9,8},{10,11... | collective-permute-start | bytes 3145736 | tf_op jit(solution)/shard_map/ppermute | solution.py:1472
  543.5 109.7 %copy-start.34 = (f32[544]{0:T(1024)S(1)}, f32[544]{0:T(1024)}, u32[]{:S(2)}) copy-start(f32[544]{0:T(1024)} %param.33) | copy-start | bytes 6532
  543.5 109.7 %copy-start.37 = (f32[544]{0:T(1024)S(1)}, f32[544]{0:T(1024)}, u32[]{:S(2)}) copy-start(f32[544]{0:T(1024)} %param.35) | copy-start | bytes 6532
  543.5 109.7 %copy-start.38 = (f32[544]{0:T(1024)S(1)}, f32[544]{0:T(1024)}, u32[]{:S(2)}) copy-start(f32[544]{0:T(1024)} %param.34) | copy-start | bytes 6532
  543.5 112.0 %copy-start.14 = (f32[2,256,1536]{2,1,0:T(8,128)S(1)}, f32[2,256,1536]{2,1,0:T(8,128)}, u32[]{:S(2)}) copy-start(f32[2,256,1536]{2,1,0:T(8,128)} %param.29) | copy-start | bytes 9437188
  543.5 112.0 %copy-start.15 = (f32[2,256,1536]{2,1,0:T(8,128)S(1)}, f32[2,256,1536]{2,1,0:T(8,128)}, u32[]{:S(2)}) copy-start(f32[2,256,1536]{2,1,0:T(8,128)} %param.28) | copy-start | bytes 9437188
  644.8 9.1 %copy-start.3 = (bf16[512,1536]{1,0:T(8,128)(2,1)S(1)}, bf16[512,1536]{1,0:T(8,128)(2,1)}, u32[]{:S(2)}) copy-start(bf16[512,1536]{1,0:T(8,128)(2,1)} %pad_maximum_fusion.refs_8_) | copy-start | bytes 4718596
  646.2 9.3 %copy-start.4 = (f32[2,256,1536]{2,1,0:T(8,128)S(1)}, f32[2,256,1536]{2,1,0:T(8,128)}, u32[]{:S(2)}) copy-start(f32[2,256,1536]{2,1,0:T(8,128)} %wide_gate.1) | copy-start | bytes 9437188
  647.5 16.2 %collective-permute-start.19 = (bf16[256,1536]{1,0:T(8,128)(2,1)S(1)}, bf16[256,1536]{1,0:T(8,128)(2,1)S(1)}, u32[]{:S(2)}, u32[]{:S(2)}) collective-permute-start(bf16[256,1536]{1,0:T(8,128)(2,1)S(1)} %pad_maximum_fusion.3), channel_id=1, source_target_pairs={{1,4},{3,6},{4,1},{6,3},{9,12},{11,14},{12,9},{14,11},{17,20},{19,... | collective-permute-start | bytes 2359304 | tf_op jit(solution)/shard_map/ppermute | solution.py:1472
  652.3 21.4 %collective-permute-start.18 = (bf16[1024,2048]{1,0:T(8,128)(2,1)}, bf16[1024,2048]{1,0:T(8,128)(2,1)}, u32[]{:S(2)}, u32[]{:S(2)}) collective-permute-start(bf16[1024,2048]{1,0:T(8,128)(2,1)} %get-tuple-element.231), channel_id=1, source_target_pairs={{0,1},{1,0},{2,3},{3,2},{4,5},{5,4},{6,7},{7,6},{8,9},{9,8},{10,11... | collective-permute-start | bytes 12582920 | tf_op jit(solution)/shard_map/ppermute | solution.py:1472
  655.5 5.1 copy-start.7
  655.5 5.1 copy-start.8
  655.5 5.1 copy-start.29
  665.0 5.5 copy-start.10
  (16 other events, 57.8 us)
